TPU v7x, 128 devices: a whole 4x4x4 slice. The times are simulated.
128 devices in a mesh: bx: 8 (over z_hi, y), by: 16 (over x, z_lo, core).
Axes of the slice: x: 4, y: 4, z: 4 (z_hi: 2, z_lo: 2; z = z_hi * 2 + z_lo), core: 2. Of those that a mesh axis runs over, the one named last changes fastest.
Arguments:
- fine_prev: float32 [32, 16, 32, 256], P(None, 'bx', 'by'), may hold values from -4 to 4
- fine_now: float32 [32, 16, 32, 256], P(None, 'bx', 'by'), may hold values from -4 to 4
- fine_kernels: bfloat16 [4, 27, 32, 32], replicated, may hold values from -0.21875 to 0.21875
- coarse_kernel: bfloat16 [27, 1024, 256], P(None, 'by'), may hold values from -0.078125 to 0.078125
- cotangent: bfloat16 [256, 8, 16, 128], P(None, 'bx', 'by'), may hold values from -6 to 6
Outputs:
- coarse_next: float32 [256, 8, 16, 128], P(None, 'bx', 'by')
- state_adjoint: float32 [256, 8, 16, 128], P(None, 'bx', 'by')
All inputs are finite; a program needn't handle non-finite values.
Results may differ from a plain program's by a relative error of at most 0.0085.
Values may be sent and summed in bfloat16 or wider, within the bound.
No kernel may reach another device: no remote copies, remote signals or barrier semaphores. Data moves between devices by JAX's collectives and lax.ppermute only.
A program may use at most 64 MiB of HBM per device.

v0:
```python
import math

import jax
import jax.numpy as jnp
import numpy as np
from jax import lax
from jax.sharding import PartitionSpec as P

LAYERS = 4


fine_step = 0.5
coarse_step = 1.5


def extended(x, sides, width):
    for axis, dim in sides:
        devices, length = (lax.axis_size(axis), x.shape[dim])
        up = [(i, (i + 1) % devices) for i in range(devices - 1)]
        down = [(j, i) for i, j in up]
        last = lax.slice_in_dim(x, length - width, length, axis=dim)
        first = lax.slice_in_dim(x, 0, width, axis=dim)
        before = lax.ppermute(last, axis, up)
        after = lax.ppermute(first, axis, down)
        x = jnp.concatenate([before, x, after], axis=dim)
    return x


def count_bits(value):
    total = 0
    for position in range(3):
        total = total + (value >> position & 1)
    return total


def haar_table():
    signs = np.zeros((8, 8))
    for output_code in range(8):
        for input_code in range(8):
            parity = count_bits(output_code & input_code)
            signs[output_code, input_code] = (-1.0) ** parity / math.sqrt(8.0)
    return signs


def coarsen(volume):
    octants = [
        volume[:, across::2, upward::2, inward::2]
        for across in range(2)
        for upward in range(2)
        for inward in range(2)
    ]
    stacked = jnp.stack(octants, 0)
    mixed = jnp.einsum(
        "hk,kcxyz->chxyz",
        jnp.asarray(haar_table(), jnp.float32),
        stacked,
        precision=lax.Precision.HIGHEST,
    )
    return mixed.reshape(
        (volume.shape[0] * 8, volume.shape[1] // 2, volume.shape[2] // 2, volume.shape[3] // 2)
    )


def tap_offsets():
    return [
        (across, upward, inward)
        for across in (-1, 0, 1)
        for upward in (-1, 0, 1)
        for inward in (-1, 0, 1)
    ]


def window_at(padded, starts, extent):
    return lax.slice(
        padded,
        (0, starts[0], starts[1], starts[2]),
        (padded.shape[0], starts[0] + extent[0], starts[1] + extent[1], starts[2] + extent[2]),
    )


def pad_depth(volume):
    return jnp.pad(volume, ((0, 0),) * (volume.ndim - 1) + ((1, 1),))


def forward_taps(padded, kernel, extent):
    totals = jnp.zeros((kernel.shape[1],) + tuple(extent), jnp.float32)
    for number, offset in enumerate(tap_offsets()):
        starts = (1 + offset[0], 1 + offset[1], 1 + offset[2])
        totals = totals + jnp.einsum(
            "oc,cxyz->oxyz",
            kernel[number],
            window_at(padded, starts, extent),
            preferred_element_type=jnp.float32,
        )
    return totals


def adjoint_taps(padded, kernel, extent):
    hidden_count = kernel.shape[1]
    totals = jnp.zeros((kernel.shape[2],) + tuple(extent), jnp.float32)
    for group in range(9):
        across = group // 3 - 1
        upward = group % 3 - 1
        windows = [
            window_at(padded, (1 - across, 1 - upward, 1 - inward), extent) for inward in (-1, 0, 1)
        ]
        stacked = jnp.concatenate(windows, 0)
        weights = kernel[3 * group : 3 * group + 3].reshape((3 * hidden_count, kernel.shape[2]))
        totals = totals + jnp.einsum(
            "kc,kxyz->cxyz", weights, stacked, preferred_element_type=jnp.float32
        )
    return totals


def local(fine_prev, fine_now, fine_kernels, coarse_kernel, cotangent):
    previous, current = (fine_prev, fine_now)
    cells_across, cells_upward, cells_inward = (
        current.shape[1],
        current.shape[2],
        current.shape[3],
    )
    for layer_index in range(LAYERS):
        kernel = fine_kernels[layer_index]
        rounded = current.astype(jnp.bfloat16)
        padded = extended(rounded, (("bx", 1), ("by", 2)), 1)
        preact = forward_taps(pad_depth(padded), kernel, (cells_across, cells_upward, cells_inward))
        squashed = jnp.tanh(preact).astype(jnp.bfloat16)
        squashed = extended(squashed, (("bx", 1), ("by", 2)), 1)
        force = adjoint_taps(
            pad_depth(squashed), kernel, (cells_across, cells_upward, cells_inward)
        )
        previous, current = (current, 2.0 * current - previous - fine_step * force)
    coarse_now = coarsen(current)
    coarse_prev = coarsen(previous)
    paired = jnp.stack([coarse_now.astype(jnp.bfloat16), cotangent], 0)
    coarse_across, coarse_upward, coarse_inward = (
        coarse_now.shape[1],
        coarse_now.shape[2],
        coarse_now.shape[3],
    )
    local_rows = extended(paired, (("bx", 2),), 1)
    slab_rows = lax.all_gather(local_rows, "by", axis=3, tiled=True)
    widened = jnp.pad(slab_rows, ((0, 0), (0, 0), (0, 0), (1, 1), (1, 1)))
    extent = (coarse_across, slab_rows.shape[3], coarse_inward)
    preact = forward_taps(widened[0], coarse_kernel, extent)
    response = forward_taps(widened[1], coarse_kernel, extent)
    squash_value = jnp.tanh(preact)
    squashed = squash_value.astype(jnp.bfloat16)
    scaled = ((1.0 - squash_value * squash_value) * response).astype(jnp.bfloat16)
    hidden = extended(jnp.stack([squashed, scaled], 0), (("bx", 2),), 1)
    hidden = jnp.pad(hidden, ((0, 0), (0, 0), (0, 0), (1, 1), (1, 1)))
    force_part = adjoint_taps(hidden[0], coarse_kernel, extent)
    adjoint_part = adjoint_taps(hidden[1], coarse_kernel, extent)
    force_sum, adjoint_sum = (
        lax.psum_scatter(force_part, "by", scatter_dimension=2, tiled=True),
        lax.psum_scatter(adjoint_part, "by", scatter_dimension=2, tiled=True),
    )
    coarse_next = 2.0 * coarse_now - coarse_prev - coarse_step * force_sum
    state_adjoint = 2.0 * cotangent.astype(jnp.float32) - coarse_step * adjoint_sum
    return (coarse_next, state_adjoint)


def solution(mesh):
    placed = (
        P(None, "bx", "by", None),
        P(None, "bx", "by", None),
        P(),
        P(None, "by", None),
        P(None, "bx", "by", None),
    )
    return jax.shard_map(
        local,
        mesh=mesh,
        in_specs=placed,
        out_specs=(P(None, "bx", "by", None), P(None, "bx", "by", None)),
        check_vma=False,
    )
```

profile of v0, /device:TPU:0, one launch (start us, length us, event | category | flops | bytes accessed | tf_op | source)
XLA Modules:
  0.0 465.5 jit_solution(4106179711232985799)
XLA Ops:
  34.6 4.2 collective-permute-done.5
  48.8 7.4 %collective-permute-start.8 = (bf16[32,1,2,256]{3,0,2,1:T(8,128)(2,1)S(1)}, bf16[32,1,2,256]{3,0,2,1:T(8,128)(2,1)S(1)}, u32[]{:S(2)}, u32[]{:S(2)}) collective-permute-start(bf16[32,1,2,256]{3,0,2,1:T(8,128)(2,1)S(1)} %get-tuple-element.247), channel_id=1, source_target_pairs={{0,16},{16,32},{32,48},{48,64},{64,80},{80,96},{96,112},{1,17},{17... | collective-permute-start | bytes 98312 | tf_op jit(solution)/shard_map/ppermute | solution.py:23
  57.8 4.2 collective-permute-done.9
  74.3 5.5 %collective-permute-start.12 = (bf16[32,1,2,256]{3,0,2,1:T(8,128)(2,1)S(1)}, bf16[32,1,2,256]{3,0,2,1:T(8,128)(2,1)S(1)}, u32[]{:S(2)}, u32[]{:S(2)}) collective-permute-start(bf16[32,1,2,256]{3,0,2,1:T(8,128)(2,1)S(1)} %get-tuple-element.245), channel_id=1, source_target_pairs={{0,16},{16,32},{32,48},{48,64},{64,80},{80,96},{96,112},{1,17},{17... | collective-permute-start | bytes 98312 | tf_op jit(solution)/shard_map/ppermute | solution.py:23
  85.7 4.3 collective-permute-start.14
  96.5 5.5 %collective-permute-start.16 = (bf16[32,1,2,256]{3,0,2,1:T(8,128)(2,1)S(1)}, bf16[32,1,2,256]{3,0,2,1:T(8,128)(2,1)S(1)}, u32[]{:S(2)}, u32[]{:S(2)}) collective-permute-start(bf16[32,1,2,256]{3,0,2,1:T(8,128)(2,1)S(1)} %get-tuple-element.243), channel_id=1, source_target_pairs={{0,16},{16,32},{32,48},{48,64},{64,80},{80,96},{96,112},{1,17},{17... | collective-permute-start | bytes 98312 | tf_op jit(solution)/shard_map/ppermute | solution.py:23
  103.7 4.2 collective-permute-done.17
  107.9 4.3 collective-permute-start.18
  121.0 5.5 %collective-permute-start.20 = (bf16[32,1,2,256]{3,0,2,1:T(8,128)(2,1)S(1)}, bf16[32,1,2,256]{3,0,2,1:T(8,128)(2,1)S(1)}, u32[]{:S(2)}, u32[]{:S(2)}) collective-permute-start(bf16[32,1,2,256]{3,0,2,1:T(8,128)(2,1)S(1)} %get-tuple-element.241), channel_id=1, source_target_pairs={{0,16},{16,32},{32,48},{48,64},{64,80},{80,96},{96,112},{1,17},{17... | collective-permute-start | bytes 98312 | tf_op jit(solution)/shard_map/ppermute | solution.py:23
  128.1 4.2 collective-permute-done.21
  132.3 4.3 collective-permute-start.22
  143.1 5.5 %collective-permute-start.24 = (bf16[32,1,2,256]{3,0,2,1:T(8,128)(2,1)S(1)}, bf16[32,1,2,256]{3,0,2,1:T(8,128)(2,1)S(1)}, u32[]{:S(2)}, u32[]{:S(2)}) collective-permute-start(bf16[32,1,2,256]{3,0,2,1:T(8,128)(2,1)S(1)} %get-tuple-element.239), channel_id=1, source_target_pairs={{0,16},{16,32},{32,48},{48,64},{64,80},{80,96},{96,112},{1,17},{17... | collective-permute-start | bytes 98312 | tf_op jit(solution)/shard_map/ppermute | solution.py:23
  150.3 4.2 collective-permute-done.25
  154.5 4.3 collective-permute-start.26
  167.6 5.5 %collective-permute-start.28 = (bf16[32,1,2,256]{3,0,2,1:T(8,128)(2,1)S(1)}, bf16[32,1,2,256]{3,0,2,1:T(8,128)(2,1)S(1)}, u32[]{:S(2)}, u32[]{:S(2)}) collective-permute-start(bf16[32,1,2,256]{3,0,2,1:T(8,128)(2,1)S(1)} %get-tuple-element.237), channel_id=1, source_target_pairs={{0,16},{16,32},{32,48},{48,64},{64,80},{80,96},{96,112},{1,17},{17... | collective-permute-start | bytes 98312 | tf_op jit(solution)/shard_map/ppermute | solution.py:23
  179.0 4.3 collective-permute-start.30
  195.1 5.5 %collective-permute-start.32 = (bf16[2,256,1,1,128]{4,1,3,2,0:T(8,128)(2,1)S(1)}, bf16[2,256,1,1,128]{4,1,3,2,0:T(8,128)(2,1)S(1)}, u32[]{:S(2)}, u32[]{:S(2)}) collective-permute-start(bf16[2,256,1,1,128]{4,1,3,2,0:T(8,128)(2,1)S(1)} %pad_maximum_fusion.26), channel_id=1, source_target_pairs={{0,16},{16,32},{32,48},{48,64},{64,80},{80,96},{96,112},{1,17},{17... | collective-permute-start | bytes 393224 | tf_op jit(solution)/shard_map/ppermute | solution.py:23
  203.2 4.4 collective-permute-done.33
  208.4 51.1 %all-gather.2.cloned.1.call-done = bf16[2,256,3,16,128]{4,1,3,2,0:T(8,128)(2,1)} async-done(((bf16[2,256,3,1,128]{4,1,3,2,0:T(8,128)(2,1)}), bf16[2,256,3,16,128]{4,1,3,2,0:T(8,128)(2,1)}) %all-gather.2.cloned.1.call-update) | async-done | bytes 6291472 | tf_op jit(solution)/shard_map/all_gather | solution.py:142
  259.5 7.0 %fusion = (bf16[256,3,18,130]{3,0,2,1:T(8,128)(2,1)S(1)}, bf16[256,3,18,130]{3,0,2,1:T(8,128)(2,1)S(1)}) fusion(bf16[2,256,3,16,128]{4,1,3,2,0:T(8,128)(2,1)} %all-gather.2.cloned.1.call-done), kind=kLoop, calls=%fused_computation.6 | loop fusion | bytes 13479936 | tf_op jit(solution)/shard_map/squeeze | solution.py:145
  297.2 10.2 %collective-permute-done.34 = bf16[2,64,1,16,128]{4,1,3,2,0:T(8,128)(2,1)S(1)} collective-permute-done((bf16[2,64,1,16,128]{4,1,3,2,0:T(8,128)(2,1)S(1)}, bf16[2,64,1,16,128]{4,1,3,2,0:T(8,128)(2,1)S(1)}, u32[]{:S(2)}, u32[]{:S(2)}) %collective-permute-start.34) | collective-permute-done | bytes 524320 | tf_op jit(solution)/shard_map/ppermute | solution.py:23
  311.5 4.2 select_maximum_fusion
  339.0 53.1 %reduce-scatter.5.cloned.1.call-done = f32[256,1,1,128]{0,3,2,1:T(8,128)} async-done(((f32[256,1,16,128]{0,3,2,1:T(8,128)}), f32[256,1,1,128]{0,3,2,1:T(8,128)}) %reduce-scatter.5.cloned.1.call-update) | async-done | bytes 131088 | tf_op jit(solution)/shard_map/reduce_scatter | solution.py:156
  393.8 63.0 %reduce-scatter.3.cloned.1.call-done = f32[256,1,1,128]{0,3,2,1:T(8,128)} async-done(((f32[256,1,16,128]{0,3,2,1:T(8,128)}), f32[256,1,1,128]{0,3,2,1:T(8,128)}) %reduce-scatter.3.cloned.1.call-update) | async-done | bytes 131088 | tf_op jit(solution)/shard_map/reduce_scatter | solution.py:155
  (393 shorter events, 172.8 us)
Async XLA Ops:
  7.2 252.3 %all-gather.2.cloned.1.call-start = ((), (), s32[]{:S(2)}) async-start(), calls=%async_computation.2 | async-start | bytes 6684672 | tf_op jit(solution)/shard_map/all_gather | solution.py:142
  11.8 5.8 %collective-permute-start.1 = (bf16[32,1,2,256]{3,0,2,1:T(8,128)(2,1)S(1)}, bf16[32,1,2,256]{3,0,2,1:T(8,128)(2,1)S(1)}, u32[]{:S(2)}, u32[]{:S(2)}) collective-permute-start(bf16[32,1,2,256]{3,0,2,1:T(8,128)(2,1)S(1)} %get-tuple-element.252), channel_id=1, source_target_pairs={{16,0},{32,16},{48,32},{64,48},{80,64},{96,80},{112,96},{17,1},{33... | collective-permute-start | bytes 98312 | tf_op jit(solution)/shard_map/ppermute | solution.py:24
  33.0 5.8 %collective-permute-start.5 = (bf16[32,1,2,256]{3,0,2,1:T(8,128)(2,1)S(1)}, bf16[32,1,2,256]{3,0,2,1:T(8,128)(2,1)S(1)}, u32[]{:S(2)}, u32[]{:S(2)}) collective-permute-start(bf16[32,1,2,256]{3,0,2,1:T(8,128)(2,1)S(1)} %get-tuple-element.250), channel_id=1, source_target_pairs={{16,0},{32,16},{48,32},{64,48},{80,64},{96,80},{112,96},{17,1},{33... | collective-permute-start | bytes 98312 | tf_op jit(solution)/shard_map/ppermute | solution.py:24
  48.8 9.0 %collective-permute-start.8 = (bf16[32,1,2,256]{3,0,2,1:T(8,128)(2,1)S(1)}, bf16[32,1,2,256]{3,0,2,1:T(8,128)(2,1)S(1)}, u32[]{:S(2)}, u32[]{:S(2)}) collective-permute-start(bf16[32,1,2,256]{3,0,2,1:T(8,128)(2,1)S(1)} %get-tuple-element.247), channel_id=1, source_target_pairs={{0,16},{16,32},{32,48},{48,64},{64,80},{80,96},{96,112},{1,17},{17... | collective-permute-start | bytes 98312 | tf_op jit(solution)/shard_map/ppermute | solution.py:23
  56.2 5.8 %collective-permute-start.9 = (bf16[32,1,2,256]{3,0,2,1:T(8,128)(2,1)S(1)}, bf16[32,1,2,256]{3,0,2,1:T(8,128)(2,1)S(1)}, u32[]{:S(2)}, u32[]{:S(2)}) collective-permute-start(bf16[32,1,2,256]{3,0,2,1:T(8,128)(2,1)S(1)} %get-tuple-element.248), channel_id=1, source_target_pairs={{16,0},{32,16},{48,32},{64,48},{80,64},{96,80},{112,96},{17,1},{33... | collective-permute-start | bytes 98312 | tf_op jit(solution)/shard_map/ppermute | solution.py:24
  74.3 7.1 %collective-permute-start.12 = (bf16[32,1,2,256]{3,0,2,1:T(8,128)(2,1)S(1)}, bf16[32,1,2,256]{3,0,2,1:T(8,128)(2,1)S(1)}, u32[]{:S(2)}, u32[]{:S(2)}) collective-permute-start(bf16[32,1,2,256]{3,0,2,1:T(8,128)(2,1)S(1)} %get-tuple-element.245), channel_id=1, source_target_pairs={{0,16},{16,32},{32,48},{48,64},{64,80},{80,96},{96,112},{1,17},{17... | collective-permute-start | bytes 98312 | tf_op jit(solution)/shard_map/ppermute | solution.py:23
  79.9 5.8 %collective-permute-start.13 = (bf16[32,1,2,256]{3,0,2,1:T(8,128)(2,1)S(1)}, bf16[32,1,2,256]{3,0,2,1:T(8,128)(2,1)S(1)}, u32[]{:S(2)}, u32[]{:S(2)}) collective-permute-start(bf16[32,1,2,256]{3,0,2,1:T(8,128)(2,1)S(1)} %get-tuple-element.246), channel_id=1, source_target_pairs={{16,0},{32,16},{48,32},{64,48},{80,64},{96,80},{112,96},{17,1},{33... | collective-permute-start | bytes 98312 | tf_op jit(solution)/shard_map/ppermute | solution.py:24
  96.5 7.1 %collective-permute-start.16 = (bf16[32,1,2,256]{3,0,2,1:T(8,128)(2,1)S(1)}, bf16[32,1,2,256]{3,0,2,1:T(8,128)(2,1)S(1)}, u32[]{:S(2)}, u32[]{:S(2)}) collective-permute-start(bf16[32,1,2,256]{3,0,2,1:T(8,128)(2,1)S(1)} %get-tuple-element.243), channel_id=1, source_target_pairs={{0,16},{16,32},{32,48},{48,64},{64,80},{80,96},{96,112},{1,17},{17... | collective-permute-start | bytes 98312 | tf_op jit(solution)/shard_map/ppermute | solution.py:23
  102.1 5.8 %collective-permute-start.17 = (bf16[32,1,2,256]{3,0,2,1:T(8,128)(2,1)S(1)}, bf16[32,1,2,256]{3,0,2,1:T(8,128)(2,1)S(1)}, u32[]{:S(2)}, u32[]{:S(2)}) collective-permute-start(bf16[32,1,2,256]{3,0,2,1:T(8,128)(2,1)S(1)} %get-tuple-element.244), channel_id=1, source_target_pairs={{16,0},{32,16},{48,32},{64,48},{80,64},{96,80},{112,96},{17,1},{33... | collective-permute-start | bytes 98312 | tf_op jit(solution)/shard_map/ppermute | solution.py:24
  107.9 5.8 %collective-permute-start.18 = (bf16[32,4,1,256]{3,0,2,1:T(8,128)(2,1)S(1)}, bf16[32,4,1,256]{3,0,2,1:T(8,128)(2,1)S(1)}, u32[]{:S(2)}, u32[]{:S(2)}) collective-permute-start(bf16[32,4,1,256]{3,0,2,1:T(8,128)(2,1)S(1)} %get-tuple-element.219), channel_id=1, source_target_pairs={{0,1},{1,2},{2,3},{3,4},{4,5},{5,6},{6,7},{7,8},{8,9},{9,10},{10,1... | collective-permute-start | bytes 196616 | tf_op jit(solution)/shard_map/ppermute | solution.py:23
  121.0 7.1 %collective-permute-start.20 = (bf16[32,1,2,256]{3,0,2,1:T(8,128)(2,1)S(1)}, bf16[32,1,2,256]{3,0,2,1:T(8,128)(2,1)S(1)}, u32[]{:S(2)}, u32[]{:S(2)}) collective-permute-start(bf16[32,1,2,256]{3,0,2,1:T(8,128)(2,1)S(1)} %get-tuple-element.241), channel_id=1, source_target_pairs={{0,16},{16,32},{32,48},{48,64},{64,80},{80,96},{96,112},{1,17},{17... | collective-permute-start | bytes 98312 | tf_op jit(solution)/shard_map/ppermute | solution.py:23
  126.5 5.8 %collective-permute-start.21 = (bf16[32,1,2,256]{3,0,2,1:T(8,128)(2,1)S(1)}, bf16[32,1,2,256]{3,0,2,1:T(8,128)(2,1)S(1)}, u32[]{:S(2)}, u32[]{:S(2)}) collective-permute-start(bf16[32,1,2,256]{3,0,2,1:T(8,128)(2,1)S(1)} %get-tuple-element.242), channel_id=1, source_target_pairs={{16,0},{32,16},{48,32},{64,48},{80,64},{96,80},{112,96},{17,1},{33... | collective-permute-start | bytes 98312 | tf_op jit(solution)/shard_map/ppermute | solution.py:24
  143.1 7.1 %collective-permute-start.24 = (bf16[32,1,2,256]{3,0,2,1:T(8,128)(2,1)S(1)}, bf16[32,1,2,256]{3,0,2,1:T(8,128)(2,1)S(1)}, u32[]{:S(2)}, u32[]{:S(2)}) collective-permute-start(bf16[32,1,2,256]{3,0,2,1:T(8,128)(2,1)S(1)} %get-tuple-element.239), channel_id=1, source_target_pairs={{0,16},{16,32},{32,48},{48,64},{64,80},{80,96},{96,112},{1,17},{17... | collective-permute-start | bytes 98312 | tf_op jit(solution)/shard_map/ppermute | solution.py:23
  148.7 5.8 %collective-permute-start.25 = (bf16[32,1,2,256]{3,0,2,1:T(8,128)(2,1)S(1)}, bf16[32,1,2,256]{3,0,2,1:T(8,128)(2,1)S(1)}, u32[]{:S(2)}, u32[]{:S(2)}) collective-permute-start(bf16[32,1,2,256]{3,0,2,1:T(8,128)(2,1)S(1)} %get-tuple-element.240), channel_id=1, source_target_pairs={{16,0},{32,16},{48,32},{64,48},{80,64},{96,80},{112,96},{17,1},{33... | collective-permute-start | bytes 98312 | tf_op jit(solution)/shard_map/ppermute | solution.py:24
  154.5 5.8 %collective-permute-start.26 = (bf16[32,4,1,256]{3,0,2,1:T(8,128)(2,1)S(1)}, bf16[32,4,1,256]{3,0,2,1:T(8,128)(2,1)S(1)}, u32[]{:S(2)}, u32[]{:S(2)}) collective-permute-start(bf16[32,4,1,256]{3,0,2,1:T(8,128)(2,1)S(1)} %get-tuple-element.211), channel_id=1, source_target_pairs={{0,1},{1,2},{2,3},{3,4},{4,5},{5,6},{6,7},{7,8},{8,9},{9,10},{10,1... | collective-permute-start | bytes 196616 | tf_op jit(solution)/shard_map/ppermute | solution.py:23
  167.6 7.1 %collective-permute-start.28 = (bf16[32,1,2,256]{3,0,2,1:T(8,128)(2,1)S(1)}, bf16[32,1,2,256]{3,0,2,1:T(8,128)(2,1)S(1)}, u32[]{:S(2)}, u32[]{:S(2)}) collective-permute-start(bf16[32,1,2,256]{3,0,2,1:T(8,128)(2,1)S(1)} %get-tuple-element.237), channel_id=1, source_target_pairs={{0,16},{16,32},{32,48},{48,64},{64,80},{80,96},{96,112},{1,17},{17... | collective-permute-start | bytes 98312 | tf_op jit(solution)/shard_map/ppermute | solution.py:23
  173.1 5.8 %collective-permute-start.29 = (bf16[32,1,2,256]{3,0,2,1:T(8,128)(2,1)S(1)}, bf16[32,1,2,256]{3,0,2,1:T(8,128)(2,1)S(1)}, u32[]{:S(2)}, u32[]{:S(2)}) collective-permute-start(bf16[32,1,2,256]{3,0,2,1:T(8,128)(2,1)S(1)} %get-tuple-element.238), channel_id=1, source_target_pairs={{16,0},{32,16},{48,32},{64,48},{80,64},{96,80},{112,96},{17,1},{33... | collective-permute-start | bytes 98312 | tf_op jit(solution)/shard_map/ppermute | solution.py:24
  179.0 5.9 %collective-permute-start.30 = (bf16[32,4,1,256]{3,0,2,1:T(8,128)(2,1)S(1)}, bf16[32,4,1,256]{3,0,2,1:T(8,128)(2,1)S(1)}, u32[]{:S(2)}, u32[]{:S(2)}) collective-permute-start(bf16[32,4,1,256]{3,0,2,1:T(8,128)(2,1)S(1)} %get-tuple-element.207), channel_id=1, source_target_pairs={{0,1},{1,2},{2,3},{3,4},{4,5},{5,6},{6,7},{7,8},{8,9},{9,10},{10,1... | collective-permute-start | bytes 196616 | tf_op jit(solution)/shard_map/ppermute | solution.py:23
  195.1 8.0 %collective-permute-start.32 = (bf16[2,256,1,1,128]{4,1,3,2,0:T(8,128)(2,1)S(1)}, bf16[2,256,1,1,128]{4,1,3,2,0:T(8,128)(2,1)S(1)}, u32[]{:S(2)}, u32[]{:S(2)}) collective-permute-start(bf16[2,256,1,1,128]{4,1,3,2,0:T(8,128)(2,1)S(1)} %pad_maximum_fusion.26), channel_id=1, source_target_pairs={{0,16},{16,32},{32,48},{48,64},{64,80},{80,96},{96,112},{1,17},{17... | collective-permute-start | bytes 393224 | tf_op jit(solution)/shard_map/ppermute | solution.py:23
  200.7 6.9 %collective-permute-start.33 = (bf16[2,256,1,1,128]{4,1,3,2,0:T(8,128)(2,1)S(1)}, bf16[2,256,1,1,128]{4,1,3,2,0:T(8,128)(2,1)S(1)}, u32[]{:S(2)}, u32[]{:S(2)}) collective-permute-start(bf16[2,256,1,1,128]{4,1,3,2,0:T(8,128)(2,1)S(1)} %pad_maximum_fusion.26), channel_id=1, source_target_pairs={{16,0},{32,16},{48,32},{64,48},{80,64},{96,80},{112,96},{17,1},{33... | collective-permute-start | bytes 393224 | tf_op jit(solution)/shard_map/ppermute | solution.py:24
  208.4 183.7 %reduce-scatter.5.cloned.1.call-start = ((), (), s32[]{:S(2)}) async-start(), calls=%async_computation.4 | async-start | bytes 2228224 | tf_op jit(solution)/shard_map/reduce_scatter | solution.py:156
  292.4 15.0 %collective-permute-start.34 = (bf16[2,64,1,16,128]{4,1,3,2,0:T(8,128)(2,1)S(1)}, bf16[2,64,1,16,128]{4,1,3,2,0:T(8,128)(2,1)S(1)}, u32[]{:S(2)}, u32[]{:S(2)}) collective-permute-start(bf16[2,64,1,16,128]{4,1,3,2,0:T(8,128)(2,1)S(1)} %pad_maximum_fusion), channel_id=1, source_target_pairs={{0,16},{16,32},{32,48},{48,64},{64,80},{80,96},{96,112},{1,17},{17... | collective-permute-start | bytes 1572872 | tf_op jit(solution)/shard_map/ppermute | solution.py:23
  295.8 15.7 %collective-permute-start.35 = (bf16[2,64,1,16,128]{4,1,3,2,0:T(8,128)(2,1)S(1)}, bf16[2,64,1,16,128]{4,1,3,2,0:T(8,128)(2,1)S(1)}, u32[]{:S(2)}, u32[]{:S(2)}) collective-permute-start(bf16[2,64,1,16,128]{4,1,3,2,0:T(8,128)(2,1)S(1)} %pad_maximum_fusion), channel_id=1, source_target_pairs={{16,0},{32,16},{48,32},{64,48},{80,64},{96,80},{112,96},{17,1},{33... | collective-permute-start | bytes 1572872 | tf_op jit(solution)/shard_map/ppermute | solution.py:24
  324.7 132.1 %reduce-scatter.3.cloned.1.call-start = ((), (), s32[]{:S(2)}) async-start(), calls=%async_computation.3 | async-start | bytes 2228224 | tf_op jit(solution)/shard_map/reduce_scatter | solution.py:155
  (21 other events, 161.4 us)
Sparse Core Ops, SparseCore 0:
  208.5 51.0 all-gather.1
  324.8 67.2 reduce-scatter.4
  394.5 62.2 reduce-scatter.2
where the time goes:
time: 475 us; the launch traced here: 465 us
  waiting for transfers between devices  244 us (51%)
  starting transfers between devices  105 us (22%)
  matrix products  66.2 us (14%)
  local copies, waits for them, and re-layouts  25.1 us (5%)
  between operations  16.3 us (3%)
  other arithmetic  9.17 us (2%)
    ppermute x18, starting transfers between devices, extended(): before = lax.ppermute(last, axis, up)  81.3 us
    reduce_scatter x1, waiting for transfers between devices, local(): lax.psum_scatter(force_part, 'by', scatter_dimension=2, tiled=True)  63 us
    ppermute x18, waiting for transfers between devices, extended(): after = lax.ppermute(first, axis, down)  63 us
    reduce_scatter x1, waiting for transfers between devices, local(): lax.psum_scatter(adjoint_part, 'by', scatter_dimension=2, tiled=True)  53.1 us
    all_gather x1, waiting for transfers between devices, local(): slab_rows = lax.all_gather(local_rows, 'by', axis=3, tiled=True)  51.1 us
    dot_general x162, matrix products, forward_taps(): jnp.einsum('oc,cxyz->oxyz', kernel[number], window_at(padded, starts, ext...  45.4 us
    ppermute x18, starting transfers between devices, extended(): after = lax.ppermute(first, axis, down)  23.5 us
    dot_general x54, matrix products, adjoint_taps(): jnp.einsum('kc,kxyz->cxyz', weights, stacked, preferred_element_type=jnp....  20.2 us
  transfers between devices with their start and end apart: 39, of which 30 were waited for; matrix products, arithmetic and copies ran while one was open for 4% of the time, Pallas kernels for 0%

commit v1 on v0

v1 whole, which is shorter than its diff:
```python
import math

import jax
import jax.numpy as jnp
import numpy as np
from jax import lax
from jax.experimental import pallas as pl
from jax.experimental.pallas import tpu as pltpu
from jax.sharding import Mesh, PartitionSpec as P


BF = jnp.bfloat16
F32 = jnp.float32
LAYERS = 4
AXES = ("b", "q", "g")
FINE_STEP = 0.5
COARSE_STEP = 1.5
NOW, PREV, OWN = 10, 8, 2
CHUNK = 2 * (NOW + PREV + OWN)


def window_start(b, q, g):
    return 4 * (4 * b + g) - 6 + 2 * q


def send_tables():
    first = np.zeros((128, 16, 256), np.float32)
    middle = np.zeros((128, 8, 512), np.float32)
    final = np.zeros((128, 16, 256), np.float32)
    for target in range(128):
        start = window_start(target // 16, target // 4 % 4, target % 4)
        for k in range(2 * NOW):
            at = start + k % NOW
            if 0 <= at < 128:
                if k < 16:
                    first[target, k, 2 * at + k // NOW] = 1
                else:
                    middle[target, k - 16, 2 * at + k // NOW] = 1
        for k in range(2 * OWN):
            at = start + 4 + k % OWN
            if 0 <= at < 128:
                middle[target, 4 + k, 256 + 128 * (k // OWN) + at] = 1
        for k in range(2 * PREV):
            at = start + 1 + k % PREV
            if 0 <= at < 128:
                final[target, k, 2 * at + k // PREV] = 1
    return (
        first.reshape(2048, 256).astype(BF),
        middle.reshape(1024, 512).astype(BF),
        final.reshape(2048, 256).astype(BF),
    )


def lane_table():
    table = np.zeros((128, 128), np.float32)
    for c in range(32):
        for ab in range(4):
            table[ab * 32 + c, c * 4 + ab] = 1
    return table.astype(BF)


def swap_table(outer, inner):
    table = np.zeros((outer * inner,) * 2, np.float32)
    for i in range(outer):
        for j in range(inner):
            table[j * outer + i, i * inner + j] = 1
    return table.astype(BF)


def haar_table():
    table = np.zeros((256, 256), np.float32)
    for code in range(8):
        a, b, d = code >> 2, code >> 1 & 1, code & 1
        for h in range(8):
            sign = (-1) ** bin(h & code).count("1")
            for c in range(32):
                table[128 * d + 64 * a + 32 * b + c, 8 * c + h] = sign
    return table.astype(BF)


def receive_table():
    table = np.zeros((128, 8, 256), np.float32)
    for source in range(128):
        group = 4 * (source // 16) + source % 4
        for k in range(8):
            table[source, k, 128 * (k // 4) + 4 * group + k % 4] = 1
    return table.reshape(1024, 256).astype(BF)


def dot(x, y):
    return jnp.dot(x, y, preferred_element_type=F32)


def dot_nt(x, y):
    return lax.dot_general(x, y, (((1,), (1,)), ((), ())), preferred_element_type=F32)


def vmem(n):
    return [pl.BlockSpec(memory_space=pltpu.VMEM)] * n


def pack_kernel(now, prev, cot, lanes, first, middle, final, out):
    now_rows = dot(lanes[...], now[...].astype(BF)).astype(BF)
    prev_rows = dot(lanes[...], prev[...].astype(BF)).astype(BF)
    both = jnp.concatenate([now_rows, cot[0:128, :], cot[128:256, :]], axis=1)
    part = 32
    for t in range(0, 128, part):
        one = dot_nt(first[pl.ds(16 * t, 16 * part), :], now_rows).reshape(part, 16, 128)
        two = dot_nt(middle[pl.ds(8 * t, 8 * part), :], both).reshape(part, 8, 128)
        three = dot_nt(final[pl.ds(16 * t, 16 * part), :], prev_rows).reshape(part, 16, 128)
        out[pl.ds(t, part)] = jnp.concatenate([one, two, three], axis=1).astype(BF)


def tap_index(dx, dy, dz, a2, b2, d2, a, b, d):
    def offset(moved, bit, to):
        place = (-1 if bit else 2) if moved else bit
        return place - to

    e = (offset(dx, a, a2), offset(dy, b, b2), offset(dz, d, d2))
    if any(abs(v) > 1 for v in e):
        return None
    return 9 * (e[0] + 1) + 3 * (e[1] + 1) + e[2] + 1


def weight_kernel(forward, adjoint, tile, out, wide):
    lane = lax.broadcasted_iota(jnp.int32, (32, 128), 1)
    masks = [jnp.where(lane // 32 == v, 1.0, 0.0).astype(BF) for v in range(4)]
    for way in range(2):
        source = (forward, adjoint)[way]
        wide[...] = dot(source[0], tile[...]).astype(BF).reshape(27, 32, 128)
        for moved in range(8):
            dx, dy, dz = moved >> 2, moved >> 1 & 1, moved & 1
            for u in range(8):
                d, a, b = u >> 2, u >> 1 & 1, u & 1
                for d2 in range(2):
                    total = jnp.zeros((32, 128), BF)
                    for v in range(4):
                        tap = tap_index(dx, dy, dz, v >> 1, v & 1, d2, a, b, d)
                        if tap is not None:
                            total = total + masks[v] * wide[26 - tap if way else tap]
                    out[0, way, moved, 32 * u : 32 * u + 32, 128 * d2 : 128 * d2 + 128] = total


def side_rows(v):
    row = lax.broadcasted_iota(jnp.int32, (16, 256), 0)
    axis = v.ndim - 2
    before = jnp.where(row == 0, 0.0, pltpu.roll(v, 1, axis))
    after = jnp.where(row == 15, 0.0, pltpu.roll(v, 15, axis))
    return before, after


def moved_rows(v):
    lane = lax.broadcasted_iota(jnp.int32, (16, 256), 1)
    before, after = side_rows(v)
    return jnp.where(lane // 32 % 2 == 1, before, after)


def block_conv(plain, turned, weights, x0, xs, z0, zs):
    rows = xs * zs * 16
    lane = lax.broadcasted_iota(jnp.int32, (1, 1, 16, 256), 3)
    high = lane // 64 % 2 == 1
    total = jnp.zeros((rows, 256), F32)

    def at(ref, dx, moved_z):
        xsl = pl.ds(x0 + 1 + dx, xs)
        if not moved_z:
            return ref[xsl, pl.ds(z0 + 1, zs)]
        return jnp.concatenate(
            [ref[xsl, pl.ds(z0 + 2, zs), :, 0:128], ref[xsl, pl.ds(z0, zs), :, 128:256]], axis=-1
        )

    for moved in range(8):
        dx, dy, dz = moved >> 2, moved >> 1 & 1, moved & 1
        ref = turned if dy else plain
        if dx:
            left = jnp.where(high, at(ref, -1, dz), at(ref, 1, dz))
        else:
            left = at(ref, 0, dz)
        total = total + dot(left.reshape(rows, 256), weights[moved])
    return total


def fine_kernel(place, chunk, weights, swap, haar, mid, base, cur, old, s0, s1, h0, h1):
    start = place[0]
    for ref in (s0, s1, h0, h1):
        for x in (0, 9):
            ref[x] = jnp.zeros((NOW + 2, 16, 256), BF)
        for z in (0, NOW + 1):
            ref[:, z] = jnp.zeros((10, 16, 256), BF)

    def keep(z):
        at = start + z
        return jnp.where((at >= 0) & (at < 128), 1.0, 0.0).astype(F32)

    def unpack(x, carry):
        rows = chunk[x].astype(F32)
        parts = []
        for k in range(0, CHUNK, 8):
            group = rows[:, k : k + 8, :].reshape(128, 128).astype(BF)
            moved = dot(swap[...], group)
            parts += [moved[16 * j : 16 * j + 16] for j in range(8)]
        for z in range(NOW):
            v = jnp.concatenate([parts[z], parts[NOW + z]], axis=1)
            cur[x, z] = v
            s0[x + 1, z + 1] = v.astype(BF)
            s1[x + 1, z + 1] = moved_rows(v).astype(BF)
        at = 2 * NOW
        for z in range(OWN):
            v = jnp.concatenate([parts[at + z], parts[at + OWN + z]], axis=1)
            mid[1, x, z] = v.astype(BF)
        at = 2 * (NOW + OWN)
        for z in range(PREV):
            old[x, z + 1] = jnp.concatenate([parts[at + z], parts[at + PREV + z]], axis=1)
        return carry

    lax.fori_loop(0, 8, unpack, 0)

    now, before = cur, old
    for layer in range(LAYERS):
        zs = NOW - 2 * layer
        xs = 4 if zs > 6 else 8

        def squash(i, carry, layer=layer, zs=zs, xs=xs):
            x0 = i * xs
            v = jnp.tanh(block_conv(s0, s1, weights.at[layer, 0], x0, xs, layer, zs))
            v = v.reshape(xs, zs, 16, 256)
            for z in range(zs):
                part = v[:, z] * keep(layer + z)
                h0[pl.ds(x0 + 1, xs), layer + z + 1] = part.astype(BF)
                h1[pl.ds(x0 + 1, xs), layer + z + 1] = moved_rows(part).astype(BF)
            return carry

        lax.fori_loop(0, 8 // xs, squash, 0)
        zs = NOW - 2 * layer - 2
        xs = 4 if zs > 6 else 8
        last = layer == LAYERS - 1

        def update(i, carry, layer=layer, zs=zs, xs=xs, now=now, before=before, last=last):
            x0 = i * xs
            v = block_conv(h0, h1, weights.at[layer, 1], x0, xs, layer + 1, zs)
            v = v.reshape(xs, zs, 16, 256)
            for z in range(zs):
                at = layer + 1 + z
                here = (pl.ds(x0, xs), at)
                part = (2.0 * now[here] - before[here] - FINE_STEP * v[:, z]) * keep(at)
                before[here] = part
                if not last:
                    s0[pl.ds(x0 + 1, xs), at + 1] = part.astype(BF)
                    s1[pl.ds(x0 + 1, xs), at + 1] = moved_rows(part).astype(BF)
            return carry

        lax.fori_loop(0, 8 // xs, update, 0)
        now, before = before, now

    def coarse(v):
        top = v.astype(BF)
        low = (v - top.astype(F32)).astype(BF)
        return (dot(top, haar[...]) + dot(low, haar[...])) * (1.0 / math.sqrt(8.0))

    own = (slice(None), slice(4, 6))
    latest = now[own].reshape(256, 256)
    earlier = before[own].reshape(256, 256)
    mid[0] = coarse(latest).astype(BF).reshape(8, 2, 16, 256)
    base[...] = coarse(2.0 * latest - earlier).reshape(8, 2, 16, 256)


def coarse_kernel_body(place, states, base, w0, w1, w2, w3, swap, out, state, hidden, weights, sems):
    start = place[0]
    quarter = place[1]
    copies = []
    for i, w in enumerate((w0, w1, w2, w3)):
        copy = pltpu.make_async_copy(w, weights.at[:, pl.ds(64 * i, 64), :], sems.at[i])
        copy.start()
        copies.append(copy)
    for s in range(2):
        for y in range(3):
            for x in (0, 9):
                state[s, y, x] = jnp.zeros((8, 16, 256), BF)
                hidden[s, y, x] = jnp.zeros((6, 16, 256), BF)
    for s in range(2):
        for q in range(4):
            piece = states[q, s]
            wide = piece.astype(F32)
            before, after = side_rows(wide)
            here = (pl.ds(1, 8), pl.ds(2 * q, 2))
            state[(s, 0) + here] = before.astype(BF)
            state[(s, 1) + here] = piece
            state[(s, 2) + here] = after.astype(BF)
    for copy in copies:
        copy.wait()
    taps = [(x, y, z) for x in (-1, 0, 1) for y in (-1, 0, 1) for z in (-1, 0, 1)]

    def forward(s):
        total = jnp.zeros((768, 256), F32)
        for number, (ex, ey, ez) in enumerate(taps):
            left = state[s, 1 + ey, pl.ds(1 + ex, 8), pl.ds(1 + ez, 6)].reshape(768, 256)
            total = total + dot_nt(left, weights[number])
        return total

    def adjoint(s):
        total = jnp.zeros((512, 256), F32)
        for number, (ex, ey, ez) in enumerate(taps):
            left = hidden[s, 1 - ey, pl.ds(1 - ex, 8), pl.ds(1 - ez, 4)].reshape(512, 256)
            total = total + dot(left, weights[number])
        return total

    def store(s, v):
        v = v.reshape(8, 6, 16, 256)
        for z in range(6):
            at = start + z
            part = v[:, z] * jnp.where((at >= 0) & (at < 128), 1.0, 0.0).astype(F32)
            before, after = side_rows(part)
            hidden[s, 0, pl.ds(1, 8), z] = before.astype(BF)
            hidden[s, 1, pl.ds(1, 8), z] = part.astype(BF)
            hidden[s, 2, pl.ds(1, 8), z] = after.astype(BF)

    squash = jnp.tanh(forward(0))
    store(0, squash)
    store(1, (1.0 - squash * squash) * forward(1))
    force = (-COARSE_STEP * adjoint(0)).reshape(8, 4, 16, 256)
    pull = (-COARSE_STEP * adjoint(1)).reshape(8, 4, 16, 256)
    near = jnp.where(quarter == 1, 1.0, 0.0).astype(F32)
    far = jnp.where(quarter == 2, 1.0, 0.0).astype(F32)
    for x in range(8):
        ground = base[x]
        rows = jnp.concatenate([force[x, 0:2] + near * ground, force[x, 2:4] + far * ground, pull[x]], axis=0)
        out[x] = dot(swap[...], rows.reshape(128, 256).astype(BF)).astype(BF).reshape(16, 8, 256)


def local(fine_prev, fine_now, fine_kernels, coarse_kernel, cotangent):
    b, q, g = (lax.axis_index(name) for name in AXES)
    first, middle, final = send_tables()
    packed = pl.pallas_call(
        pack_kernel,
        out_shape=jax.ShapeDtypeStruct((128, CHUNK, 128), BF),
        in_specs=vmem(7),
        out_specs=pl.BlockSpec(memory_space=pltpu.VMEM),
        compiler_params=pltpu.CompilerParams(vmem_limit_bytes=48 << 20),
        name="pack",
    )(
        fine_now.reshape(128, 256),
        fine_prev.reshape(128, 256),
        cotangent.reshape(256, 128),
        lane_table(),
        first,
        middle,
        final,
    )
    chunk = lax.all_to_all(packed, AXES, 0, 0).reshape(8, 16, CHUNK, 128)

    tile = np.tile(np.eye(32, dtype=np.float32), (1, 4)).astype(BF)
    weights = pl.pallas_call(
        weight_kernel,
        grid=(LAYERS,),
        out_shape=jax.ShapeDtypeStruct((LAYERS, 2, 8, 256, 256), BF),
        in_specs=[
            pl.BlockSpec((1, 864, 32), lambda i: (i, 0, 0)),
            pl.BlockSpec((1, 864, 32), lambda i: (i, 0, 0)),
            pl.BlockSpec((32, 128), lambda i: (0, 0)),
        ],
        out_specs=pl.BlockSpec((1, 2, 8, 256, 256), lambda i: (i, 0, 0, 0, 0)),
        scratch_shapes=[pltpu.VMEM((27, 32, 128), BF)],
        compiler_params=pltpu.CompilerParams(vmem_limit_bytes=32 << 20),
        cost_estimate=pl.CostEstimate(flops=10**10, bytes_accessed=10**7, transcendentals=0),
        name="spread_weights",
    )(
        jnp.swapaxes(fine_kernels, 2, 3).reshape(LAYERS, 864, 32),
        fine_kernels.reshape(LAYERS, 864, 32),
        tile,
    )

    start = 4 * (4 * b + g) - 6 + 2 * q
    buffer = pltpu.VMEM((10, NOW + 2, 16, 256), BF)
    mid, base = pl.pallas_call(
        fine_kernel,
        out_shape=(
            jax.ShapeDtypeStruct((2, 8, OWN, 16, 256), BF),
            jax.ShapeDtypeStruct((8, OWN, 16, 256), F32),
        ),
        in_specs=[pl.BlockSpec(memory_space=pltpu.SMEM)] + vmem(4),
        out_specs=tuple(vmem(2)),
        scratch_shapes=[pltpu.VMEM((8, NOW, 16, 256), F32)] * 2 + [buffer] * 4,
        compiler_params=pltpu.CompilerParams(vmem_limit_bytes=56 << 20),
        cost_estimate=pl.CostEstimate(flops=10**10, bytes_accessed=10**7, transcendentals=10**6),
        name="fine_layers",
    )(jnp.stack([start, q]).astype(jnp.int32), chunk, weights, swap_table(16, 8), haar_table())

    across = lax.ppermute(coarse_kernel, "g", [(i, i ^ 2) for i in range(4)])
    there = lax.ppermute(coarse_kernel, "g", [(i, i ^ 1) for i in range(4)])
    opposite = lax.ppermute(across, "g", [(i, i ^ 1) for i in range(4)])
    states = lax.all_gather(mid, "q")
    partial = pl.pallas_call(
        coarse_kernel_body,
        out_shape=jax.ShapeDtypeStruct((8, 16, 8, 256), BF),
        in_specs=[pl.BlockSpec(memory_space=pltpu.SMEM)] + vmem(2) + [pl.BlockSpec(memory_space=pl.ANY)] * 4 + vmem(1),
        out_specs=pl.BlockSpec(memory_space=pltpu.VMEM),
        scratch_shapes=[
            pltpu.VMEM((2, 3, 10, 8, 16, 256), BF),
            pltpu.VMEM((2, 3, 10, 6, 16, 256), BF),
            pltpu.VMEM((27, 256, 256), BF),
            pltpu.SemaphoreType.DMA((4,)),
        ],
        compiler_params=pltpu.CompilerParams(vmem_limit_bytes=56 << 20),
        cost_estimate=pl.CostEstimate(flops=2 * 10**10, bytes_accessed=10**7, transcendentals=10**6),
        name="coarse_layer",
    )(
        jnp.stack([4 * (4 * b + g) - 1, q]).astype(jnp.int32),
        states,
        base,
        coarse_kernel,
        across,
        there,
        opposite,
        swap_table(8, 16),
    )
    parts = lax.all_to_all(partial.reshape(128, 8, 256), AXES, 0, 0)
    sums = lax.dot_general(
        parts.reshape(1024, 256), receive_table(), (((0,), (0,)), ((), ())), preferred_element_type=F32
    )
    coarse_next = sums[:, 0:128].reshape(256, 1, 1, 128)
    state_adjoint = 2.0 * cotangent.astype(F32) + sums[:, 128:256].reshape(256, 1, 1, 128)
    return coarse_next, state_adjoint


def solution(mesh):
    split = Mesh(mesh.devices.reshape(8, 4, 4), AXES)
    rows = P(None, "b", ("q", "g"), None)
    return jax.shard_map(
        local,
        mesh=split,
        in_specs=(rows, rows, P(), P(None, ("q", "g"), None), rows),
        out_specs=(rows, rows),
        check_vma=False,
    )
```

time: 475 us -> 135 us (0.28); the launches traced: 465 us -> 133 us
  waiting for transfers between devices: 244 us -> 33.4 us
  starting transfers between devices: 105 us -> 12.9 us
  matrix products: 66.2 us -> 0.33 us
  Pallas kernels: 0 us -> 35.7 us
  blocking collectives: 0 us -> 22.1 us
  local copies, waits for them, and re-layouts: 25.1 us -> 12.9 us
  other arithmetic: 9.17 us -> 1.97 us
    reduce_scatter x2 -> x0, waiting for transfers between devices: 116 us -> none  [the longest x1 63 us: local(): lax.psum_scatter(force_part, 'by', scatter_dimension=2, tiled=True)]
    ppermute x36 -> x3, starting transfers between devices: 105 us -> 1.74 us  [the longest x1 1.16 us: local(): across = lax.ppermute(coarse_kernel, 'g', [(i, i ^ 2) for i in range(4)])]
    ppermute x36 -> x3, waiting for transfers between devices: 76.3 us -> 2.73 us  [the longest x1 1.47 us: local(): there = lax.ppermute(coarse_kernel, 'g', [(i, i ^ 1) for i in range(4)])]
    dot_general x218 -> x1, matrix products: 66.2 us -> 0.33 us  [local(): lax.dot_general(parts.reshape(1024, 256), receive_table(), (((0,), (0,)),...]
    pallas_call x0 -> x4, Pallas kernels: none -> 35.7 us  [the longest x1 17.7 us: local(): pl.pallas_call(fine_kernel, out_shape=(jax.ShapeDtypeStruct((2, 8, OWN, 1...]
    all_gather x1, waiting for transfers between devices: 51.1 us -> 16.8 us  [local(): states = lax.all_gather(mid, 'q')]
    all_to_all x0 -> x1, blocking collectives: none -> 22.1 us  [local(): parts = lax.all_to_all(partial.reshape(128, 8, 256), AXES, 0, 0)]
    slice x51 -> x1, local copies, waits for them, and re-layouts: 15 us -> 0.66 us  [local(): coarse_next = sums[:, 0:128].reshape(256, 1, 1, 128)]
  transfers between devices with their start and end apart: 39 -> 5, of which waited for: 30 -> 4; matrix products, arithmetic and copies ran while one was open for 4% -> 1% of each run, Pallas kernels for 0% -> 15%
where the time goes in v1:
time: 135 us; the launch traced here: 133 us
  Pallas kernels  35.7 us (26%)
  waiting for transfers between devices  33.4 us (25%)
  blocking collectives  22.1 us (16%)
  between operations  14.1 us (10%)
  local copies, waits for them, and re-layouts  12.9 us (10%)
  starting transfers between devices  12.9 us (10%)
  other arithmetic  1.97 us (1%)
    all_to_all x1, blocking collectives, local(): parts = lax.all_to_all(partial.reshape(128, 8, 256), AXES, 0, 0)  22.1 us
    pallas_call x1, Pallas kernels, local(): pl.pallas_call(fine_kernel, out_shape=(jax.ShapeDtypeStruct((2, 8, OWN, 1...  17.7 us
    all_gather x1, waiting for transfers between devices, local(): states = lax.all_gather(mid, 'q')  16.8 us
    all_to_all x1, waiting for transfers between devices, local(): chunk = lax.all_to_all(packed, AXES, 0, 0).reshape(8, 16, CHUNK, 128)  13.9 us
    pallas_call x1, Pallas kernels, local(): pl.pallas_call(coarse_kernel_body, out_shape=jax.ShapeDtypeStruct((8, 16,...  13.8 us
    all_to_all x1, starting transfers between devices, local(): chunk = lax.all_to_all(packed, AXES, 0, 0).reshape(8, 16, CHUNK, 128)  11.1 us
    unnamed x26, local copies, waits for them, and re-layouts  9.67 us
  transfers between devices with their start and end apart: 5, of which 4 were waited for; matrix products, arithmetic and copies ran while one was open for 1% of the time, Pallas kernels for 15%

profile of v1, /device:TPU:0, one launch (start us, length us, event | category | flops | bytes accessed | tf_op | source)
XLA Modules:
  0.0 133.4 jit_solution(7932271442653994715)
XLA Ops:
  7.2 1.0 reshape.34.now
  8.2 1.0 reshape.35.prev
  9.2 1.2 copy-done
  10.4 1.2 copy-done.1
  11.6 1.2 copy-done.2
  12.8 0.8 copy-done.4
  13.7 0.8 copy-done.6
  14.4 2.3 %pack.1 = bf16[128,40,128]{2,1,0:T(8,128)(2,1)} custom-call(f32[128,256]{1,0:T(8,128)S(1)} %reshape.34.now, f32[128,256]{1,0:T(8,128)S(1)} %reshape.35.prev, bf16[256,128]{1,0:T(8,128)(2,1)S(1)} %bitcast.25, bf16[128,128]{1,0:T(8,128)(2,1)S(1)} %copy-done.6, bf16[2048,256]{1,0:T(8,128)(2,1)S(1)} %copy-done, bf16[1024,512]{1,0:T(8,128)(2,1)S(1)} %copy-done.1, ...), custom_call_target="tpu_custom_call" | custom-call | tf_op jit(solution)/shard_map/pack/pallas_call | solution.py:333
  16.7 11.1 %all-to-all-start = ((bf16[128,40,128]{2,1,0:T(8,128)(2,1)}), bf16[128,40,128]{2,1,0:T(8,128)(2,1)S(1)}, u32[]{:S(2)}, u32[]{:S(2)}) async-start(bf16[128,40,128]{2,1,0:T(8,128)(2,1)} %pack.1), calls=%async_computation | async-start | bytes 2621440 | tf_op jit(solution)/shard_map/all_to_all | solution.py:349
  27.9 1.2 collective-permute-start
  29.7 0.7 pad_add_fusion.1.place
  30.3 1.9 %spread_weights.1.weights = bf16[4,2,8,256,256]{4,3,2,1,0:T(8,128)(2,1)S(1)} custom-call(bf16[4,864,32]{2,1,0:T(8,128)(2,1)S(1)} %bitcast.24, bf16[4,864,32]{2,1,0:T(8,128)(2,1)S(1)} %bitcast.23, bf16[32,128]{1,0:T(8,128)(2,1)S(1)} %copy-done.7), custom_call_target="tpu_custom_call" | custom-call | flops 10000000000 | bytes 10000000 | tf_op jit(solution)/shard_map/spread_weights/pallas_call | solution.py:352
  32.3 3.2 %copy-done.8 = bf16[4,2,8,256,256]{4,3,2,1,0:T(8,128)(2,1)} copy-done((bf16[4,2,8,256,256]{4,3,2,1,0:T(8,128)(2,1)}, bf16[4,2,8,256,256]{4,3,2,1,0:T(8,128)(2,1)S(1)}, u32[]{:S(2)}) %copy-start.8) | copy-done | bytes 8388632
  35.5 13.9 %all-to-all-done = bf16[128,40,128]{2,1,0:T(8,128)(2,1)S(1)} async-done(((bf16[128,40,128]{2,1,0:T(8,128)(2,1)}), bf16[128,40,128]{2,1,0:T(8,128)(2,1)S(1)}, u32[]{:S(2)}, u32[]{:S(2)}) %all-to-all-start) | async-done | bytes 1310752 | tf_op jit(solution)/shard_map/all_to_all | solution.py:349
  49.4 1.1 copy-done.9
  50.5 17.7 %fine_layers.1 = (bf16[2,8,2,16,256]{4,3,2,1,0:T(8,128)(2,1)}, f32[8,2,16,256]{3,2,1,0:T(8,128)}) custom-call(s32[2]{0:T(128)} %pad_add_fusion.1.place, bf16[8,16,40,128]{3,2,1,0:T(8,128)(2,1)} %bitcast.26, bf16[4,2,8,256,256]{4,3,2,1,0:T(8,128)(2,1)} %copy-done.8, bf16[128,128]{1,0:T(8,128)(2,1)} %constant.48.clone.swap, bf16[256,256]{1,0:T(8,128)(2,1)} %constant.49.clone.haar), custom_call_target="tpu_custom_call" | custom-call | flops 10000000000 | bytes 10000000 | tf_op jit(solution)/shard_map/fine_layers/pallas_call | solution.py:374
  68.8 0.7 pad_add_fusion.place
  69.5 1.5 %collective-permute-done.1.w2 = bf16[27,64,256]{2,1,0:T(8,128)(2,1)S(1)} collective-permute-done((bf16[27,64,256]{2,1,0:T(8,128)(2,1)}, bf16[27,64,256]{2,1,0:T(8,128)(2,1)S(1)}, u32[]{:S(2)}, u32[]{:S(2)}) %collective-permute-start.1) | collective-permute-done | bytes 884768 | tf_op jit(solution)/shard_map/ppermute | solution.py:389
  70.9 1.3 collective-permute-done.2.w3
  72.2 16.8 %all-gather.3.cloned.1.call-done = bf16[8,8,2,16,256]{4,3,2,1,0:T(8,128)(2,1)} async-done(((bf16[2,8,2,16,256]{4,3,2,1,0:T(8,128)(2,1)}), bf16[8,8,2,16,256]{4,3,2,1,0:T(8,128)(2,1)}) %all-gather.3.cloned.1.call-update) | async-done | bytes 1048592 | tf_op jit(solution)/shard_map/all_gather | solution.py:391
  89.0 13.8 %coarse_layer.1 = bf16[8,16,8,256]{3,2,1,0:T(8,128)(2,1)} custom-call(s32[2]{0:T(128)} %pad_add_fusion.place, bf16[4,2,8,2,16,256]{5,4,3,2,1,0:T(8,128)(2,1)} %bitcast.30, f32[8,2,16,256]{3,2,1,0:T(8,128)} %get-tuple-element.5.base, bf16[27,64,256]{2,1,0:T(8,128)(2,1)} %w0.1, bf16[27,64,256]{2,1,0:T(8,128)(2,1)} %collective-permute-done.w1, ...), custom_call_target="tpu_custom_call" | custom-call | flops 20000000000 | bytes 10000000 | tf_op jit(solution)/shard_map/coarse_layer/pallas_call | solution.py:392
  102.8 22.1 %all_to_all.10 = bf16[128,8,256]{2,1,0:T(8,128)(2,1)S(1)} all-to-all(bf16[128,8,256]{2,1,0:T(8,128)(2,1)} %bitcast.27), channel_id=1, replica_groups=mesh['b'=8,'q'=4,'g'=4] {'b','q','g'}, dimensions={0} | all-to-all | bytes 1048576 | tf_op jit(solution)/shard_map/all_to_all | solution.py:416
  125.2 0.7 slice.8
  125.9 0.7 fusion.2
  (26 shorter events, 1.6 us)
Async XLA Ops:
  9.2 1.2 copy-start
  10.4 1.2 copy-start.1
  11.6 1.2 copy-start.2
  12.8 0.8 copy-start.4
  13.7 0.8 copy-start.6
  16.7 12.4 %copy-start.3 = (bf16[4,27,32,32]{3,2,1,0:T(8,128)(2,1)S(1)}, bf16[4,27,32,32]{3,2,1,0:T(8,128)(2,1)}, u32[]{:S(2)}) copy-start(bf16[4,27,32,32]{3,2,1,0:T(8,128)(2,1)} %param.16) | copy-start | bytes 663556
  16.7 32.7 %all-to-all-start = ((bf16[128,40,128]{2,1,0:T(8,128)(2,1)}), bf16[128,40,128]{2,1,0:T(8,128)(2,1)S(1)}, u32[]{:S(2)}, u32[]{:S(2)}) async-start(bf16[128,40,128]{2,1,0:T(8,128)(2,1)} %pack.1), calls=%async_computation | async-start | bytes 2621440 | tf_op jit(solution)/shard_map/all_to_all | solution.py:349
  27.9 2.5 %copy-start.7 = (bf16[32,128]{1,0:T(8,128)(2,1)S(1)}, bf16[32,128]{1,0:T(8,128)(2,1)}, u32[]{:S(2)}) copy-start(bf16[32,128]{1,0:T(8,128)(2,1)} %constant.47.clone.tile) | copy-start | bytes 24580
  27.9 61.1 %all-gather.3.cloned.1.call-start = ((), (), s32[]{:S(2)}) async-start(), calls=%async_computation.2 | async-start | bytes 1310720 | tf_op jit(solution)/shard_map/all_gather | solution.py:391
  27.9 40.4 %collective-permute-start = (bf16[27,64,256]{2,1,0:T(8,128)(2,1)}, bf16[27,64,256]{2,1,0:T(8,128)(2,1)}, u32[]{:S(2)}, u32[]{:S(2)}) collective-permute-start(bf16[27,64,256]{2,1,0:T(8,128)(2,1)} %w0.1), channel_id=1, source_target_pairs={{0,2},{1,3},{2,0},{3,1},{4,6},{5,7},{6,4},{7,5},{8,10},{9,11},{10,... | collective-permute-start | bytes 2654216 | tf_op jit(solution)/shard_map/ppermute | solution.py:388
  32.2 3.2 %copy-start.8 = (bf16[4,2,8,256,256]{4,3,2,1,0:T(8,128)(2,1)}, bf16[4,2,8,256,256]{4,3,2,1,0:T(8,128)(2,1)S(1)}, u32[]{:S(2)}) copy-start(bf16[4,2,8,256,256]{4,3,2,1,0:T(8,128)(2,1)S(1)} %spread_weights.1.weights) | copy-start | bytes 25165828
  49.4 1.1 copy-start.9
  68.2 2.7 %collective-permute-start.1 = (bf16[27,64,256]{2,1,0:T(8,128)(2,1)}, bf16[27,64,256]{2,1,0:T(8,128)(2,1)S(1)}, u32[]{:S(2)}, u32[]{:S(2)}) collective-permute-start(bf16[27,64,256]{2,1,0:T(8,128)(2,1)} %w0.1), channel_id=1, source_target_pairs={{0,1},{1,0},{2,3},{3,2},{4,5},{5,4},{6,7},{7,6},{8,9},{9,8},{10,11... | collective-permute-start | bytes 2654216 | tf_op jit(solution)/shard_map/ppermute | solution.py:389
  68.3 3.9 %collective-permute-start.2 = (bf16[27,64,256]{2,1,0:T(8,128)(2,1)}, bf16[27,64,256]{2,1,0:T(8,128)(2,1)S(1)}, u32[]{:S(2)}, u32[]{:S(2)}) collective-permute-start(bf16[27,64,256]{2,1,0:T(8,128)(2,1)} %collective-permute-done.w1), channel_id=1, source_target_pairs={{0,1},{1,0},{2,3},{3,2},{4,5},{5,4},{6,7},{7,6},{8,9},{9,8},{10,11... | collective-permute-start | bytes 2654216 | tf_op jit(solution)/shard_map/ppermute | solution.py:390
  70.9 18.0 %copy-start.11 = (bf16[27,64,256]{2,1,0:T(8,128)(2,1)}, bf16[27,64,256]{2,1,0:T(8,128)(2,1)S(1)}, u32[]{:S(2)}) copy-start(bf16[27,64,256]{2,1,0:T(8,128)(2,1)S(1)} %collective-permute-done.1.w2) | copy-start | bytes 2654212
  72.2 16.8 %copy-start.12 = (bf16[27,64,256]{2,1,0:T(8,128)(2,1)}, bf16[27,64,256]{2,1,0:T(8,128)(2,1)S(1)}, u32[]{:S(2)}) copy-start(bf16[27,64,256]{2,1,0:T(8,128)(2,1)S(1)} %collective-permute-done.2.w3) | copy-start | bytes 2654212
  89.0 35.9 %copy-start.10 = (bf16[1024,256]{1,0:T(8,128)(2,1)S(1)}, bf16[1024,256]{1,0:T(8,128)(2,1)}, u32[]{:S(2)}) copy-start(bf16[1024,256]{1,0:T(8,128)(2,1)} %constant.51.clone) | copy-start | bytes 1572868
  102.8 23.1 %copy-start.5 = (bf16[256,1,1,128]{3,0,2,1:T(8,128)(2,1)S(1)}, bf16[256,1,1,128]{3,0,2,1:T(8,128)(2,1)}, u32[]{:S(2)}) copy-start(bf16[256,1,1,128]{3,0,2,1:T(8,128)(2,1)} %param.18) | copy-start | bytes 196612
Sparse Core Ops, SparseCore 0:
  68.3 20.5 all-gather.2

commit v2 on v1

--- a/solution.py
+++ b/solution.py
@@ -23,59 +23,25 @@
     return 4 * (4 * b + g) - 6 + 2 * q
 
 
-def send_tables():
-    first = np.zeros((128, 16, 256), np.float32)
-    middle = np.zeros((128, 8, 512), np.float32)
-    final = np.zeros((128, 16, 256), np.float32)
-    for target in range(128):
-        start = window_start(target // 16, target // 4 % 4, target % 4)
-        for k in range(2 * NOW):
-            at = start + k % NOW
-            if 0 <= at < 128:
-                if k < 16:
-                    first[target, k, 2 * at + k // NOW] = 1
-                else:
-                    middle[target, k - 16, 2 * at + k // NOW] = 1
-        for k in range(2 * OWN):
-            at = start + 4 + k % OWN
-            if 0 <= at < 128:
-                middle[target, 4 + k, 256 + 128 * (k // OWN) + at] = 1
-        for k in range(2 * PREV):
-            at = start + 1 + k % PREV
-            if 0 <= at < 128:
-                final[target, k, 2 * at + k // PREV] = 1
-    return (
-        first.reshape(2048, 256).astype(BF),
-        middle.reshape(1024, 512).astype(BF),
-        final.reshape(2048, 256).astype(BF),
-    )
-
-
-def lane_table():
-    table = np.zeros((128, 128), np.float32)
-    for c in range(32):
-        for ab in range(4):
-            table[ab * 32 + c, c * 4 + ab] = 1
-    return table.astype(BF)
+def iota(shape, axis):
+    return lax.broadcasted_iota(jnp.int32, shape, axis)
+
+
+def ones_where(mask):
+    return jnp.where(mask, 1.0, 0.0).astype(F32)
 
 
 def swap_table(outer, inner):
-    table = np.zeros((outer * inner,) * 2, np.float32)
-    for i in range(outer):
-        for j in range(inner):
-            table[j * outer + i, i * inner + j] = 1
-    return table.astype(BF)
-
-
-def haar_table():
-    table = np.zeros((256, 256), np.float32)
-    for code in range(8):
-        a, b, d = code >> 2, code >> 1 & 1, code & 1
-        for h in range(8):
-            sign = (-1) ** bin(h & code).count("1")
-            for c in range(32):
-                table[128 * d + 64 * a + 32 * b + c, 8 * c + h] = sign
-    return table.astype(BF)
+    n = outer * inner
+    row, column = iota((n, n), 0), iota((n, n), 1)
+    return ones_where(column == row % outer * inner + row // outer).astype(BF)
+
+
+def haar_signs(lane, channel):
+    code = lane // 64 % 2 * 4 + lane // 32 % 2 * 2 + lane // 128
+    both = code & channel % 8
+    odd = (both ^ both // 2 ^ both // 4) & 1
+    return jnp.where(lane % 32 == channel // 8, 1.0 - 2.0 * odd.astype(F32), 0.0).astype(BF)
 
 
 def receive_table():
@@ -99,16 +65,54 @@
     return [pl.BlockSpec(memory_space=pltpu.VMEM)] * n
 
 
-def pack_kernel(now, prev, cot, lanes, first, middle, final, out):
-    now_rows = dot(lanes[...], now[...].astype(BF)).astype(BF)
-    prev_rows = dot(lanes[...], prev[...].astype(BF)).astype(BF)
+def parity_rows(ref):
+    return jnp.concatenate([ref[:, a, b, :] for a in range(2) for b in range(2)], axis=0)
+
+
+def pack_kernel(now, prev, cot, out, first, middle, final):
+    now_rows = parity_rows(now)
+    speed = (now_rows - parity_rows(prev)).astype(BF)
+    now_rows = now_rows.astype(BF)
     both = jnp.concatenate([now_rows, cot[0:128, :], cot[128:256, :]], axis=1)
+    k, lane = iota((16, 256), 0), iota((16, 256), 1)
+    for_first = lane - 2 * (k % NOW) - k // NOW
+    for_final = lane - 2 * (1 + k % PREV) - k // PREV
+    k, lane = iota((8, 512), 0), iota((8, 512), 1)
+    for_middle = jnp.where(k < 4, jnp.where(lane < 256, lane - 2 * (k + 6) - 1, -1000), -1000)
+    at = 2 * (lane % 128 - 4 - k % OWN)
+    for_middle = jnp.where((k >= 4) & (lane >= 256) & (lane // 128 - 2 == (k - 4) // OWN), at, for_middle)
+    for target in range(128):
+        at = 2 * window_start(target // 16, target // 4 % 4, target % 4)
+        first[16 * target : 16 * target + 16] = ones_where(for_first == at).astype(BF)
+        final[16 * target : 16 * target + 16] = ones_where(for_final == at).astype(BF)
+        middle[8 * target : 8 * target + 8] = ones_where(for_middle == at)
     part = 32
     for t in range(0, 128, part):
         one = dot_nt(first[pl.ds(16 * t, 16 * part), :], now_rows).reshape(part, 16, 128)
-        two = dot_nt(middle[pl.ds(8 * t, 8 * part), :], both).reshape(part, 8, 128)
-        three = dot_nt(final[pl.ds(16 * t, 16 * part), :], prev_rows).reshape(part, 16, 128)
+        two = dot_nt(middle[pl.ds(8 * t, 8 * part), :].astype(BF), both).reshape(part, 8, 128)
+        three = dot_nt(final[pl.ds(16 * t, 16 * part), :], speed).reshape(part, 16, 128)
         out[pl.ds(t, part)] = jnp.concatenate([one, two, three], axis=1).astype(BF)
+
+
+def split_dot(x, y, exact_left):
+    wide = y if exact_left else x
+    top = wide.astype(BF)
+    rest = wide - top.astype(F32)
+    low = rest.astype(BF)
+    last = (rest - low.astype(F32)).astype(BF)
+    if exact_left:
+        return dot(x, top) + dot(x, low) + dot(x, last)
+    return dot(top, y) + dot(low, y) + dot(last, y)
+
+
+def drift_kernel(now, prev, out):
+    rows = 6.0 * parity_rows(now) - 5.0 * parity_rows(prev)
+    total = jnp.zeros((256, 128), F32)
+    for d in range(2):
+        pick = ones_where(iota((256, 128), 0) == 2 * iota((256, 128), 1) + d).astype(BF)
+        signs = haar_signs(iota((256, 128), 1) + 128 * d, iota((256, 128), 0))
+        total = total + split_dot(signs, split_dot(rows, pick, False), True)
+    out[...] = total * (1.0 / math.sqrt(8.0))
 
 
 def tap_index(dx, dy, dz, a2, b2, d2, a, b, d):
@@ -180,8 +184,9 @@
     return total
 
 
-def fine_kernel(place, chunk, weights, swap, haar, mid, base, cur, old, s0, s1, h0, h1):
-    start = place[0]
+def fine_kernel(chunk, weights, mid, base, cur, old, line, s0, s1, h0, h1):
+    start = window_start(*(lax.axis_index(name) for name in AXES))
+    swap = swap_table(16, 8)
     for ref in (s0, s1, h0, h1):
         for x in (0, 9):
             ref[x] = jnp.zeros((NOW + 2, 16, 256), BF)
@@ -197,20 +202,19 @@
         parts = []
         for k in range(0, CHUNK, 8):
             group = rows[:, k : k + 8, :].reshape(128, 128).astype(BF)
-            moved = dot(swap[...], group)
+            moved = dot(swap, group)
             parts += [moved[16 * j : 16 * j + 16] for j in range(8)]
         for z in range(NOW):
             v = jnp.concatenate([parts[z], parts[NOW + z]], axis=1)
             cur[x, z] = v
             s0[x + 1, z + 1] = v.astype(BF)
             s1[x + 1, z + 1] = moved_rows(v).astype(BF)
-        at = 2 * NOW
-        for z in range(OWN):
-            v = jnp.concatenate([parts[at + z], parts[at + OWN + z]], axis=1)
-            mid[1, x, z] = v.astype(BF)
         at = 2 * (NOW + OWN)
         for z in range(PREV):
-            old[x, z + 1] = jnp.concatenate([parts[at + z], parts[at + PREV + z]], axis=1)
+            v = jnp.concatenate([parts[at + z], parts[at + PREV + z]], axis=1)
+            old[x, z + 1] = cur[x, z + 1] - v
+            if z in (3, 4):
+                line[x, z - 3] = cur[x, z + 1] + 5.0 * v
         return carry
 
     lax.fori_loop(0, 8, unpack, 0)
@@ -252,23 +256,24 @@
         lax.fori_loop(0, 8 // xs, update, 0)
         now, before = before, now
 
-    def coarse(v):
-        top = v.astype(BF)
-        low = (v - top.astype(F32)).astype(BF)
-        return (dot(top, haar[...]) + dot(low, haar[...])) * (1.0 / math.sqrt(8.0))
-
+    haar = haar_signs(iota((256, 256), 0), iota((256, 256), 1))
+    scale = 1.0 / math.sqrt(8.0)
     own = (slice(None), slice(4, 6))
     latest = now[own].reshape(256, 256)
     earlier = before[own].reshape(256, 256)
-    mid[0] = coarse(latest).astype(BF).reshape(8, 2, 16, 256)
-    base[...] = coarse(2.0 * latest - earlier).reshape(8, 2, 16, 256)
-
-
-def coarse_kernel_body(place, states, base, w0, w1, w2, w3, swap, out, state, hidden, weights, sems):
-    start = place[0]
-    quarter = place[1]
+    forced = 2.0 * latest - earlier - line[...].reshape(256, 256)
+    mid[...] = (split_dot(latest, haar, False) * scale).astype(BF).reshape(8, OWN, 16, 256)
+    base[...] = (split_dot(forced, haar, False) * scale).reshape(8, OWN, 16, 256)
+
+
+def coarse_kernel_body(*refs):
+    own, cots, base = refs[0:4], refs[4:8], refs[8]
+    pieces, out, state, hidden, weights, sems = refs[9:13], refs[13], refs[14], refs[15], refs[16], refs[17]
+    b, quarter, g = (lax.axis_index(name) for name in AXES)
+    start = 4 * (4 * b + g) - 1
+    swap = swap_table(16, 8)
     copies = []
-    for i, w in enumerate((w0, w1, w2, w3)):
+    for i, w in enumerate(pieces):
         copy = pltpu.make_async_copy(w, weights.at[:, pl.ds(64 * i, 64), :], sems.at[i])
         copy.start()
         copies.append(copy)
@@ -277,15 +282,25 @@
             for x in (0, 9):
                 state[s, y, x] = jnp.zeros((8, 16, 256), BF)
                 hidden[s, y, x] = jnp.zeros((6, 16, 256), BF)
-    for s in range(2):
-        for q in range(4):
-            piece = states[q, s]
-            wide = piece.astype(F32)
-            before, after = side_rows(wide)
-            here = (pl.ds(1, 8), pl.ds(2 * q, 2))
-            state[(s, 0) + here] = before.astype(BF)
-            state[(s, 1) + here] = piece
-            state[(s, 2) + here] = after.astype(BF)
+    def place(s, x, xs, z, wide):
+        before, after = side_rows(wide)
+        state[s, 0, pl.ds(x + 1, xs), z] = before.astype(BF)
+        state[s, 1, pl.ds(x + 1, xs), z] = wide.astype(BF)
+        state[s, 2, pl.ds(x + 1, xs), z] = after.astype(BF)
+
+    for k in range(4):
+        z0 = OWN * ((quarter + 4 - k) % 4)
+        for z in range(OWN):
+            place(0, 0, 8, z0 + z, own[k][:, z].astype(F32))
+
+        def unpack(x, carry, k=k, z0=z0):
+            moved = dot(swap, cots[k][x].astype(F32).reshape(128, 128).astype(BF))
+            for z in range(OWN):
+                low, high = (moved[16 * j : 16 * j + 16] for j in (4 + z, 4 + OWN + z))
+                place(1, x, 1, z0 + z, jnp.concatenate([low, high], axis=1)[None])
+            return carry
+
+        lax.fori_loop(0, 8, unpack, 0)
     for copy in copies:
         copy.wait()
     taps = [(x, y, z) for x in (-1, 0, 1) for y in (-1, 0, 1) for z in (-1, 0, 1)]
@@ -320,33 +335,37 @@
     force = (-COARSE_STEP * adjoint(0)).reshape(8, 4, 16, 256)
     pull = (-COARSE_STEP * adjoint(1)).reshape(8, 4, 16, 256)
     near = jnp.where(quarter == 1, 1.0, 0.0).astype(F32)
+    back = swap_table(8, 16)
     far = jnp.where(quarter == 2, 1.0, 0.0).astype(F32)
     for x in range(8):
         ground = base[x]
         rows = jnp.concatenate([force[x, 0:2] + near * ground, force[x, 2:4] + far * ground, pull[x]], axis=0)
-        out[x] = dot(swap[...], rows.reshape(128, 256).astype(BF)).astype(BF).reshape(16, 8, 256)
+        out[x] = dot(back, rows.reshape(128, 256).astype(BF)).astype(BF).reshape(16, 8, 256)
 
 
 def local(fine_prev, fine_now, fine_kernels, coarse_kernel, cotangent):
-    b, q, g = (lax.axis_index(name) for name in AXES)
-    first, middle, final = send_tables()
     packed = pl.pallas_call(
         pack_kernel,
         out_shape=jax.ShapeDtypeStruct((128, CHUNK, 128), BF),
-        in_specs=vmem(7),
+        in_specs=vmem(3),
         out_specs=pl.BlockSpec(memory_space=pltpu.VMEM),
-        compiler_params=pltpu.CompilerParams(vmem_limit_bytes=48 << 20),
+        scratch_shapes=[
+            pltpu.VMEM((2048, 256), BF),
+            pltpu.VMEM((1024, 512), F32),
+            pltpu.VMEM((2048, 256), BF),
+        ],
+        compiler_params=pltpu.CompilerParams(vmem_limit_bytes=32 << 20),
         name="pack",
-    )(
-        fine_now.reshape(128, 256),
-        fine_prev.reshape(128, 256),
-        cotangent.reshape(256, 128),
-        lane_table(),
-        first,
-        middle,
-        final,
-    )
+    )(fine_now, fine_prev, cotangent.reshape(256, 128))
     chunk = lax.all_to_all(packed, AXES, 0, 0).reshape(8, 16, CHUNK, 128)
+    drift = pl.pallas_call(
+        drift_kernel,
+        out_shape=jax.ShapeDtypeStruct((256, 128), F32),
+        in_specs=vmem(2),
+        out_specs=pl.BlockSpec(memory_space=pltpu.VMEM),
+        cost_estimate=pl.CostEstimate(flops=10**9, bytes_accessed=10**6, transcendentals=0),
+        name="drift",
+    )(fine_now, fine_prev)
 
     tile = np.tile(np.eye(32, dtype=np.float32), (1, 4)).astype(BF)
     weights = pl.pallas_call(
@@ -369,30 +388,36 @@
         tile,
     )
 
-    start = 4 * (4 * b + g) - 6 + 2 * q
+    kernel_part, weights = lax.optimization_barrier((coarse_kernel, weights))
+    across = lax.ppermute(kernel_part, "g", [(i, i ^ 2) for i in range(4)])
+    there = lax.ppermute(kernel_part, "g", [(i, i ^ 1) for i in range(4)])
+
+    def round_ring(v):
+        return [v] + [lax.ppermute(v, "q", [(i, (i + k) % 4) for i in range(4)]) for k in range(1, 4)]
+
+    cots = round_ring(lax.slice_in_dim(chunk, 16, 24, axis=2))
     buffer = pltpu.VMEM((10, NOW + 2, 16, 256), BF)
     mid, base = pl.pallas_call(
         fine_kernel,
         out_shape=(
-            jax.ShapeDtypeStruct((2, 8, OWN, 16, 256), BF),
+            jax.ShapeDtypeStruct((8, OWN, 16, 256), BF),
             jax.ShapeDtypeStruct((8, OWN, 16, 256), F32),
         ),
-        in_specs=[pl.BlockSpec(memory_space=pltpu.SMEM)] + vmem(4),
+        in_specs=vmem(2),
         out_specs=tuple(vmem(2)),
-        scratch_shapes=[pltpu.VMEM((8, NOW, 16, 256), F32)] * 2 + [buffer] * 4,
-        compiler_params=pltpu.CompilerParams(vmem_limit_bytes=56 << 20),
-        cost_estimate=pl.CostEstimate(flops=10**10, bytes_accessed=10**7, transcendentals=10**6),
+        scratch_shapes=[pltpu.VMEM((8, NOW, 16, 256), F32)] * 2
+        + [pltpu.VMEM((8, OWN, 16, 256), F32)]
+        + [buffer] * 4,
+        compiler_params=pltpu.CompilerParams(vmem_limit_bytes=48 << 20),
+        cost_estimate=pl.CostEstimate(flops=2 * 10**10, bytes_accessed=10**7, transcendentals=10**6),
         name="fine_layers",
-    )(jnp.stack([start, q]).astype(jnp.int32), chunk, weights, swap_table(16, 8), haar_table())
-
-    across = lax.ppermute(coarse_kernel, "g", [(i, i ^ 2) for i in range(4)])
-    there = lax.ppermute(coarse_kernel, "g", [(i, i ^ 1) for i in range(4)])
+    )(chunk, weights)
+    mid, across, *cots = lax.optimization_barrier((mid, across, *cots))
     opposite = lax.ppermute(across, "g", [(i, i ^ 1) for i in range(4)])
-    states = lax.all_gather(mid, "q")
     partial = pl.pallas_call(
         coarse_kernel_body,
         out_shape=jax.ShapeDtypeStruct((8, 16, 8, 256), BF),
-        in_specs=[pl.BlockSpec(memory_space=pltpu.SMEM)] + vmem(2) + [pl.BlockSpec(memory_space=pl.ANY)] * 4 + vmem(1),
+        in_specs=vmem(9) + [pl.BlockSpec(memory_space=pl.ANY)] * 4,
         out_specs=pl.BlockSpec(memory_space=pltpu.VMEM),
         scratch_shapes=[
             pltpu.VMEM((2, 3, 10, 8, 16, 256), BF),
@@ -400,24 +425,15 @@
             pltpu.VMEM((27, 256, 256), BF),
             pltpu.SemaphoreType.DMA((4,)),
         ],
-        compiler_params=pltpu.CompilerParams(vmem_limit_bytes=56 << 20),
+        compiler_params=pltpu.CompilerParams(vmem_limit_bytes=48 << 20),
         cost_estimate=pl.CostEstimate(flops=2 * 10**10, bytes_accessed=10**7, transcendentals=10**6),
         name="coarse_layer",
-    )(
-        jnp.stack([4 * (4 * b + g) - 1, q]).astype(jnp.int32),
-        states,
-        base,
-        coarse_kernel,
-        across,
-        there,
-        opposite,
-        swap_table(8, 16),
-    )
+    )(*round_ring(mid), *cots, base, coarse_kernel, across, there, opposite)
     parts = lax.all_to_all(partial.reshape(128, 8, 256), AXES, 0, 0)
     sums = lax.dot_general(
         parts.reshape(1024, 256), receive_table(), (((0,), (0,)), ((), ())), preferred_element_type=F32
     )
-    coarse_next = sums[:, 0:128].reshape(256, 1, 1, 128)
+    coarse_next = (drift + sums[:, 0:128]).reshape(256, 1, 1, 128)
     state_adjoint = 2.0 * cotangent.astype(F32) + sums[:, 128:256].reshape(256, 1, 1, 128)
     return coarse_next, state_adjoint
 

time: 135 us -> 108 us (0.80)
  blocking collectives: 22.1 us -> 0 us
  starting transfers between devices: 12.9 us -> 27.5 us
  between operations: 14.1 us -> 0.8 us
  local copies, waits for them, and re-layouts: 12.9 us -> 6.63 us
  Pallas kernels: 35.7 us -> 39.4 us
  waiting for transfers between devices: 33.4 us -> 30.7 us
    all_to_all x1 -> x0, blocking collectives: 22.1 us -> none  [local(): parts = lax.all_to_all(partial.reshape(128, 8, 256), AXES, 0, 0)]
    all_gather x1 -> x0, waiting for transfers between devices: 16.8 us -> none  [local(): states = lax.all_gather(mid, 'q')]
    all_to_all x0 -> x1, waiting for transfers between devices: none -> 10.5 us  [local(): parts = lax.all_to_all(partial.reshape(128, 8, 256), AXES, 0, 0)]
    ppermute x2 -> x8, starting transfers between devices: 1.25 us -> 10 us  [the longest x6 8.92 us: round_ring(): lax.ppermute(v, 'q', [(i, (i + k) % 4) for i in range(4)])]
    all_to_all x0 -> x1, starting transfers between devices: none -> 6.31 us  [local(): parts = lax.all_to_all(partial.reshape(128, 8, 256), AXES, 0, 0)]
    ppermute x2 -> x8, waiting for transfers between devices: 1.47 us -> 5.66 us  [the longest x6 5.66 us: round_ring(): lax.ppermute(v, 'q', [(i, (i + k) % 4) for i in range(4)])]
    unnamed x26 -> x18, local copies, waits for them, and re-layouts: 9.67 us -> 6.01 us
    pallas_call x1, Pallas kernels: 13.8 us -> 15.8 us  [local(): pl.pallas_call(coarse_kernel_body, out_shape=jax.ShapeDtypeStruct((8, 16,...]
  transfers between devices with their start and end apart: 5 -> 11, of which waited for: 4 -> 4; matrix products, arithmetic and copies ran while one was open for 1% -> 1% of each run, Pallas kernels for 15% -> 20%
where the time goes in v2:
time: 108 us; the launch traced here: 107 us
  Pallas kernels  39.4 us (36%)
  waiting for transfers between devices  30.7 us (28%)
  starting transfers between devices  27.5 us (25%)
  local copies, waits for them, and re-layouts  6.63 us (6%)
  other arithmetic  1.35 us (1%)
    pallas_call x1, Pallas kernels, local(): pl.pallas_call(fine_kernel, out_shape=(jax.ShapeDtypeStruct((8, OWN, 16,...  17 us
    pallas_call x1, Pallas kernels, local(): pl.pallas_call(coarse_kernel_body, out_shape=jax.ShapeDtypeStruct((8, 16,...  15.8 us
    all_to_all x1, waiting for transfers between devices, local(): chunk = lax.all_to_all(packed, AXES, 0, 0).reshape(8, 16, CHUNK, 128)  14.5 us
    all_to_all x1, starting transfers between devices, local(): chunk = lax.all_to_all(packed, AXES, 0, 0).reshape(8, 16, CHUNK, 128)  11.1 us
    all_to_all x1, waiting for transfers between devices, local(): parts = lax.all_to_all(partial.reshape(128, 8, 256), AXES, 0, 0)  10.5 us
    ppermute x6, starting transfers between devices, round_ring(): lax.ppermute(v, 'q', [(i, (i + k) % 4) for i in range(4)])  8.92 us
    all_to_all x1, starting transfers between devices, local(): parts = lax.all_to_all(partial.reshape(128, 8, 256), AXES, 0, 0)  6.31 us
    unnamed x18, local copies, waits for them, and re-layouts  6.01 us
  transfers between devices with their start and end apart: 11, of which 4 were waited for; matrix products, arithmetic and copies ran while one was open for 1% of the time, Pallas kernels for 20%

profile of v2, /device:TPU:0, one launch (start us, length us, event | category | flops | bytes accessed | tf_op | source)
XLA Modules:
  0.0 106.8 jit_solution(8928526653711752028)
XLA Ops:
  0.6 0.8 copy-done.1
  1.5 0.9 copy-done.3
  2.4 0.9 copy-done.4
  3.3 2.2 %pack.1 = bf16[128,40,128]{2,1,0:T(8,128)(2,1)} custom-call(f32[32,2,2,256]{3,2,1,0:T(2,128)S(1)} %copy-done.3, f32[32,2,2,256]{3,2,1,0:T(2,128)S(1)} %copy-done.4, bf16[256,128]{1,0:T(8,128)(2,1)S(1)} %bitcast.23), custom_call_target="tpu_custom_call" | custom-call | tf_op jit(solution)/shard_map/pack/pallas_call | solution.py:347
  5.4 11.1 %all-to-all-start = ((bf16[128,40,128]{2,1,0:T(8,128)(2,1)}), bf16[128,40,128]{2,1,0:T(8,128)(2,1)S(1)}, u32[]{:S(2)}, u32[]{:S(2)}) async-start(bf16[128,40,128]{2,1,0:T(8,128)(2,1)} %pack.1), calls=%async_computation | async-start | bytes 2621440 | tf_op jit(solution)/shard_map/all_to_all | solution.py:360
  16.6 0.6 copy.9
  17.3 1.9 %spread_weights.1.weights = bf16[4,2,8,256,256]{4,3,2,1,0:T(8,128)(2,1)S(1)} custom-call(bf16[4,864,32]{2,1,0:T(8,128)(2,1)S(1)} %bitcast.22, bf16[4,864,32]{2,1,0:T(8,128)(2,1)S(1)} %bitcast.21, bf16[32,128]{1,0:T(8,128)(2,1)S(1)} %copy-done.5), custom_call_target="tpu_custom_call" | custom-call | flops 10000000000 | bytes 10000000 | tf_op jit(solution)/shard_map/spread_weights/pallas_call | solution.py:371
  19.2 3.2 %copy-done.6 = bf16[4,2,8,256,256]{4,3,2,1,0:T(8,128)(2,1)} copy-done((bf16[4,2,8,256,256]{4,3,2,1,0:T(8,128)(2,1)}, bf16[4,2,8,256,256]{4,3,2,1,0:T(8,128)(2,1)S(1)}, u32[]{:S(2)}) %copy-start.6) | copy-done | bytes 8388632
  22.5 1.1 %collective-permute-start = (bf16[27,64,256]{2,1,0:T(8,128)(2,1)}, bf16[27,64,256]{2,1,0:T(8,128)(2,1)S(1)}, u32[]{:S(2)}, u32[]{:S(2)}) collective-permute-start(bf16[27,64,256]{2,1,0:T(8,128)(2,1)} %refs_9_.1), channel_id=1, source_target_pairs={{0,2},{1,3},{2,0},{3,1},{4,6},{5,7},{6,4},{7,5},{8,10},{9,11},{10,... | collective-permute-start | bytes 2654216 | tf_op jit(solution)/shard_map/ppermute | solution.py:392
  23.5 14.5 %all-to-all-done = bf16[128,40,128]{2,1,0:T(8,128)(2,1)S(1)} async-done(((bf16[128,40,128]{2,1,0:T(8,128)(2,1)}), bf16[128,40,128]{2,1,0:T(8,128)(2,1)S(1)}, u32[]{:S(2)}, u32[]{:S(2)}) %all-to-all-start) | async-done | bytes 1310752 | tf_op jit(solution)/shard_map/all_to_all | solution.py:360
  38.2 1.8 %collective-permute-start.2 = (bf16[8,16,8,128]{3,2,1,0:T(8,128)(2,1)S(1)}, bf16[8,16,8,128]{3,2,1,0:T(8,128)(2,1)S(1)}, u32[]{:S(2)}, u32[]{:S(2)}) collective-permute-start(bf16[8,16,8,128]{3,2,1,0:T(8,128)(2,1)S(1)} %slice.12.refs_4_), channel_id=1, source_target_pairs={{0,8},{4,12},{8,0},{12,4},{1,9},{5,13},{9,1},{13,5},{2,10},{6,14},... | collective-permute-start | bytes 786440 | tf_op jit(solution)/shard_map/ppermute | solution.py:396
  40.0 2.2 %collective-permute-start.3 = (bf16[8,16,8,128]{3,2,1,0:T(8,128)(2,1)S(1)}, bf16[8,16,8,128]{3,2,1,0:T(8,128)(2,1)S(1)}, u32[]{:S(2)}, u32[]{:S(2)}) collective-permute-start(bf16[8,16,8,128]{3,2,1,0:T(8,128)(2,1)S(1)} %slice.12.refs_4_), channel_id=1, source_target_pairs={{0,12},{4,0},{8,4},{12,8},{1,13},{5,1},{9,5},{13,9},{2,14},{6,2},{... | collective-permute-start | bytes 786440 | tf_op jit(solution)/shard_map/ppermute | solution.py:396
  42.2 17.0 %fine_layers.1 = (bf16[8,2,16,256]{3,2,1,0:T(8,128)(2,1)S(1)}, f32[8,2,16,256]{3,2,1,0:T(8,128)S(1)}) custom-call(bf16[8,16,40,128]{3,2,1,0:T(8,128)(2,1)S(1)} %bitcast.19, bf16[4,2,8,256,256]{4,3,2,1,0:T(8,128)(2,1)} %copy-done.6), custom_call_target="tpu_custom_call" | custom-call | flops 20000000000 | bytes 10000000 | tf_op jit(solution)/shard_map/fine_layers/pallas_call | solution.py:400
  59.5 2.2 %collective-permute-start.5 = (bf16[8,2,16,256]{3,2,1,0:T(8,128)(2,1)S(1)}, bf16[8,2,16,256]{3,2,1,0:T(8,128)(2,1)S(1)}, u32[]{:S(2)}, u32[]{:S(2)}) collective-permute-start(bf16[8,2,16,256]{3,2,1,0:T(8,128)(2,1)S(1)} %get-tuple-element.15.refs_0_), channel_id=1, source_target_pairs={{0,8},{4,12},{8,0},{12,4},{1,9},{5,13},{9,1},{13,5},{2,10},{6,14},... | collective-permute-start | bytes 393224 | tf_op jit(solution)/shard_map/ppermute | solution.py:396
  61.7 2.5 %collective-permute-start.6 = (bf16[8,2,16,256]{3,2,1,0:T(8,128)(2,1)S(1)}, bf16[8,2,16,256]{3,2,1,0:T(8,128)(2,1)S(1)}, u32[]{:S(2)}, u32[]{:S(2)}) collective-permute-start(bf16[8,2,16,256]{3,2,1,0:T(8,128)(2,1)S(1)} %get-tuple-element.15.refs_0_), channel_id=1, source_target_pairs={{0,12},{4,0},{8,4},{12,8},{1,13},{5,1},{9,5},{13,9},{2,14},{6,2},{... | collective-permute-start | bytes 393224 | tf_op jit(solution)/shard_map/ppermute | solution.py:396
  64.2 5.1 %collective-permute-done.4.refs_1_ = bf16[8,2,16,256]{3,2,1,0:T(8,128)(2,1)S(1)} collective-permute-done((bf16[8,2,16,256]{3,2,1,0:T(8,128)(2,1)S(1)}, bf16[8,2,16,256]{3,2,1,0:T(8,128)(2,1)S(1)}, u32[]{:S(2)}, u32[]{:S(2)}) %collective-permute-start.4) | collective-permute-done | bytes 131104 | tf_op jit(solution)/shard_map/ppermute | solution.py:396
  69.3 0.6 collective-permute-done.6.refs_3_
  69.9 15.8 %coarse_layer.1 = bf16[8,16,8,256]{3,2,1,0:T(8,128)(2,1)} custom-call(bf16[8,2,16,256]{3,2,1,0:T(8,128)(2,1)S(1)} %get-tuple-element.15.refs_0_, bf16[8,2,16,256]{3,2,1,0:T(8,128)(2,1)S(1)} %collective-permute-done.4.refs_1_, bf16[8,2,16,256]{3,2,1,0:T(8,128)(2,1)S(1)} %collective-permute-done.5.refs_2_, ...), custom_call_target="tpu_custom_call" | custom-call | flops 20000000000 | bytes 10000000 | tf_op jit(solution)/shard_map/coarse_layer/pallas_call | solution.py:417
  85.7 6.3 %all-to-all-start.1 = ((bf16[128,8,256]{2,1,0:T(8,128)(2,1)}), bf16[128,8,256]{2,1,0:T(8,128)(2,1)S(1)}, u32[]{:S(2)}, u32[]{:S(2)}) async-start(bf16[128,8,256]{2,1,0:T(8,128)(2,1)} %bitcast.5), calls=%async_computation.1 | async-start | bytes 1048576 | tf_op jit(solution)/shard_map/all_to_all | solution.py:432
  92.1 2.5 %drift.1 = f32[256,128]{1,0:T(8,128)} custom-call(f32[32,2,2,256]{3,2,1,0:T(2,128)} %now.3, f32[32,2,2,256]{3,2,1,0:T(2,128)} %prev.3), custom_call_target="tpu_custom_call" | custom-call | flops 1000000000 | bytes 1000000 | tf_op jit(solution)/shard_map/drift/pallas_call | solution.py:361
  94.5 10.5 %all-to-all-done.1 = bf16[128,8,256]{2,1,0:T(8,128)(2,1)S(1)} async-done(((bf16[128,8,256]{2,1,0:T(8,128)(2,1)}), bf16[128,8,256]{2,1,0:T(8,128)(2,1)S(1)}, u32[]{:S(2)}, u32[]{:S(2)}) %all-to-all-start.1) | async-done | bytes 524320 | tf_op jit(solution)/shard_map/all_to_all | solution.py:432
  105.1 0.3 fusion
  105.4 0.7 fusion.2
  106.1 0.7 slice_add_fusion
  (26 shorter events, 0.5 us)
Async XLA Ops:
  0.6 0.8 copy-start.1
  1.5 0.9 copy-start.3
  2.4 0.9 copy-start.4
  5.4 11.2 %copy-start = (bf16[4,27,32,32]{3,2,1,0:T(8,128)(2,1)S(1)}, bf16[4,27,32,32]{3,2,1,0:T(8,128)(2,1)}, u32[]{:S(2)}) copy-start(bf16[4,27,32,32]{3,2,1,0:T(8,128)(2,1)} %param.9) | copy-start | bytes 663556
  5.4 32.6 %all-to-all-start = ((bf16[128,40,128]{2,1,0:T(8,128)(2,1)}), bf16[128,40,128]{2,1,0:T(8,128)(2,1)S(1)}, u32[]{:S(2)}, u32[]{:S(2)}) async-start(bf16[128,40,128]{2,1,0:T(8,128)(2,1)} %pack.1), calls=%async_computation | async-start | bytes 2621440 | tf_op jit(solution)/shard_map/all_to_all | solution.py:360
  16.6 0.7 copy-start.5
  19.2 3.3 %copy-start.6 = (bf16[4,2,8,256,256]{4,3,2,1,0:T(8,128)(2,1)}, bf16[4,2,8,256,256]{4,3,2,1,0:T(8,128)(2,1)S(1)}, u32[]{:S(2)}) copy-start(bf16[4,2,8,256,256]{4,3,2,1,0:T(8,128)(2,1)S(1)} %spread_weights.1.weights) | copy-start | bytes 25165828
  22.5 36.8 %collective-permute-start = (bf16[27,64,256]{2,1,0:T(8,128)(2,1)}, bf16[27,64,256]{2,1,0:T(8,128)(2,1)S(1)}, u32[]{:S(2)}, u32[]{:S(2)}) collective-permute-start(bf16[27,64,256]{2,1,0:T(8,128)(2,1)} %refs_9_.1), channel_id=1, source_target_pairs={{0,2},{1,3},{2,0},{3,1},{4,6},{5,7},{6,4},{7,5},{8,10},{9,11},{10,... | collective-permute-start | bytes 2654216 | tf_op jit(solution)/shard_map/ppermute | solution.py:392
  23.5 40.7 %collective-permute-start.7 = (bf16[27,64,256]{2,1,0:T(8,128)(2,1)}, bf16[27,64,256]{2,1,0:T(8,128)(2,1)S(1)}, u32[]{:S(2)}, u32[]{:S(2)}) collective-permute-start(bf16[27,64,256]{2,1,0:T(8,128)(2,1)} %refs_9_.1), channel_id=1, source_target_pairs={{0,1},{1,0},{2,3},{3,2},{4,5},{5,4},{6,7},{7,6},{8,9},{9,8},{10,11... | collective-permute-start | bytes 2654216 | tf_op jit(solution)/shard_map/ppermute | solution.py:393
  38.1 21.1 %collective-permute-start.1 = (bf16[8,16,8,128]{3,2,1,0:T(8,128)(2,1)S(1)}, bf16[8,16,8,128]{3,2,1,0:T(8,128)(2,1)S(1)}, u32[]{:S(2)}, u32[]{:S(2)}) collective-permute-start(bf16[8,16,8,128]{3,2,1,0:T(8,128)(2,1)S(1)} %slice.12.refs_4_), channel_id=1, source_target_pairs={{0,4},{4,8},{8,12},{12,0},{1,5},{5,9},{9,13},{13,1},{2,6},{6,10},{... | collective-permute-start | bytes 786440 | tf_op jit(solution)/shard_map/ppermute | solution.py:396
  38.2 21.0 %collective-permute-start.2 = (bf16[8,16,8,128]{3,2,1,0:T(8,128)(2,1)S(1)}, bf16[8,16,8,128]{3,2,1,0:T(8,128)(2,1)S(1)}, u32[]{:S(2)}, u32[]{:S(2)}) collective-permute-start(bf16[8,16,8,128]{3,2,1,0:T(8,128)(2,1)S(1)} %slice.12.refs_4_), channel_id=1, source_target_pairs={{0,8},{4,12},{8,0},{12,4},{1,9},{5,13},{9,1},{13,5},{2,10},{6,14},... | collective-permute-start | bytes 786440 | tf_op jit(solution)/shard_map/ppermute | solution.py:396
  40.0 19.3 %collective-permute-start.3 = (bf16[8,16,8,128]{3,2,1,0:T(8,128)(2,1)S(1)}, bf16[8,16,8,128]{3,2,1,0:T(8,128)(2,1)S(1)}, u32[]{:S(2)}, u32[]{:S(2)}) collective-permute-start(bf16[8,16,8,128]{3,2,1,0:T(8,128)(2,1)S(1)} %slice.12.refs_4_), channel_id=1, source_target_pairs={{0,12},{4,0},{8,4},{12,8},{1,13},{5,1},{9,5},{13,9},{2,14},{6,2},{... | collective-permute-start | bytes 786440 | tf_op jit(solution)/shard_map/ppermute | solution.py:396
  59.3 10.6 %collective-permute-start.8 = (bf16[27,64,256]{2,1,0:T(8,128)(2,1)S(1)}, bf16[27,64,256]{2,1,0:T(8,128)(2,1)S(1)}, u32[]{:S(2)}, u32[]{:S(2)}) collective-permute-start(bf16[27,64,256]{2,1,0:T(8,128)(2,1)S(1)} %collective-permute-done.refs_10_), channel_id=1, source_target_pairs={{0,1},{1,0},{2,3},{3,2},{4,5},{5,4},{6,7},{7,6},{8,9},{9,8},{10,11... | collective-permute-start | bytes 2654216 | tf_op jit(solution)/shard_map/ppermute | solution.py:416
  59.4 9.9 %collective-permute-start.4 = (bf16[8,2,16,256]{3,2,1,0:T(8,128)(2,1)S(1)}, bf16[8,2,16,256]{3,2,1,0:T(8,128)(2,1)S(1)}, u32[]{:S(2)}, u32[]{:S(2)}) collective-permute-start(bf16[8,2,16,256]{3,2,1,0:T(8,128)(2,1)S(1)} %get-tuple-element.15.refs_0_), channel_id=1, source_target_pairs={{0,4},{4,8},{8,12},{12,0},{1,5},{5,9},{9,13},{13,1},{2,6},{6,10},{... | collective-permute-start | bytes 393224 | tf_op jit(solution)/shard_map/ppermute | solution.py:396
  59.5 9.8 %collective-permute-start.5 = (bf16[8,2,16,256]{3,2,1,0:T(8,128)(2,1)S(1)}, bf16[8,2,16,256]{3,2,1,0:T(8,128)(2,1)S(1)}, u32[]{:S(2)}, u32[]{:S(2)}) collective-permute-start(bf16[8,2,16,256]{3,2,1,0:T(8,128)(2,1)S(1)} %get-tuple-element.15.refs_0_), channel_id=1, source_target_pairs={{0,8},{4,12},{8,0},{12,4},{1,9},{5,13},{9,1},{13,5},{2,10},{6,14},... | collective-permute-start | bytes 393224 | tf_op jit(solution)/shard_map/ppermute | solution.py:396
  61.7 8.2 %collective-permute-start.6 = (bf16[8,2,16,256]{3,2,1,0:T(8,128)(2,1)S(1)}, bf16[8,2,16,256]{3,2,1,0:T(8,128)(2,1)S(1)}, u32[]{:S(2)}, u32[]{:S(2)}) collective-permute-start(bf16[8,2,16,256]{3,2,1,0:T(8,128)(2,1)S(1)} %get-tuple-element.15.refs_0_), channel_id=1, source_target_pairs={{0,12},{4,0},{8,4},{12,8},{1,13},{5,1},{9,5},{13,9},{2,14},{6,2},{... | collective-permute-start | bytes 393224 | tf_op jit(solution)/shard_map/ppermute | solution.py:396
  85.7 19.3 %all-to-all-start.1 = ((bf16[128,8,256]{2,1,0:T(8,128)(2,1)}), bf16[128,8,256]{2,1,0:T(8,128)(2,1)S(1)}, u32[]{:S(2)}, u32[]{:S(2)}) async-start(bf16[128,8,256]{2,1,0:T(8,128)(2,1)} %bitcast.5), calls=%async_computation.1 | async-start | bytes 1048576 | tf_op jit(solution)/shard_map/all_to_all | solution.py:432
  92.0 13.0 %copy-start.7 = (bf16[1024,256]{1,0:T(8,128)(2,1)S(1)}, bf16[1024,256]{1,0:T(8,128)(2,1)}, u32[]{:S(2)}) copy-start(bf16[1024,256]{1,0:T(8,128)(2,1)} %constant.7.clone) | copy-start | bytes 1572868
  94.5 10.9 %copy-start.2 = (bf16[256,1,1,128]{3,0,2,1:T(8,128)(2,1)S(1)}, bf16[256,1,1,128]{3,0,2,1:T(8,128)(2,1)}, u32[]{:S(2)}) copy-start(bf16[256,1,1,128]{3,0,2,1:T(8,128)(2,1)} %param.11) | copy-start | bytes 196612
  94.5 11.6 %copy-start.8 = (f32[256,128]{1,0:T(8,128)S(1)}, f32[256,128]{1,0:T(8,128)}, u32[]{:S(2)}) copy-start(f32[256,128]{1,0:T(8,128)} %drift.1) | copy-start | bytes 393220

commit v3 on v2

--- a/solution.py
+++ b/solution.py
@@ -70,9 +70,8 @@
 
 
 def pack_kernel(now, prev, cot, out, first, middle, final):
-    now_rows = parity_rows(now)
-    speed = (now_rows - parity_rows(prev)).astype(BF)
-    now_rows = now_rows.astype(BF)
+    now_rows = parity_rows(now).astype(BF)
+    prev_rows = parity_rows(prev).astype(BF)
     both = jnp.concatenate([now_rows, cot[0:128, :], cot[128:256, :]], axis=1)
     k, lane = iota((16, 256), 0), iota((16, 256), 1)
     for_first = lane - 2 * (k % NOW) - k // NOW
@@ -90,29 +89,14 @@
     for t in range(0, 128, part):
         one = dot_nt(first[pl.ds(16 * t, 16 * part), :], now_rows).reshape(part, 16, 128)
         two = dot_nt(middle[pl.ds(8 * t, 8 * part), :].astype(BF), both).reshape(part, 8, 128)
-        three = dot_nt(final[pl.ds(16 * t, 16 * part), :], speed).reshape(part, 16, 128)
+        three = dot_nt(final[pl.ds(16 * t, 16 * part), :], prev_rows).reshape(part, 16, 128)
         out[pl.ds(t, part)] = jnp.concatenate([one, two, three], axis=1).astype(BF)
 
 
-def split_dot(x, y, exact_left):
-    wide = y if exact_left else x
-    top = wide.astype(BF)
-    rest = wide - top.astype(F32)
-    low = rest.astype(BF)
-    last = (rest - low.astype(F32)).astype(BF)
-    if exact_left:
-        return dot(x, top) + dot(x, low) + dot(x, last)
-    return dot(top, y) + dot(low, y) + dot(last, y)
-
-
-def drift_kernel(now, prev, out):
-    rows = 6.0 * parity_rows(now) - 5.0 * parity_rows(prev)
-    total = jnp.zeros((256, 128), F32)
-    for d in range(2):
-        pick = ones_where(iota((256, 128), 0) == 2 * iota((256, 128), 1) + d).astype(BF)
-        signs = haar_signs(iota((256, 128), 1) + 128 * d, iota((256, 128), 0))
-        total = total + split_dot(signs, split_dot(rows, pick, False), True)
-    out[...] = total * (1.0 / math.sqrt(8.0))
+def split_dot(x, y):
+    top = x.astype(BF)
+    low = (x - top.astype(F32)).astype(BF)
+    return dot(top, y) + dot(low, y)
 
 
 def tap_index(dx, dy, dz, a2, b2, d2, a, b, d):
@@ -184,7 +168,12 @@
     return total
 
 
-def fine_kernel(chunk, weights, mid, base, cur, old, line, s0, s1, h0, h1):
+def fine_kernel(chunk, spread, mid, base, cur, old, s0, s1, h0, h1, weights, sems):
+    copies = []
+    for layer in range(LAYERS):
+        copy = pltpu.make_async_copy(spread.at[layer], weights.at[layer], sems.at[layer])
+        copy.start()
+        copies.append(copy)
     start = window_start(*(lax.axis_index(name) for name in AXES))
     swap = swap_table(16, 8)
     for ref in (s0, s1, h0, h1):
@@ -212,17 +201,16 @@
         at = 2 * (NOW + OWN)
         for z in range(PREV):
             v = jnp.concatenate([parts[at + z], parts[at + PREV + z]], axis=1)
-            old[x, z + 1] = cur[x, z + 1] - v
-            if z in (3, 4):
-                line[x, z - 3] = cur[x, z + 1] + 5.0 * v
+            old[x, z + 1] = v
         return carry
 
     lax.fori_loop(0, 8, unpack, 0)
 
     now, before = cur, old
     for layer in range(LAYERS):
+        copies[layer].wait()
         zs = NOW - 2 * layer
-        xs = 4 if zs > 6 else 8
+        xs = max(1, 128 // (16 * zs)) if zs > 6 else 8 // zs + (zs == 6)
 
         def squash(i, carry, layer=layer, zs=zs, xs=xs):
             x0 = i * xs
@@ -234,9 +222,9 @@
                 h1[pl.ds(x0 + 1, xs), layer + z + 1] = moved_rows(part).astype(BF)
             return carry
 
-        lax.fori_loop(0, 8 // xs, squash, 0)
+        lax.fori_loop(0, 8 // xs, squash, 0, unroll=True)
         zs = NOW - 2 * layer - 2
-        xs = 4 if zs > 6 else 8
+        xs = max(1, 128 // (16 * zs)) if zs > 6 else 8 // zs + (zs == 6)
         last = layer == LAYERS - 1
 
         def update(i, carry, layer=layer, zs=zs, xs=xs, now=now, before=before, last=last):
@@ -253,7 +241,7 @@
                     s1[pl.ds(x0 + 1, xs), at + 1] = moved_rows(part).astype(BF)
             return carry
 
-        lax.fori_loop(0, 8 // xs, update, 0)
+        lax.fori_loop(0, 8 // xs, update, 0, unroll=True)
         now, before = before, now
 
     haar = haar_signs(iota((256, 256), 0), iota((256, 256), 1))
@@ -261,9 +249,8 @@
     own = (slice(None), slice(4, 6))
     latest = now[own].reshape(256, 256)
     earlier = before[own].reshape(256, 256)
-    forced = 2.0 * latest - earlier - line[...].reshape(256, 256)
-    mid[...] = (split_dot(latest, haar, False) * scale).astype(BF).reshape(8, OWN, 16, 256)
-    base[...] = (split_dot(forced, haar, False) * scale).reshape(8, OWN, 16, 256)
+    mid[...] = (split_dot(latest, haar) * scale).astype(BF).reshape(8, OWN, 16, 256)
+    base[...] = (split_dot(2.0 * latest - earlier, haar) * scale).reshape(8, OWN, 16, 256)
 
 
 def coarse_kernel_body(*refs):
@@ -300,46 +287,53 @@
                 place(1, x, 1, z0 + z, jnp.concatenate([low, high], axis=1)[None])
             return carry
 
-        lax.fori_loop(0, 8, unpack, 0)
+        lax.fori_loop(0, 8, unpack, 0, unroll=True)
     for copy in copies:
         copy.wait()
     taps = [(x, y, z) for x in (-1, 0, 1) for y in (-1, 0, 1) for z in (-1, 0, 1)]
 
-    def forward(s):
-        total = jnp.zeros((768, 256), F32)
+    def forward(s, x0, xs):
+        rows = xs * 96
+        total = jnp.zeros((rows, 256), F32)
         for number, (ex, ey, ez) in enumerate(taps):
-            left = state[s, 1 + ey, pl.ds(1 + ex, 8), pl.ds(1 + ez, 6)].reshape(768, 256)
+            left = state[s, 1 + ey, pl.ds(x0 + 1 + ex, xs), pl.ds(1 + ez, 6)].reshape(rows, 256)
             total = total + dot_nt(left, weights[number])
         return total
 
-    def adjoint(s):
-        total = jnp.zeros((512, 256), F32)
+    def adjoint(s, x0, xs):
+        rows = xs * 64
+        total = jnp.zeros((rows, 256), F32)
         for number, (ex, ey, ez) in enumerate(taps):
-            left = hidden[s, 1 - ey, pl.ds(1 - ex, 8), pl.ds(1 - ez, 4)].reshape(512, 256)
+            left = hidden[s, 1 - ey, pl.ds(x0 + 1 - ex, xs), pl.ds(1 - ez, 4)].reshape(rows, 256)
             total = total + dot(left, weights[number])
-        return total
-
-    def store(s, v):
-        v = v.reshape(8, 6, 16, 256)
+        return (-COARSE_STEP * total).reshape(xs, 4, 16, 256)
+
+    def store(s, v, x0, xs):
+        v = v.reshape(xs, 6, 16, 256)
         for z in range(6):
             at = start + z
             part = v[:, z] * jnp.where((at >= 0) & (at < 128), 1.0, 0.0).astype(F32)
             before, after = side_rows(part)
-            hidden[s, 0, pl.ds(1, 8), z] = before.astype(BF)
-            hidden[s, 1, pl.ds(1, 8), z] = part.astype(BF)
-            hidden[s, 2, pl.ds(1, 8), z] = after.astype(BF)
-
-    squash = jnp.tanh(forward(0))
-    store(0, squash)
-    store(1, (1.0 - squash * squash) * forward(1))
-    force = (-COARSE_STEP * adjoint(0)).reshape(8, 4, 16, 256)
-    pull = (-COARSE_STEP * adjoint(1)).reshape(8, 4, 16, 256)
+            here = (pl.ds(x0 + 1, xs), z)
+            hidden[(s, 0) + here] = before.astype(BF)
+            hidden[(s, 1) + here] = part.astype(BF)
+            hidden[(s, 2) + here] = after.astype(BF)
+
+    xs = 4
+    for x0 in range(0, 8, xs):
+        squash = jnp.tanh(forward(0, x0, xs))
+        store(0, squash, x0, xs)
+        store(1, (1.0 - squash * squash) * forward(1, x0, xs), x0, xs)
     near = jnp.where(quarter == 1, 1.0, 0.0).astype(F32)
     back = swap_table(8, 16)
     far = jnp.where(quarter == 2, 1.0, 0.0).astype(F32)
+    xs = 4
     for x in range(8):
+        if x % xs == 0:
+            force, pull = adjoint(0, x, xs), adjoint(1, x, xs)
+        at = x % xs
         ground = base[x]
-        rows = jnp.concatenate([force[x, 0:2] + near * ground, force[x, 2:4] + far * ground, pull[x]], axis=0)
+        rows = jnp.concatenate([force[at, 0:2] + near * ground, force[at, 2:4] + far * ground, pull[at]], axis=0)
         out[x] = dot(back, rows.reshape(128, 256).astype(BF)).astype(BF).reshape(16, 8, 256)
 
 
@@ -358,15 +352,6 @@
         name="pack",
     )(fine_now, fine_prev, cotangent.reshape(256, 128))
     chunk = lax.all_to_all(packed, AXES, 0, 0).reshape(8, 16, CHUNK, 128)
-    drift = pl.pallas_call(
-        drift_kernel,
-        out_shape=jax.ShapeDtypeStruct((256, 128), F32),
-        in_specs=vmem(2),
-        out_specs=pl.BlockSpec(memory_space=pltpu.VMEM),
-        cost_estimate=pl.CostEstimate(flops=10**9, bytes_accessed=10**6, transcendentals=0),
-        name="drift",
-    )(fine_now, fine_prev)
-
     tile = np.tile(np.eye(32, dtype=np.float32), (1, 4)).astype(BF)
     weights = pl.pallas_call(
         weight_kernel,
@@ -403,11 +388,11 @@
             jax.ShapeDtypeStruct((8, OWN, 16, 256), BF),
             jax.ShapeDtypeStruct((8, OWN, 16, 256), F32),
         ),
-        in_specs=vmem(2),
+        in_specs=vmem(1) + [pl.BlockSpec(memory_space=pl.ANY)],
         out_specs=tuple(vmem(2)),
         scratch_shapes=[pltpu.VMEM((8, NOW, 16, 256), F32)] * 2
-        + [pltpu.VMEM((8, OWN, 16, 256), F32)]
-        + [buffer] * 4,
+        + [buffer] * 4
+        + [pltpu.VMEM((LAYERS, 2, 8, 256, 256), BF), pltpu.SemaphoreType.DMA((LAYERS,))],
         compiler_params=pltpu.CompilerParams(vmem_limit_bytes=48 << 20),
         cost_estimate=pl.CostEstimate(flops=2 * 10**10, bytes_accessed=10**7, transcendentals=10**6),
         name="fine_layers",
@@ -433,7 +418,7 @@
     sums = lax.dot_general(
         parts.reshape(1024, 256), receive_table(), (((0,), (0,)), ((), ())), preferred_element_type=F32
     )
-    coarse_next = (drift + sums[:, 0:128]).reshape(256, 1, 1, 128)
+    coarse_next = sums[:, 0:128].reshape(256, 1, 1, 128)
     state_adjoint = 2.0 * cotangent.astype(F32) + sums[:, 128:256].reshape(256, 1, 1, 128)
     return coarse_next, state_adjoint
 

time: 108 us -> 98.5 us (0.912)
  blocking collectives: 0 us -> 20.7 us
  Pallas kernels: 39.4 us -> 24.9 us
  waiting for transfers between devices: 30.7 us -> 21.4 us
  starting transfers between devices: 27.5 us -> 21.3 us
    all_to_all x0 -> x1, blocking collectives: none -> 20.7 us  [local(): parts = lax.all_to_all(partial.reshape(128, 8, 256), AXES, 0, 0)]
    all_to_all x1 -> x0, waiting for transfers between devices: 10.5 us -> none  [local(): parts = lax.all_to_all(partial.reshape(128, 8, 256), AXES, 0, 0)]
    pallas_call x1, Pallas kernels: 17 us -> 9.92 us  [local(): pl.pallas_call(fine_kernel, out_shape=(jax.ShapeDtypeStruct((8, OWN, 16,...]
    all_to_all x1 -> x0, starting transfers between devices: 6.31 us -> none  [local(): parts = lax.all_to_all(partial.reshape(128, 8, 256), AXES, 0, 0)]
    pallas_call x1, Pallas kernels: 15.8 us -> 10.9 us  [local(): pl.pallas_call(coarse_kernel_body, out_shape=jax.ShapeDtypeStruct((8, 16,...]
    pallas_call x1 -> x0, Pallas kernels: 2.48 us -> none  [local(): pl.pallas_call(drift_kernel, out_shape=jax.ShapeDtypeStruct((256, 128), F...]
    unnamed x18 -> x16, local copies, waits for them, and re-layouts: 6.01 us -> 5.99 us
  transfers between devices with their start and end apart: 11 -> 10, of which waited for: 4 -> 6; matrix products, arithmetic and copies ran while one was open for 1% -> 1% of each run, Pallas kernels for 20% -> 12%
where the time goes in v3:
time: 98.5 us; the launch traced here: 97.3 us
  Pallas kernels  24.9 us (25%)
  waiting for transfers between devices  21.4 us (22%)
  starting transfers between devices  21.3 us (22%)
  blocking collectives  20.7 us (21%)
  local copies, waits for them, and re-layouts  7.27 us (7%)
    all_to_all x1, blocking collectives, local(): parts = lax.all_to_all(partial.reshape(128, 8, 256), AXES, 0, 0)  20.7 us
    all_to_all x1, waiting for transfers between devices, local(): chunk = lax.all_to_all(packed, AXES, 0, 0).reshape(8, 16, CHUNK, 128)  14.6 us
    all_to_all x1, starting transfers between devices, local(): chunk = lax.all_to_all(packed, AXES, 0, 0).reshape(8, 16, CHUNK, 128)  11.1 us
    pallas_call x1, Pallas kernels, local(): pl.pallas_call(coarse_kernel_body, out_shape=jax.ShapeDtypeStruct((8, 16,...  10.9 us
    pallas_call x1, Pallas kernels, local(): pl.pallas_call(fine_kernel, out_shape=(jax.ShapeDtypeStruct((8, OWN, 16,...  9.92 us
    ppermute x6, starting transfers between devices, round_ring(): lax.ppermute(v, 'q', [(i, (i + k) % 4) for i in range(4)])  9.02 us
    ppermute x6, waiting for transfers between devices, round_ring(): lax.ppermute(v, 'q', [(i, (i + k) % 4) for i in range(4)])  6.56 us
    unnamed x16, local copies, waits for them, and re-layouts  5.99 us
  transfers between devices with their start and end apart: 10, of which 6 were waited for; matrix products, arithmetic and copies ran while one was open for 1% of the time, Pallas kernels for 12%

profile of v3, /device:TPU:0, one launch (start us, length us, event | category | flops | bytes accessed | tf_op | source)
XLA Modules:
  0.0 97.3 jit_solution(4699786539878973767)
XLA Ops:
  0.6 0.8 copy-done.1
  1.5 0.9 copy-done.3
  2.4 0.9 copy-done.4
  3.3 2.2 %pack.1 = bf16[128,40,128]{2,1,0:T(8,128)(2,1)} custom-call(f32[32,2,2,256]{3,2,1,0:T(2,128)S(1)} %copy-done.3, f32[32,2,2,256]{3,2,1,0:T(2,128)S(1)} %copy-done.4, bf16[256,128]{1,0:T(8,128)(2,1)S(1)} %bitcast.24), custom_call_target="tpu_custom_call" | custom-call | tf_op jit(solution)/shard_map/pack/pallas_call | solution.py:341
  5.5 11.1 %all-to-all-start = ((bf16[128,40,128]{2,1,0:T(8,128)(2,1)}), bf16[128,40,128]{2,1,0:T(8,128)(2,1)S(1)}, u32[]{:S(2)}, u32[]{:S(2)}) async-start(bf16[128,40,128]{2,1,0:T(8,128)(2,1)} %pack.1), calls=%async_computation | async-start | bytes 2621440 | tf_op jit(solution)/shard_map/all_to_all | solution.py:354
  16.6 0.6 copy.9
  17.3 1.9 %spread_weights.1.spread = bf16[4,2,8,256,256]{4,3,2,1,0:T(8,128)(2,1)S(1)} custom-call(bf16[4,864,32]{2,1,0:T(8,128)(2,1)S(1)} %bitcast.22, bf16[4,864,32]{2,1,0:T(8,128)(2,1)S(1)} %bitcast.21, bf16[32,128]{1,0:T(8,128)(2,1)S(1)} %copy-done.5), custom_call_target="tpu_custom_call" | custom-call | flops 10000000000 | bytes 10000000 | tf_op jit(solution)/shard_map/spread_weights/pallas_call | solution.py:356
  19.2 3.2 %copy-done.6 = bf16[4,2,8,256,256]{4,3,2,1,0:T(8,128)(2,1)} copy-done((bf16[4,2,8,256,256]{4,3,2,1,0:T(8,128)(2,1)}, bf16[4,2,8,256,256]{4,3,2,1,0:T(8,128)(2,1)S(1)}, u32[]{:S(2)}) %copy-start.6) | copy-done | bytes 8388632
  22.5 1.1 %collective-permute-start = (bf16[27,64,256]{2,1,0:T(8,128)(2,1)}, bf16[27,64,256]{2,1,0:T(8,128)(2,1)S(1)}, u32[]{:S(2)}, u32[]{:S(2)}) collective-permute-start(bf16[27,64,256]{2,1,0:T(8,128)(2,1)} %refs_9_.1), channel_id=1, source_target_pairs={{0,2},{1,3},{2,0},{3,1},{4,6},{5,7},{6,4},{7,5},{8,10},{9,11},{10,... | collective-permute-start | bytes 2654216 | tf_op jit(solution)/shard_map/ppermute | solution.py:377
  23.6 14.6 %all-to-all-done = bf16[128,40,128]{2,1,0:T(8,128)(2,1)S(1)} async-done(((bf16[128,40,128]{2,1,0:T(8,128)(2,1)}), bf16[128,40,128]{2,1,0:T(8,128)(2,1)S(1)}, u32[]{:S(2)}, u32[]{:S(2)}) %all-to-all-start) | async-done | bytes 1310752 | tf_op jit(solution)/shard_map/all_to_all | solution.py:354
  38.2 1.8 %collective-permute-start.2 = (bf16[8,16,8,128]{3,2,1,0:T(8,128)(2,1)S(1)}, bf16[8,16,8,128]{3,2,1,0:T(8,128)(2,1)S(1)}, u32[]{:S(2)}, u32[]{:S(2)}) collective-permute-start(bf16[8,16,8,128]{3,2,1,0:T(8,128)(2,1)S(1)} %slice.12.refs_4_), channel_id=1, source_target_pairs={{0,8},{4,12},{8,0},{12,4},{1,9},{5,13},{9,1},{13,5},{2,10},{6,14},... | collective-permute-start | bytes 786440 | tf_op jit(solution)/shard_map/ppermute | solution.py:381
  40.0 2.2 %collective-permute-start.3 = (bf16[8,16,8,128]{3,2,1,0:T(8,128)(2,1)S(1)}, bf16[8,16,8,128]{3,2,1,0:T(8,128)(2,1)S(1)}, u32[]{:S(2)}, u32[]{:S(2)}) collective-permute-start(bf16[8,16,8,128]{3,2,1,0:T(8,128)(2,1)S(1)} %slice.12.refs_4_), channel_id=1, source_target_pairs={{0,12},{4,0},{8,4},{12,8},{1,13},{5,1},{9,5},{13,9},{2,14},{6,2},{... | collective-permute-start | bytes 786440 | tf_op jit(solution)/shard_map/ppermute | solution.py:381
  42.2 9.9 %fine_layers.1 = (bf16[8,2,16,256]{3,2,1,0:T(8,128)(2,1)S(1)}, f32[8,2,16,256]{3,2,1,0:T(8,128)S(1)}) custom-call(bf16[8,16,40,128]{3,2,1,0:T(8,128)(2,1)S(1)} %bitcast.19, bf16[4,2,8,256,256]{4,3,2,1,0:T(8,128)(2,1)} %copy-done.6), custom_call_target="tpu_custom_call" | custom-call | flops 20000000000 | bytes 10000000 | tf_op jit(solution)/shard_map/fine_layers/pallas_call | solution.py:385
  52.7 0.5 collective-permute-done.3.refs_7_
  53.2 1.7 %collective-permute-start.4 = (bf16[8,2,16,256]{3,2,1,0:T(8,128)(2,1)S(1)}, bf16[8,2,16,256]{3,2,1,0:T(8,128)(2,1)S(1)}, u32[]{:S(2)}, u32[]{:S(2)}) collective-permute-start(bf16[8,2,16,256]{3,2,1,0:T(8,128)(2,1)S(1)} %get-tuple-element.15.refs_0_), channel_id=1, source_target_pairs={{0,4},{4,8},{8,12},{12,0},{1,5},{5,9},{9,13},{13,1},{2,6},{6,10},{... | collective-permute-start | bytes 393224 | tf_op jit(solution)/shard_map/ppermute | solution.py:381
  54.9 2.4 %collective-permute-start.5 = (bf16[8,2,16,256]{3,2,1,0:T(8,128)(2,1)S(1)}, bf16[8,2,16,256]{3,2,1,0:T(8,128)(2,1)S(1)}, u32[]{:S(2)}, u32[]{:S(2)}) collective-permute-start(bf16[8,2,16,256]{3,2,1,0:T(8,128)(2,1)S(1)} %get-tuple-element.15.refs_0_), channel_id=1, source_target_pairs={{0,8},{4,12},{8,0},{12,4},{1,9},{5,13},{9,1},{13,5},{2,10},{6,14},... | collective-permute-start | bytes 393224 | tf_op jit(solution)/shard_map/ppermute | solution.py:381
  57.3 0.8 collective-permute-start.6
  58.2 2.2 %collective-permute-done.4.refs_1_ = bf16[8,2,16,256]{3,2,1,0:T(8,128)(2,1)S(1)} collective-permute-done((bf16[8,2,16,256]{3,2,1,0:T(8,128)(2,1)S(1)}, bf16[8,2,16,256]{3,2,1,0:T(8,128)(2,1)S(1)}, u32[]{:S(2)}, u32[]{:S(2)}) %collective-permute-start.4) | collective-permute-done | bytes 131104 | tf_op jit(solution)/shard_map/ppermute | solution.py:381
  60.3 3.7 %collective-permute-done.5.refs_2_ = bf16[8,2,16,256]{3,2,1,0:T(8,128)(2,1)S(1)} collective-permute-done((bf16[8,2,16,256]{3,2,1,0:T(8,128)(2,1)S(1)}, bf16[8,2,16,256]{3,2,1,0:T(8,128)(2,1)S(1)}, u32[]{:S(2)}, u32[]{:S(2)}) %collective-permute-start.5) | collective-permute-done | bytes 131104 | tf_op jit(solution)/shard_map/ppermute | solution.py:381
  64.0 10.9 %coarse_layer.1 = bf16[8,16,8,256]{3,2,1,0:T(8,128)(2,1)S(1)} custom-call(bf16[8,2,16,256]{3,2,1,0:T(8,128)(2,1)S(1)} %get-tuple-element.15.refs_0_, bf16[8,2,16,256]{3,2,1,0:T(8,128)(2,1)S(1)} %collective-permute-done.4.refs_1_, bf16[8,2,16,256]{3,2,1,0:T(8,128)(2,1)S(1)} %collective-permute-done.5.refs_2_, ...), custom_call_target="tpu_custom_call" | custom-call | flops 20000000000 | bytes 10000000 | tf_op jit(solution)/shard_map/coarse_layer/pallas_call | solution.py:402
  75.0 20.7 %all_to_all.10 = bf16[128,8,256]{2,1,0:T(8,128)(2,1)S(1)} all-to-all(bf16[128,8,256]{2,1,0:T(8,128)(2,1)S(1)} %bitcast.23), channel_id=1, replica_groups=mesh['b'=8,'q'=4,'g'=4] {'b','q','g'}, dimensions={0} | all-to-all | bytes 1048576 | tf_op jit(solution)/shard_map/all_to_all | solution.py:417
  95.6 0.3 fusion
  96.0 0.7 slice.13
  96.6 0.7 fusion.2
  (22 shorter events, 0.8 us)
Async XLA Ops:
  0.6 0.8 copy-start.1
  1.5 0.9 copy-start.3
  2.4 0.9 copy-start.4
  5.4 11.2 %copy-start = (bf16[4,27,32,32]{3,2,1,0:T(8,128)(2,1)S(1)}, bf16[4,27,32,32]{3,2,1,0:T(8,128)(2,1)}, u32[]{:S(2)}) copy-start(bf16[4,27,32,32]{3,2,1,0:T(8,128)(2,1)} %param.9) | copy-start | bytes 663556
  5.5 32.7 %all-to-all-start = ((bf16[128,40,128]{2,1,0:T(8,128)(2,1)}), bf16[128,40,128]{2,1,0:T(8,128)(2,1)S(1)}, u32[]{:S(2)}, u32[]{:S(2)}) async-start(bf16[128,40,128]{2,1,0:T(8,128)(2,1)} %pack.1), calls=%async_computation | async-start | bytes 2621440 | tf_op jit(solution)/shard_map/all_to_all | solution.py:354
  16.6 0.7 copy-start.5
  19.2 3.2 %copy-start.6 = (bf16[4,2,8,256,256]{4,3,2,1,0:T(8,128)(2,1)}, bf16[4,2,8,256,256]{4,3,2,1,0:T(8,128)(2,1)S(1)}, u32[]{:S(2)}) copy-start(bf16[4,2,8,256,256]{4,3,2,1,0:T(8,128)(2,1)S(1)} %spread_weights.1.spread) | copy-start | bytes 25165828
  22.5 30.0 %collective-permute-start = (bf16[27,64,256]{2,1,0:T(8,128)(2,1)}, bf16[27,64,256]{2,1,0:T(8,128)(2,1)S(1)}, u32[]{:S(2)}, u32[]{:S(2)}) collective-permute-start(bf16[27,64,256]{2,1,0:T(8,128)(2,1)} %refs_9_.1), channel_id=1, source_target_pairs={{0,2},{1,3},{2,0},{3,1},{4,6},{5,7},{6,4},{7,5},{8,10},{9,11},{10,... | collective-permute-start | bytes 2654216 | tf_op jit(solution)/shard_map/ppermute | solution.py:377
  23.6 34.6 %collective-permute-start.7 = (bf16[27,64,256]{2,1,0:T(8,128)(2,1)}, bf16[27,64,256]{2,1,0:T(8,128)(2,1)S(1)}, u32[]{:S(2)}, u32[]{:S(2)}) collective-permute-start(bf16[27,64,256]{2,1,0:T(8,128)(2,1)} %refs_9_.1), channel_id=1, source_target_pairs={{0,1},{1,0},{2,3},{3,2},{4,5},{5,4},{6,7},{7,6},{8,9},{9,8},{10,11... | collective-permute-start | bytes 2654216 | tf_op jit(solution)/shard_map/ppermute | solution.py:378
  38.2 14.3 %collective-permute-start.1 = (bf16[8,16,8,128]{3,2,1,0:T(8,128)(2,1)S(1)}, bf16[8,16,8,128]{3,2,1,0:T(8,128)(2,1)S(1)}, u32[]{:S(2)}, u32[]{:S(2)}) collective-permute-start(bf16[8,16,8,128]{3,2,1,0:T(8,128)(2,1)S(1)} %slice.12.refs_4_), channel_id=1, source_target_pairs={{0,4},{4,8},{8,12},{12,0},{1,5},{5,9},{9,13},{13,1},{2,6},{6,10},{... | collective-permute-start | bytes 786440 | tf_op jit(solution)/shard_map/ppermute | solution.py:381
  38.2 14.5 %collective-permute-start.2 = (bf16[8,16,8,128]{3,2,1,0:T(8,128)(2,1)S(1)}, bf16[8,16,8,128]{3,2,1,0:T(8,128)(2,1)S(1)}, u32[]{:S(2)}, u32[]{:S(2)}) collective-permute-start(bf16[8,16,8,128]{3,2,1,0:T(8,128)(2,1)S(1)} %slice.12.refs_4_), channel_id=1, source_target_pairs={{0,8},{4,12},{8,0},{12,4},{1,9},{5,13},{9,1},{13,5},{2,10},{6,14},... | collective-permute-start | bytes 786440 | tf_op jit(solution)/shard_map/ppermute | solution.py:381
  40.0 13.2 %collective-permute-start.3 = (bf16[8,16,8,128]{3,2,1,0:T(8,128)(2,1)S(1)}, bf16[8,16,8,128]{3,2,1,0:T(8,128)(2,1)S(1)}, u32[]{:S(2)}, u32[]{:S(2)}) collective-permute-start(bf16[8,16,8,128]{3,2,1,0:T(8,128)(2,1)S(1)} %slice.12.refs_4_), channel_id=1, source_target_pairs={{0,12},{4,0},{8,4},{12,8},{1,13},{5,1},{9,5},{13,9},{2,14},{6,2},{... | collective-permute-start | bytes 786440 | tf_op jit(solution)/shard_map/ppermute | solution.py:381
  53.2 10.8 %collective-permute-start.8 = (bf16[27,64,256]{2,1,0:T(8,128)(2,1)S(1)}, bf16[27,64,256]{2,1,0:T(8,128)(2,1)S(1)}, u32[]{:S(2)}, u32[]{:S(2)}) collective-permute-start(bf16[27,64,256]{2,1,0:T(8,128)(2,1)S(1)} %collective-permute-done.refs_10_), channel_id=1, source_target_pairs={{0,1},{1,0},{2,3},{3,2},{4,5},{5,4},{6,7},{7,6},{8,9},{9,8},{10,11... | collective-permute-start | bytes 2654216 | tf_op jit(solution)/shard_map/ppermute | solution.py:401
  53.2 7.1 %collective-permute-start.4 = (bf16[8,2,16,256]{3,2,1,0:T(8,128)(2,1)S(1)}, bf16[8,2,16,256]{3,2,1,0:T(8,128)(2,1)S(1)}, u32[]{:S(2)}, u32[]{:S(2)}) collective-permute-start(bf16[8,2,16,256]{3,2,1,0:T(8,128)(2,1)S(1)} %get-tuple-element.15.refs_0_), channel_id=1, source_target_pairs={{0,4},{4,8},{8,12},{12,0},{1,5},{5,9},{9,13},{13,1},{2,6},{6,10},{... | collective-permute-start | bytes 393224 | tf_op jit(solution)/shard_map/ppermute | solution.py:381
  54.9 9.1 %collective-permute-start.5 = (bf16[8,2,16,256]{3,2,1,0:T(8,128)(2,1)S(1)}, bf16[8,2,16,256]{3,2,1,0:T(8,128)(2,1)S(1)}, u32[]{:S(2)}, u32[]{:S(2)}) collective-permute-start(bf16[8,2,16,256]{3,2,1,0:T(8,128)(2,1)S(1)} %get-tuple-element.15.refs_0_), channel_id=1, source_target_pairs={{0,8},{4,12},{8,0},{12,4},{1,9},{5,13},{9,1},{13,5},{2,10},{6,14},... | collective-permute-start | bytes 393224 | tf_op jit(solution)/shard_map/ppermute | solution.py:381
  57.3 6.7 %collective-permute-start.6 = (bf16[8,2,16,256]{3,2,1,0:T(8,128)(2,1)S(1)}, bf16[8,2,16,256]{3,2,1,0:T(8,128)(2,1)S(1)}, u32[]{:S(2)}, u32[]{:S(2)}) collective-permute-start(bf16[8,2,16,256]{3,2,1,0:T(8,128)(2,1)S(1)} %get-tuple-element.15.refs_0_), channel_id=1, source_target_pairs={{0,12},{4,0},{8,4},{12,8},{1,13},{5,1},{9,5},{13,9},{2,14},{6,2},{... | collective-permute-start | bytes 393224 | tf_op jit(solution)/shard_map/ppermute | solution.py:381
  64.0 31.6 %copy-start.7 = (bf16[1024,256]{1,0:T(8,128)(2,1)S(1)}, bf16[1024,256]{1,0:T(8,128)(2,1)}, u32[]{:S(2)}) copy-start(bf16[1024,256]{1,0:T(8,128)(2,1)} %constant.7.clone) | copy-start | bytes 1572868
  74.9 21.7 %copy-start.2 = (bf16[256,1,1,128]{3,0,2,1:T(8,128)(2,1)S(1)}, bf16[256,1,1,128]{3,0,2,1:T(8,128)(2,1)}, u32[]{:S(2)}) copy-start(bf16[256,1,1,128]{3,0,2,1:T(8,128)(2,1)} %param.11) | copy-start | bytes 196612

commit v4 on v3

--- a/solution.py
+++ b/solution.py
@@ -12,15 +12,20 @@
 BF = jnp.bfloat16
 F32 = jnp.float32
 LAYERS = 4
-AXES = ("b", "q", "g")
+AXES = ("b", "q", "l", "c")
+CHIPS = AXES[:3]
 FINE_STEP = 0.5
 COARSE_STEP = 1.5
-NOW, PREV, OWN = 10, 8, 2
-CHUNK = 2 * (NOW + PREV + OWN)
-
-
-def window_start(b, q, g):
-    return 4 * (4 * b + g) - 6 + 2 * q
+NOW, OWN = 10, 2
+SHIFT = 4
+NOWS, PREVS, COTS = NOW + SHIFT, NOW - 2 + SHIFT, 8 + SHIFT
+ROWS = (32, 2 * PREVS, 2 * COTS)
+CHUNK = sum(ROWS)
+EARLY = 13
+
+
+def window_start(b, q, l):
+    return 16 * b + 8 * l - 6 + 2 * q
 
 
 def iota(shape, axis):
@@ -44,15 +49,6 @@
     return jnp.where(lane % 32 == channel // 8, 1.0 - 2.0 * odd.astype(F32), 0.0).astype(BF)
 
 
-def receive_table():
-    table = np.zeros((128, 8, 256), np.float32)
-    for source in range(128):
-        group = 4 * (source // 16) + source % 4
-        for k in range(8):
-            table[source, k, 128 * (k // 4) + 4 * group + k % 4] = 1
-    return table.reshape(1024, 256).astype(BF)
-
-
 def dot(x, y):
     return jnp.dot(x, y, preferred_element_type=F32)
 
@@ -69,28 +65,53 @@
     return jnp.concatenate([ref[:, a, b, :] for a in range(2) for b in range(2)], axis=0)
 
 
-def pack_kernel(now, prev, cot, out, first, middle, final):
+def pack_kernel(now_in, prev_in, cot_in, out, now, prev, cot, first, second, third, sems):
+    copies = []
+    for i, (source, target) in enumerate(((now_in, now), (prev_in, prev), (cot_in, cot))):
+        copy = pltpu.make_async_copy(source, target, sems.at[i])
+        copy.start()
+        copies.append(copy)
+    k, lane = iota((32, 256), 0), iota((32, 256), 1)
+    for_first = jnp.where(k < 2 * NOWS, lane - 2 * (k % NOWS) - k // NOWS, -1000)
+    k, lane = iota((24, 256), 0), iota((24, 256), 1)
+    for_second = lane - 2 * (1 + k % PREVS) - k // PREVS
+    for_third = jnp.where(lane // 128 == k // COTS, lane % 128 - k % COTS, -1000)
+    for target in range(0, 64, 2):
+        spots = [(t // 8, t // 2 % 4, t % 2) for t in (target, target + 1)]
+        for t, spot in enumerate(spots):
+            at = 32 * (target + t)
+            first[at : at + 32] = ones_where(for_first == 2 * window_start(*spot)).astype(BF)
+        pair = [ones_where(for_second == 2 * window_start(*spot)) for spot in spots]
+        second[24 * target : 24 * target + 48] = jnp.concatenate(pair, axis=0).astype(BF)
+        pair = [ones_where(for_third == 16 * b + 8 * l - 2) for b, _, l in spots]
+        third[24 * target : 24 * target + 48] = jnp.concatenate(pair, axis=0).astype(BF)
+    for copy in copies:
+        copy.wait()
     now_rows = parity_rows(now).astype(BF)
     prev_rows = parity_rows(prev).astype(BF)
-    both = jnp.concatenate([now_rows, cot[0:128, :], cot[128:256, :]], axis=1)
-    k, lane = iota((16, 256), 0), iota((16, 256), 1)
-    for_first = lane - 2 * (k % NOW) - k // NOW
-    for_final = lane - 2 * (1 + k % PREV) - k // PREV
-    k, lane = iota((8, 512), 0), iota((8, 512), 1)
-    for_middle = jnp.where(k < 4, jnp.where(lane < 256, lane - 2 * (k + 6) - 1, -1000), -1000)
-    at = 2 * (lane % 128 - 4 - k % OWN)
-    for_middle = jnp.where((k >= 4) & (lane >= 256) & (lane // 128 - 2 == (k - 4) // OWN), at, for_middle)
-    for target in range(128):
-        at = 2 * window_start(target // 16, target // 4 % 4, target % 4)
-        first[16 * target : 16 * target + 16] = ones_where(for_first == at).astype(BF)
-        final[16 * target : 16 * target + 16] = ones_where(for_final == at).astype(BF)
-        middle[8 * target : 8 * target + 8] = ones_where(for_middle == at)
-    part = 32
-    for t in range(0, 128, part):
-        one = dot_nt(first[pl.ds(16 * t, 16 * part), :], now_rows).reshape(part, 16, 128)
-        two = dot_nt(middle[pl.ds(8 * t, 8 * part), :].astype(BF), both).reshape(part, 8, 128)
-        three = dot_nt(final[pl.ds(16 * t, 16 * part), :], prev_rows).reshape(part, 16, 128)
-        out[pl.ds(t, part)] = jnp.concatenate([one, two, three], axis=1).astype(BF)
+    cot_rows = jnp.concatenate([cot[0:128, :], cot[128:256, :]], axis=1)
+    part = 16
+    for t in range(0, 64, part):
+        groups = []
+        for table, size, rows in zip((first, second, third), ROWS, (now_rows, prev_rows, cot_rows)):
+            groups.append(dot_nt(table[pl.ds(size * t, size * part), :], rows).reshape(part, size, 128))
+        out[pl.ds(t, part)] = jnp.concatenate(groups, axis=1).astype(BF)
+
+
+def sort_table(core):
+    row, column = iota((128, 128), 0), iota((128, 128), 1)
+    y = row % 16
+    source = (y + core) % 2
+    return ones_where(column == (source * 8 + y // 2) * 8 + row // 16).astype(BF)
+
+
+def sorted_parts(table, mine, other, x, start, stop):
+    rows = jnp.concatenate([mine[x].astype(F32), other[x].astype(F32)], axis=0)
+    parts = []
+    for k in range(start, stop, 8):
+        moved = dot(table, rows[:, k : k + 8, :].reshape(128, 128).astype(BF))
+        parts += [moved[16 * j : 16 * j + 16] for j in range(8)]
+    return parts
 
 
 def split_dot(x, y):
@@ -168,14 +189,16 @@
     return total
 
 
-def fine_kernel(chunk, spread, mid, base, cur, old, s0, s1, h0, h1, weights, sems):
+def fine_kernel(mine, other, spread, mid, base, cur, old, s0, s1, h0, h1, weights, sems):
     copies = []
     for layer in range(LAYERS):
         copy = pltpu.make_async_copy(spread.at[layer], weights.at[layer], sems.at[layer])
         copy.start()
         copies.append(copy)
-    start = window_start(*(lax.axis_index(name) for name in AXES))
-    swap = swap_table(16, 8)
+    core = lax.axis_index("c")
+    shift = SHIFT * core
+    start = window_start(*(lax.axis_index(name) for name in CHIPS)) + shift
+    table = sort_table(core)
     for ref in (s0, s1, h0, h1):
         for x in (0, 9):
             ref[x] = jnp.zeros((NOW + 2, 16, 256), BF)
@@ -187,21 +210,16 @@
         return jnp.where((at >= 0) & (at < 128), 1.0, 0.0).astype(F32)
 
     def unpack(x, carry):
-        rows = chunk[x].astype(F32)
-        parts = []
-        for k in range(0, CHUNK, 8):
-            group = rows[:, k : k + 8, :].reshape(128, 128).astype(BF)
-            moved = dot(swap, group)
-            parts += [moved[16 * j : 16 * j + 16] for j in range(8)]
+        parts = sorted_parts(table, mine, other, x, 0, ROWS[0] + ROWS[1])
+        for z in range(NOWS):
+            cur[x, z] = jnp.concatenate([parts[z], parts[NOWS + z]], axis=1)
+        at = ROWS[0]
+        for z in range(PREVS):
+            old[x, z + 1] = jnp.concatenate([parts[at + z], parts[at + PREVS + z]], axis=1)
         for z in range(NOW):
-            v = jnp.concatenate([parts[z], parts[NOW + z]], axis=1)
-            cur[x, z] = v
+            v = cur[x, shift + z]
             s0[x + 1, z + 1] = v.astype(BF)
             s1[x + 1, z + 1] = moved_rows(v).astype(BF)
-        at = 2 * (NOW + OWN)
-        for z in range(PREV):
-            v = jnp.concatenate([parts[at + z], parts[at + PREV + z]], axis=1)
-            old[x, z + 1] = v
         return carry
 
     lax.fori_loop(0, 8, unpack, 0)
@@ -233,7 +251,7 @@
             v = v.reshape(xs, zs, 16, 256)
             for z in range(zs):
                 at = layer + 1 + z
-                here = (pl.ds(x0, xs), at)
+                here = (pl.ds(x0, xs), shift + at)
                 part = (2.0 * now[here] - before[here] - FINE_STEP * v[:, z]) * keep(at)
                 before[here] = part
                 if not last:
@@ -246,7 +264,7 @@
 
     haar = haar_signs(iota((256, 256), 0), iota((256, 256), 1))
     scale = 1.0 / math.sqrt(8.0)
-    own = (slice(None), slice(4, 6))
+    own = (slice(None), pl.ds(shift + 4, OWN))
     latest = now[own].reshape(256, 256)
     earlier = before[own].reshape(256, 256)
     mid[...] = (split_dot(latest, haar) * scale).astype(BF).reshape(8, OWN, 16, 256)
@@ -254,14 +272,16 @@
 
 
 def coarse_kernel_body(*refs):
-    own, cots, base = refs[0:4], refs[4:8], refs[8]
-    pieces, out, state, hidden, weights, sems = refs[9:13], refs[13], refs[14], refs[15], refs[16], refs[17]
-    b, quarter, g = (lax.axis_index(name) for name in AXES)
-    start = 4 * (4 * b + g) - 1
-    swap = swap_table(16, 8)
+    own, mine, other, base, pieces = refs[0:4], refs[4], refs[5], refs[6], refs[7:13]
+    out, state, hidden, weights, cots, sems = refs[13:19]
+    b, quarter, l, core = (lax.axis_index(name) for name in AXES)
+    start = 4 * (4 * b + 2 * l + core) - 1
+    table = sort_table(core)
     copies = []
-    for i, w in enumerate(pieces):
-        copy = pltpu.make_async_copy(w, weights.at[:, pl.ds(64 * i, 64), :], sems.at[i])
+    spots = ((0, 27, 0), (0, 27, 1), (0, EARLY, 2), (EARLY, 27, 2), (0, EARLY, 3), (EARLY, 27, 3))
+    for i, (w, (low, high, part)) in enumerate(zip(pieces, spots)):
+        target = weights.at[pl.ds(low, high - low), pl.ds(64 * part, 64), :]
+        copy = pltpu.make_async_copy(w, target, sems.at[i])
         copy.start()
         copies.append(copy)
     for s in range(2):
@@ -280,14 +300,12 @@
         for z in range(OWN):
             place(0, 0, 8, z0 + z, own[k][:, z].astype(F32))
 
-        def unpack(x, carry, k=k, z0=z0):
-            moved = dot(swap, cots[k][x].astype(F32).reshape(128, 128).astype(BF))
-            for z in range(OWN):
-                low, high = (moved[16 * j : 16 * j + 16] for j in (4 + z, 4 + OWN + z))
-                place(1, x, 1, z0 + z, jnp.concatenate([low, high], axis=1)[None])
-            return carry
-
-        lax.fori_loop(0, 8, unpack, 0, unroll=True)
+    for x in range(8):
+        parts = sorted_parts(table, mine, other, x, ROWS[0] + ROWS[1], CHUNK)
+        for z in range(COTS):
+            cots[x, z] = jnp.concatenate([parts[z], parts[COTS + z]], axis=1)
+        for z in range(8):
+            place(1, x, 1, z, cots[x, SHIFT * core + z][None])
     for copy in copies:
         copy.wait()
     taps = [(x, y, z) for x in (-1, 0, 1) for y in (-1, 0, 1) for z in (-1, 0, 1)]
@@ -337,21 +355,30 @@
         out[x] = dot(back, rows.reshape(128, 256).astype(BF)).astype(BF).reshape(16, 8, 256)
 
 
+def receive_table():
+    row = np.arange(1024)
+    at = row // 128 * 16 + row // 8 % 4 * 4 + row % 4 + row // 4 % 2 * 128
+    return (np.arange(256)[None] == at[:, None]).astype(BF)
+
+
 def local(fine_prev, fine_now, fine_kernels, coarse_kernel, cotangent):
     packed = pl.pallas_call(
         pack_kernel,
-        out_shape=jax.ShapeDtypeStruct((128, CHUNK, 128), BF),
-        in_specs=vmem(3),
+        out_shape=jax.ShapeDtypeStruct((64, CHUNK, 128), BF),
+        in_specs=[pl.BlockSpec(memory_space=pltpu.HBM)] * 3,
         out_specs=pl.BlockSpec(memory_space=pltpu.VMEM),
-        scratch_shapes=[
-            pltpu.VMEM((2048, 256), BF),
-            pltpu.VMEM((1024, 512), F32),
-            pltpu.VMEM((2048, 256), BF),
-        ],
-        compiler_params=pltpu.CompilerParams(vmem_limit_bytes=32 << 20),
+        scratch_shapes=[pltpu.VMEM((32, 2, 2, 256), F32)] * 2
+        + [pltpu.VMEM((256, 128), BF)]
+        + [pltpu.VMEM((64 * size, 256), BF) for size in ROWS]
+        + [pltpu.SemaphoreType.DMA((3,))],
+        compiler_params=pltpu.CompilerParams(vmem_limit_bytes=60 << 20),
         name="pack",
     )(fine_now, fine_prev, cotangent.reshape(256, 128))
-    chunk = lax.all_to_all(packed, AXES, 0, 0).reshape(8, 16, CHUNK, 128)
+    packed, kernel_part = lax.optimization_barrier((packed, coarse_kernel))
+    early = lax.ppermute(kernel_part[:EARLY], "l", [(0, 1), (1, 0)])
+    across = lax.ppermute(kernel_part[EARLY:], "l", [(0, 1), (1, 0)])
+    there = lax.ppermute(kernel_part, "c", [(0, 1), (1, 0)])
+    mine = lax.all_to_all(packed, CHIPS, 0, 0)
     tile = np.tile(np.eye(32, dtype=np.float32), (1, 4)).astype(BF)
     weights = pl.pallas_call(
         weight_kernel,
@@ -364,7 +391,7 @@
         ],
         out_specs=pl.BlockSpec((1, 2, 8, 256, 256), lambda i: (i, 0, 0, 0, 0)),
         scratch_shapes=[pltpu.VMEM((27, 32, 128), BF)],
-        compiler_params=pltpu.CompilerParams(vmem_limit_bytes=32 << 20),
+        compiler_params=pltpu.CompilerParams(vmem_limit_bytes=60 << 20),
         cost_estimate=pl.CostEstimate(flops=10**10, bytes_accessed=10**7, transcendentals=0),
         name="spread_weights",
     )(
@@ -373,14 +400,12 @@
         tile,
     )
 
-    kernel_part, weights = lax.optimization_barrier((coarse_kernel, weights))
-    across = lax.ppermute(kernel_part, "g", [(i, i ^ 2) for i in range(4)])
-    there = lax.ppermute(kernel_part, "g", [(i, i ^ 1) for i in range(4)])
-
+    mine, weights, there, early = lax.optimization_barrier((mine, weights, there, early))
+    other = lax.ppermute(mine, "c", [(0, 1), (1, 0)]).reshape(8, 8, CHUNK, 128)
+    mine = mine.reshape(8, 8, CHUNK, 128)
     def round_ring(v):
         return [v] + [lax.ppermute(v, "q", [(i, (i + k) % 4) for i in range(4)]) for k in range(1, 4)]
 
-    cots = round_ring(lax.slice_in_dim(chunk, 16, 24, axis=2))
     buffer = pltpu.VMEM((10, NOW + 2, 16, 256), BF)
     mid, base = pl.pallas_call(
         fine_kernel,
@@ -388,48 +413,52 @@
             jax.ShapeDtypeStruct((8, OWN, 16, 256), BF),
             jax.ShapeDtypeStruct((8, OWN, 16, 256), F32),
         ),
-        in_specs=vmem(1) + [pl.BlockSpec(memory_space=pl.ANY)],
+        in_specs=vmem(2) + [pl.BlockSpec(memory_space=pl.ANY)],
         out_specs=tuple(vmem(2)),
-        scratch_shapes=[pltpu.VMEM((8, NOW, 16, 256), F32)] * 2
+        scratch_shapes=[pltpu.VMEM((8, NOWS, 16, 256), F32)] * 2
         + [buffer] * 4
         + [pltpu.VMEM((LAYERS, 2, 8, 256, 256), BF), pltpu.SemaphoreType.DMA((LAYERS,))],
         compiler_params=pltpu.CompilerParams(vmem_limit_bytes=48 << 20),
-        cost_estimate=pl.CostEstimate(flops=2 * 10**10, bytes_accessed=10**7, transcendentals=10**6),
+        cost_estimate=pl.CostEstimate(flops=10**9, bytes_accessed=10**6, transcendentals=10**6),
         name="fine_layers",
-    )(chunk, weights)
-    mid, across, *cots = lax.optimization_barrier((mid, across, *cots))
-    opposite = lax.ppermute(across, "g", [(i, i ^ 1) for i in range(4)])
+    )(mine, other, weights)
+    mid, across = lax.optimization_barrier((mid, across))
+    states = round_ring(mid)
+    opposite = lax.ppermute(across, "c", [(0, 1), (1, 0)])
+    early_opposite = lax.ppermute(early, "c", [(0, 1), (1, 0)])
     partial = pl.pallas_call(
         coarse_kernel_body,
         out_shape=jax.ShapeDtypeStruct((8, 16, 8, 256), BF),
-        in_specs=vmem(9) + [pl.BlockSpec(memory_space=pl.ANY)] * 4,
+        in_specs=vmem(7) + [pl.BlockSpec(memory_space=pl.ANY)] * 6,
         out_specs=pl.BlockSpec(memory_space=pltpu.VMEM),
         scratch_shapes=[
             pltpu.VMEM((2, 3, 10, 8, 16, 256), BF),
             pltpu.VMEM((2, 3, 10, 6, 16, 256), BF),
             pltpu.VMEM((27, 256, 256), BF),
-            pltpu.SemaphoreType.DMA((4,)),
+            pltpu.VMEM((8, COTS, 16, 256), F32),
+            pltpu.SemaphoreType.DMA((6,)),
         ],
         compiler_params=pltpu.CompilerParams(vmem_limit_bytes=48 << 20),
         cost_estimate=pl.CostEstimate(flops=2 * 10**10, bytes_accessed=10**7, transcendentals=10**6),
         name="coarse_layer",
-    )(*round_ring(mid), *cots, base, coarse_kernel, across, there, opposite)
+    )(*states, mine, other, base, coarse_kernel, there, early, across, early_opposite, opposite)
     parts = lax.all_to_all(partial.reshape(128, 8, 256), AXES, 0, 0)
-    sums = lax.dot_general(
-        parts.reshape(1024, 256), receive_table(), (((0,), (0,)), ((), ())), preferred_element_type=F32
-    )
-    coarse_next = sums[:, 0:128].reshape(256, 1, 1, 128)
-    state_adjoint = 2.0 * cotangent.astype(F32) + sums[:, 128:256].reshape(256, 1, 1, 128)
-    return coarse_next, state_adjoint
+    parts = parts.reshape(1024, 256)
+    table = receive_table()
+    over_rows = (((0,), (0,)), ((), ()))
+    coarse_next = lax.dot_general(parts, table[:, 0:128], over_rows, preferred_element_type=F32)
+    state_adjoint = lax.dot_general(parts, table[:, 128:256], over_rows, preferred_element_type=F32)
+    state_adjoint = state_adjoint + 2.0 * cotangent.reshape(256, 128).astype(F32)
+    return coarse_next.reshape(256, 1, 1, 128), state_adjoint.reshape(256, 1, 1, 128)
 
 
 def solution(mesh):
-    split = Mesh(mesh.devices.reshape(8, 4, 4), AXES)
-    rows = P(None, "b", ("q", "g"), None)
+    split = Mesh(mesh.devices.reshape(8, 4, 2, 2), AXES)
+    rows = P(None, "b", ("q", "l", "c"), None)
     return jax.shard_map(
         local,
         mesh=split,
-        in_specs=(rows, rows, P(), P(None, ("q", "g"), None), rows),
+        in_specs=(rows, rows, P(), P(None, ("q", "l", "c"), None), rows),
         out_specs=(rows, rows),
         check_vma=False,
     )

time: 98.5 us -> 103 us (1.046)
  Pallas kernels: 24.9 us -> 32 us
  local copies, waits for them, and re-layouts: 7.27 us -> 3.06 us
  matrix products: 0.33 us -> 1.99 us
  starting transfers between devices: 21.3 us -> 20.1 us
    ppermute x3 -> x6, waiting for transfers between devices: 0.3 us -> 17.3 us  [the longest x1 15.1 us: local(): early = lax.ppermute(kernel_part[:EARLY], 'l', [(0, 1), (1, 0)])]
    all_to_all x1, waiting for transfers between devices: 14.6 us -> 0.01 us  [local(): mine = lax.all_to_all(packed, CHIPS, 0, 0)]
    unnamed x16 -> x10, local copies, waits for them, and re-layouts: 5.99 us -> 0.03 us
    pallas_call x1, Pallas kernels: 1.92 us -> 6.22 us  [local(): pl.pallas_call(weight_kernel, grid=(LAYERS,), out_shape=jax.ShapeDtypeStr...]
    ppermute x6 -> x3, starting transfers between devices: 9.02 us -> 5.42 us  [round_ring(): lax.ppermute(v, 'q', [(i, (i + k) % 4) for i in range(4)])]
    ppermute x3 -> x6, starting transfers between devices: 1.09 us -> 3.06 us  [the longest x1 1.57 us: local(): early = lax.ppermute(kernel_part[:EARLY], 'l', [(0, 1), (1, 0)])]
    dot_general x1 -> x2, matrix products: 0.33 us -> 1.99 us  [the longest x1 1 us: local(): lax.dot_general(parts, table[:, 0:128], over_rows, preferred_element_type...]
    transpose x1, local copies, waits for them, and re-layouts: 0.57 us -> 2.2 us  [local(): jnp.swapaxes(fine_kernels, 2, 3).reshape(LAYERS, 864, 32)]
  transfers between devices with their start and end apart: 10 -> 10, of which waited for: 6 -> 4; matrix products, arithmetic and copies ran while one was open for 1% -> 3% of each run, Pallas kernels for 12% -> 16%
where the time goes in v4:
time: 103 us; the launch traced here: 102 us
  Pallas kernels  32 us (31%)
  waiting for transfers between devices  22.3 us (22%)
  blocking collectives  21.3 us (21%)
  starting transfers between devices  20.1 us (20%)
  local copies, waits for them, and re-layouts  3.06 us (3%)
  matrix products  1.99 us (2%)
    all_to_all x1, blocking collectives, local(): parts = lax.all_to_all(partial.reshape(128, 8, 256), AXES, 0, 0)  21.3 us
    ppermute x1, waiting for transfers between devices, local(): early = lax.ppermute(kernel_part[:EARLY], 'l', [(0, 1), (1, 0)])  15.1 us
    pallas_call x1, Pallas kernels, local(): pl.pallas_call(coarse_kernel_body, out_shape=jax.ShapeDtypeStruct((8, 16,...  12.4 us
    all_to_all x1, starting transfers between devices, local(): mine = lax.all_to_all(packed, CHIPS, 0, 0)  11.6 us
    pallas_call x1, Pallas kernels, local(): pl.pallas_call(fine_kernel, out_shape=(jax.ShapeDtypeStruct((8, OWN, 16,...  10.4 us
    pallas_call x1, Pallas kernels, local(): pl.pallas_call(weight_kernel, grid=(LAYERS,), out_shape=jax.ShapeDtypeStr...  6.22 us
    ppermute x3, starting transfers between devices, round_ring(): lax.ppermute(v, 'q', [(i, (i + k) % 4) for i in range(4)])  5.42 us
    ppermute x3, waiting for transfers between devices, round_ring(): lax.ppermute(v, 'q', [(i, (i + k) % 4) for i in range(4)])  5.05 us
  transfers between devices with their start and end apart: 10, of which 4 were waited for; matrix products, arithmetic and copies ran while one was open for 3% of the time, Pallas kernels for 16%

profile of v4, /device:TPU:0, one launch (start us, length us, event | category | flops | bytes accessed | tf_op | source)
XLA Modules:
  0.0 101.6 jit_solution(1395592642296487474)
XLA Ops:
  0.6 3.0 %pack.1 = bf16[64,80,128]{2,1,0:T(8,128)(2,1)} custom-call(f32[32,2,2,256]{3,2,1,0:T(2,128)} %now_in.1, f32[32,2,2,256]{3,2,1,0:T(2,128)} %prev_in.1, bf16[256,128]{1,0:T(8,128)(2,1)} %bitcast.29), custom_call_target="tpu_custom_call" | custom-call | tf_op jit(solution)/shard_map/pack/pallas_call | solution.py:365
  3.7 11.6 %all-to-all-start = ((bf16[64,80,128]{2,1,0:T(8,128)(2,1)}), bf16[64,80,128]{2,1,0:T(8,128)(2,1)S(1)}, u32[]{:S(2)}, u32[]{:S(2)}) async-start(bf16[64,80,128]{2,1,0:T(8,128)(2,1)} %pack.1), calls=%async_computation | async-start | bytes 2621440 | tf_op jit(solution)/shard_map/all_to_all | solution.py:381
  15.3 0.1 collective-permute-start
  15.4 0.8 slice.6
  16.2 1.6 %collective-permute-start.1 = (bf16[13,64,256]{2,1,0:T(8,128)(2,1)}, bf16[13,64,256]{2,1,0:T(8,128)(2,1)S(1)}, u32[]{:S(2)}, u32[]{:S(2)}) collective-permute-start(bf16[13,64,256]{2,1,0:T(8,128)(2,1)} %slice.6), channel_id=1, source_target_pairs={{0,2},{2,0},{1,3},{3,1},{4,6},{6,4},{5,7},{7,5},{8,10},{10,8},{9,1... | collective-permute-start | bytes 1277960 | tf_op jit(solution)/shard_map/ppermute | solution.py:378
  17.8 2.2 %copy.10 = bf16[4,27,32,32]{3,2,1,0:T(8,128)(2,1)} copy(bf16[4,27,32,32]{2,3,1,0:T(8,128)(2,1)} %bitcast.26) | data formatting | bytes 442368 | tf_op jit(solution)/shard_map/transpose | solution.py:398
  20.0 6.2 %spread_weights.1.spread = bf16[4,2,8,256,256]{4,3,2,1,0:T(8,128)(2,1)} custom-call(bf16[4,864,32]{2,1,0:T(8,128)(2,1)} %bitcast.28, bf16[4,864,32]{2,1,0:T(8,128)(2,1)} %bitcast.27, bf16[32,128]{1,0:T(8,128)(2,1)} %constant.8.clone.tile), custom_call_target="tpu_custom_call" | custom-call | flops 10000000000 | bytes 10000000 | tf_op jit(solution)/shard_map/spread_weights/pallas_call | solution.py:383
  26.2 15.1 %collective-permute-done.1.refs_9_ = bf16[13,64,256]{2,1,0:T(8,128)(2,1)S(1)} collective-permute-done((bf16[13,64,256]{2,1,0:T(8,128)(2,1)}, bf16[13,64,256]{2,1,0:T(8,128)(2,1)S(1)}, u32[]{:S(2)}, u32[]{:S(2)}) %collective-permute-start.1) | collective-permute-done | bytes 426016 | tf_op jit(solution)/shard_map/ppermute | solution.py:378
  41.3 0.0 collective-permute-start.2
  41.4 0.8 collective-permute-start.3
  42.2 2.2 %collective-permute-done.2 = bf16[64,80,128]{2,1,0:T(8,128)(2,1)S(1)} collective-permute-done((bf16[64,80,128]{2,1,0:T(8,128)(2,1)S(1)}, bf16[64,80,128]{2,1,0:T(8,128)(2,1)S(1)}, u32[]{:S(2)}, u32[]{:S(2)}) %collective-permute-start.2) | collective-permute-done | bytes 1310752 | tf_op jit(solution)/shard_map/ppermute | solution.py:404
  44.3 10.4 %fine_layers.1 = (bf16[8,2,16,256]{3,2,1,0:T(8,128)(2,1)S(1)}, f32[8,2,16,256]{3,2,1,0:T(8,128)S(1)}) custom-call(bf16[8,8,80,128]{3,2,1,0:T(8,128)(2,1)S(1)} %bitcast.21, bf16[8,8,80,128]{3,2,1,0:T(8,128)(2,1)S(1)} %bitcast.23, bf16[4,2,8,256,256]{4,3,2,1,0:T(8,128)(2,1)} %spread_weights.1.spread), custom_call_target="tpu_custom_call" | custom-call | flops 1000000000 | bytes 1000000 | tf_op jit(solution)/shard_map/fine_layers/pallas_call | solution.py:410
  54.8 0.2 collective-permute-start.8
  55.0 0.4 collective-permute-start.7
  55.4 1.2 %collective-permute-start.4 = (bf16[8,2,16,256]{3,2,1,0:T(8,128)(2,1)S(1)}, bf16[8,2,16,256]{3,2,1,0:T(8,128)(2,1)S(1)}, u32[]{:S(2)}, u32[]{:S(2)}) collective-permute-start(bf16[8,2,16,256]{3,2,1,0:T(8,128)(2,1)S(1)} %get-tuple-element.17.refs_0_), channel_id=1, source_target_pairs={{0,4},{4,8},{8,12},{12,0},{1,5},{5,9},{9,13},{13,1},{2,6},{6,10},{... | collective-permute-start | bytes 393224 | tf_op jit(solution)/shard_map/ppermute | solution.py:407
  56.6 2.8 %collective-permute-start.5 = (bf16[8,2,16,256]{3,2,1,0:T(8,128)(2,1)S(1)}, bf16[8,2,16,256]{3,2,1,0:T(8,128)(2,1)S(1)}, u32[]{:S(2)}, u32[]{:S(2)}) collective-permute-start(bf16[8,2,16,256]{3,2,1,0:T(8,128)(2,1)S(1)} %get-tuple-element.17.refs_0_), channel_id=1, source_target_pairs={{0,8},{4,12},{8,0},{12,4},{1,9},{5,13},{9,1},{13,5},{2,10},{6,14},... | collective-permute-start | bytes 393224 | tf_op jit(solution)/shard_map/ppermute | solution.py:407
  59.4 1.4 %collective-permute-start.6 = (bf16[8,2,16,256]{3,2,1,0:T(8,128)(2,1)S(1)}, bf16[8,2,16,256]{3,2,1,0:T(8,128)(2,1)S(1)}, u32[]{:S(2)}, u32[]{:S(2)}) collective-permute-start(bf16[8,2,16,256]{3,2,1,0:T(8,128)(2,1)S(1)} %get-tuple-element.17.refs_0_), channel_id=1, source_target_pairs={{0,12},{4,0},{8,4},{12,8},{1,13},{5,1},{9,5},{13,9},{2,14},{6,2},{... | collective-permute-start | bytes 393224 | tf_op jit(solution)/shard_map/ppermute | solution.py:407
  60.8 1.5 %collective-permute-done.4.refs_1_ = bf16[8,2,16,256]{3,2,1,0:T(8,128)(2,1)S(1)} collective-permute-done((bf16[8,2,16,256]{3,2,1,0:T(8,128)(2,1)S(1)}, bf16[8,2,16,256]{3,2,1,0:T(8,128)(2,1)S(1)}, u32[]{:S(2)}, u32[]{:S(2)}) %collective-permute-start.4) | collective-permute-done | bytes 131104 | tf_op jit(solution)/shard_map/ppermute | solution.py:407
  62.2 3.6 %collective-permute-done.5.refs_2_ = bf16[8,2,16,256]{3,2,1,0:T(8,128)(2,1)S(1)} collective-permute-done((bf16[8,2,16,256]{3,2,1,0:T(8,128)(2,1)S(1)}, bf16[8,2,16,256]{3,2,1,0:T(8,128)(2,1)S(1)}, u32[]{:S(2)}, u32[]{:S(2)}) %collective-permute-start.5) | collective-permute-done | bytes 131104 | tf_op jit(solution)/shard_map/ppermute | solution.py:407
  65.8 12.4 %coarse_layer.1 = bf16[8,16,8,256]{3,2,1,0:T(8,128)(2,1)S(1)} custom-call(bf16[8,2,16,256]{3,2,1,0:T(8,128)(2,1)S(1)} %get-tuple-element.17.refs_0_, bf16[8,2,16,256]{3,2,1,0:T(8,128)(2,1)S(1)} %collective-permute-done.4.refs_1_, bf16[8,2,16,256]{3,2,1,0:T(8,128)(2,1)S(1)} %collective-permute-done.5.refs_2_, ...), custom_call_target="tpu_custom_call" | custom-call | flops 20000000000 | bytes 10000000 | tf_op jit(solution)/shard_map/coarse_layer/pallas_call | solution.py:429
  78.3 0.0 copy-start.2
  78.3 21.3 %all_to_all.10 = bf16[128,8,256]{2,1,0:T(8,128)(2,1)S(1)} all-to-all(bf16[128,8,256]{2,1,0:T(8,128)(2,1)S(1)} %bitcast.25), channel_id=1, replica_groups=mesh['b'=8,'q'=4,'l'=2,'c'=2] {'b','q','l','c'}, dimensions={0} | all-to-all | bytes 1048576 | tf_op jit(solution)/shard_map/all_to_all | solution.py:445
  99.6 1.0 convolution_add_fusion
  100.6 1.0 fusion.1
  (16 shorter events, 0.1 us)
Async XLA Ops:
  3.6 11.7 %copy-start.1 = (bf16[27,64,256]{2,1,0:T(8,128)(2,1)S(1)}, bf16[27,64,256]{2,1,0:T(8,128)(2,1)}, u32[]{:S(2)}) copy-start(bf16[27,64,256]{2,1,0:T(8,128)(2,1)} %refs_7_.1) | copy-start | bytes 2654212
  3.7 37.6 %all-to-all-start = ((bf16[64,80,128]{2,1,0:T(8,128)(2,1)}), bf16[64,80,128]{2,1,0:T(8,128)(2,1)S(1)}, u32[]{:S(2)}, u32[]{:S(2)}) async-start(bf16[64,80,128]{2,1,0:T(8,128)(2,1)} %pack.1), calls=%async_computation | async-start | bytes 2621440 | tf_op jit(solution)/shard_map/all_to_all | solution.py:381
  15.3 26.0 %collective-permute-start = (bf16[27,64,256]{2,1,0:T(8,128)(2,1)S(1)}, bf16[27,64,256]{2,1,0:T(8,128)(2,1)S(1)}, u32[]{:S(2)}, u32[]{:S(2)}) collective-permute-start(bf16[27,64,256]{2,1,0:T(8,128)(2,1)S(1)} %copy-done.1), channel_id=1, source_target_pairs={{0,1},{1,0},{2,3},{3,2},{4,5},{5,4},{6,7},{7,6},{8,9},{9,8},{10,11... | collective-permute-start | bytes 2654216 | tf_op jit(solution)/shard_map/ppermute | solution.py:380
  16.2 25.1 %collective-permute-start.1 = (bf16[13,64,256]{2,1,0:T(8,128)(2,1)}, bf16[13,64,256]{2,1,0:T(8,128)(2,1)S(1)}, u32[]{:S(2)}, u32[]{:S(2)}) collective-permute-start(bf16[13,64,256]{2,1,0:T(8,128)(2,1)} %slice.6), channel_id=1, source_target_pairs={{0,2},{2,0},{1,3},{3,1},{4,6},{6,4},{5,7},{7,5},{8,10},{10,8},{9,1... | collective-permute-start | bytes 1277960 | tf_op jit(solution)/shard_map/ppermute | solution.py:378
  41.3 3.0 %collective-permute-start.2 = (bf16[64,80,128]{2,1,0:T(8,128)(2,1)S(1)}, bf16[64,80,128]{2,1,0:T(8,128)(2,1)S(1)}, u32[]{:S(2)}, u32[]{:S(2)}) collective-permute-start(bf16[64,80,128]{2,1,0:T(8,128)(2,1)S(1)} %all-to-all-done), channel_id=1, source_target_pairs={{0,1},{1,0},{2,3},{3,2},{4,5},{5,4},{6,7},{7,6},{8,9},{9,8},{10,11... | collective-permute-start | bytes 3932168 | tf_op jit(solution)/shard_map/ppermute | solution.py:404
  41.4 13.4 %collective-permute-start.3 = (bf16[14,64,256]{2,1,0:T(8,128)(2,1)S(1)}, bf16[14,64,256]{2,1,0:T(8,128)(2,1)S(1)}, u32[]{:S(2)}, u32[]{:S(2)}) collective-permute-start(bf16[14,64,256]{2,1,0:T(8,128)(2,1)S(1)} %slice.7), channel_id=1, source_target_pairs={{0,2},{2,0},{1,3},{3,1},{4,6},{6,4},{5,7},{7,5},{8,10},{10,8},{9,1... | collective-permute-start | bytes 1376264 | tf_op jit(solution)/shard_map/ppermute | solution.py:379
  44.3 10.4 %copy-start = (bf16[64,80,128]{2,1,0:T(8,128)(2,1)}, bf16[64,80,128]{2,1,0:T(8,128)(2,1)S(1)}, u32[]{:S(2)}) copy-start(bf16[64,80,128]{2,1,0:T(8,128)(2,1)S(1)} %collective-permute-done.2) | copy-start | bytes 3932164
  54.8 11.1 %collective-permute-start.8 = (bf16[14,64,256]{2,1,0:T(8,128)(2,1)S(1)}, bf16[14,64,256]{2,1,0:T(8,128)(2,1)S(1)}, u32[]{:S(2)}, u32[]{:S(2)}) collective-permute-start(bf16[14,64,256]{2,1,0:T(8,128)(2,1)S(1)} %collective-permute-done.3.refs_10_), channel_id=1, source_target_pairs={{0,1},{1,0},{2,3},{3,2},{4,5},{5,4},{6,7},{7,6},{8,9},{9,8},{10,11... | collective-permute-start | bytes 1376264 | tf_op jit(solution)/shard_map/ppermute | solution.py:427
  55.0 5.8 %collective-permute-start.7 = (bf16[13,64,256]{2,1,0:T(8,128)(2,1)S(1)}, bf16[13,64,256]{2,1,0:T(8,128)(2,1)S(1)}, u32[]{:S(2)}, u32[]{:S(2)}) collective-permute-start(bf16[13,64,256]{2,1,0:T(8,128)(2,1)S(1)} %collective-permute-done.1.refs_9_), channel_id=1, source_target_pairs={{0,1},{1,0},{2,3},{3,2},{4,5},{5,4},{6,7},{7,6},{8,9},{9,8},{10,11... | collective-permute-start | bytes 1277960 | tf_op jit(solution)/shard_map/ppermute | solution.py:428
  55.4 6.9 %collective-permute-start.4 = (bf16[8,2,16,256]{3,2,1,0:T(8,128)(2,1)S(1)}, bf16[8,2,16,256]{3,2,1,0:T(8,128)(2,1)S(1)}, u32[]{:S(2)}, u32[]{:S(2)}) collective-permute-start(bf16[8,2,16,256]{3,2,1,0:T(8,128)(2,1)S(1)} %get-tuple-element.17.refs_0_), channel_id=1, source_target_pairs={{0,4},{4,8},{8,12},{12,0},{1,5},{5,9},{9,13},{13,1},{2,6},{6,10},{... | collective-permute-start | bytes 393224 | tf_op jit(solution)/shard_map/ppermute | solution.py:407
  56.6 9.2 %collective-permute-start.5 = (bf16[8,2,16,256]{3,2,1,0:T(8,128)(2,1)S(1)}, bf16[8,2,16,256]{3,2,1,0:T(8,128)(2,1)S(1)}, u32[]{:S(2)}, u32[]{:S(2)}) collective-permute-start(bf16[8,2,16,256]{3,2,1,0:T(8,128)(2,1)S(1)} %get-tuple-element.17.refs_0_), channel_id=1, source_target_pairs={{0,8},{4,12},{8,0},{12,4},{1,9},{5,13},{9,1},{13,5},{2,10},{6,14},... | collective-permute-start | bytes 393224 | tf_op jit(solution)/shard_map/ppermute | solution.py:407
  59.4 6.5 %collective-permute-start.6 = (bf16[8,2,16,256]{3,2,1,0:T(8,128)(2,1)S(1)}, bf16[8,2,16,256]{3,2,1,0:T(8,128)(2,1)S(1)}, u32[]{:S(2)}, u32[]{:S(2)}) collective-permute-start(bf16[8,2,16,256]{3,2,1,0:T(8,128)(2,1)S(1)} %get-tuple-element.17.refs_0_), channel_id=1, source_target_pairs={{0,12},{4,0},{8,4},{12,8},{1,13},{5,1},{9,5},{13,9},{2,14},{6,2},{... | collective-permute-start | bytes 393224 | tf_op jit(solution)/shard_map/ppermute | solution.py:407
  65.8 33.7 %copy-start.3 = (bf16[1024,128]{1,0:T(8,128)(2,1)S(1)}, bf16[1024,128]{1,0:T(8,128)(2,1)}, u32[]{:S(2)}) copy-start(bf16[1024,128]{1,0:T(8,128)(2,1)} %constant.10.clone) | copy-start | bytes 786436
  65.8 33.7 %copy-start.4 = (bf16[256,1,1,128]{3,0,2,1:T(8,128)(2,1)S(1)}, bf16[256,1,1,128]{3,0,2,1:T(8,128)(2,1)}, u32[]{:S(2)}) copy-start(bf16[256,1,1,128]{3,0,2,1:T(8,128)(2,1)} %param.12) | copy-start | bytes 196612
  78.3 22.3 %copy-start.2 = (bf16[1024,128]{1,0:T(8,128)(2,1)S(1)}, bf16[1024,128]{1,0:T(8,128)(2,1)}, u32[]{:S(2)}) copy-start(bf16[1024,128]{1,0:T(8,128)(2,1)} %constant.9.clone) | copy-start | bytes 786436

commit v5 on v4

--- a/solution.py
+++ b/solution.py
@@ -21,7 +21,7 @@
 NOWS, PREVS, COTS = NOW + SHIFT, NOW - 2 + SHIFT, 8 + SHIFT
 ROWS = (32, 2 * PREVS, 2 * COTS)
 CHUNK = sum(ROWS)
-EARLY = 13
+LOWER = 13
 
 
 def window_start(b, q, l):
@@ -272,16 +272,20 @@
 
 
 def coarse_kernel_body(*refs):
-    own, mine, other, base, pieces = refs[0:4], refs[4], refs[5], refs[6], refs[7:13]
-    out, state, hidden, weights, cots, sems = refs[13:19]
+    own, base, chunks, pieces = refs[0:4], refs[4], refs[5:7], refs[7:13]
+    out, state, hidden, weights, rows, cots, sems = refs[13:20]
     b, quarter, l, core = (lax.axis_index(name) for name in AXES)
     start = 4 * (4 * b + 2 * l + core) - 1
     table = sort_table(core)
     copies = []
-    spots = ((0, 27, 0), (0, 27, 1), (0, EARLY, 2), (EARLY, 27, 2), (0, EARLY, 3), (EARLY, 27, 3))
+    spots = ((0, 27, 0), (0, 27, 1), (0, LOWER, 2), (LOWER, 27, 2), (0, LOWER, 3), (LOWER, 27, 3))
     for i, (w, (low, high, part)) in enumerate(zip(pieces, spots)):
         target = weights.at[pl.ds(low, high - low), pl.ds(64 * part, 64), :]
         copy = pltpu.make_async_copy(w, target, sems.at[i])
+        copy.start()
+        copies.append(copy)
+    for i, chunk in enumerate(chunks):
+        copy = pltpu.make_async_copy(chunk.at[:, :, pl.ds(48, 32), :], rows.at[i], sems.at[6 + i])
         copy.start()
         copies.append(copy)
     for s in range(2):
@@ -300,13 +304,15 @@
         for z in range(OWN):
             place(0, 0, 8, z0 + z, own[k][:, z].astype(F32))
 
+    for copy in copies[6:]:
+        copy.wait()
     for x in range(8):
-        parts = sorted_parts(table, mine, other, x, ROWS[0] + ROWS[1], CHUNK)
+        parts = sorted_parts(table, rows.at[0], rows.at[1], x, 8, 32)
         for z in range(COTS):
             cots[x, z] = jnp.concatenate([parts[z], parts[COTS + z]], axis=1)
         for z in range(8):
             place(1, x, 1, z, cots[x, SHIFT * core + z][None])
-    for copy in copies:
+    for copy in copies[:6]:
         copy.wait()
     taps = [(x, y, z) for x in (-1, 0, 1) for y in (-1, 0, 1) for z in (-1, 0, 1)]
 
@@ -375,8 +381,7 @@
         name="pack",
     )(fine_now, fine_prev, cotangent.reshape(256, 128))
     packed, kernel_part = lax.optimization_barrier((packed, coarse_kernel))
-    early = lax.ppermute(kernel_part[:EARLY], "l", [(0, 1), (1, 0)])
-    across = lax.ppermute(kernel_part[EARLY:], "l", [(0, 1), (1, 0)])
+    lower_part, upper_part = kernel_part[:LOWER], kernel_part[LOWER:]
     there = lax.ppermute(kernel_part, "c", [(0, 1), (1, 0)])
     mine = lax.all_to_all(packed, CHIPS, 0, 0)
     tile = np.tile(np.eye(32, dtype=np.float32), (1, 4)).astype(BF)
@@ -400,7 +405,11 @@
         tile,
     )
 
-    mine, weights, there, early = lax.optimization_barrier((mine, weights, there, early))
+    mine, weights, there, lower_part, upper_part = lax.optimization_barrier(
+        (mine, weights, there, lower_part, upper_part)
+    )
+    lower = lax.ppermute(lower_part, "l", [(0, 1), (1, 0)])
+    upper = lax.ppermute(upper_part, ("b", "l"), [(i, i ^ 9) for i in range(16)])
     other = lax.ppermute(mine, "c", [(0, 1), (1, 0)]).reshape(8, 8, CHUNK, 128)
     mine = mine.reshape(8, 8, CHUNK, 128)
     def round_ring(v):
@@ -422,33 +431,32 @@
         cost_estimate=pl.CostEstimate(flops=10**9, bytes_accessed=10**6, transcendentals=10**6),
         name="fine_layers",
     )(mine, other, weights)
-    mid, across = lax.optimization_barrier((mid, across))
+    mid, lower, upper = lax.optimization_barrier((mid, lower, upper))
     states = round_ring(mid)
-    opposite = lax.ppermute(across, "c", [(0, 1), (1, 0)])
-    early_opposite = lax.ppermute(early, "c", [(0, 1), (1, 0)])
+    far_lower = lax.ppermute(lower, "c", [(0, 1), (1, 0)])
+    far_upper = lax.ppermute(upper, "c", [(0, 1), (1, 0)])
     partial = pl.pallas_call(
         coarse_kernel_body,
         out_shape=jax.ShapeDtypeStruct((8, 16, 8, 256), BF),
-        in_specs=vmem(7) + [pl.BlockSpec(memory_space=pl.ANY)] * 6,
+        in_specs=vmem(5) + [pl.BlockSpec(memory_space=pl.ANY)] * 8,
         out_specs=pl.BlockSpec(memory_space=pltpu.VMEM),
         scratch_shapes=[
             pltpu.VMEM((2, 3, 10, 8, 16, 256), BF),
             pltpu.VMEM((2, 3, 10, 6, 16, 256), BF),
             pltpu.VMEM((27, 256, 256), BF),
+            pltpu.VMEM((2, 8, 8, 32, 128), BF),
             pltpu.VMEM((8, COTS, 16, 256), F32),
-            pltpu.SemaphoreType.DMA((6,)),
+            pltpu.SemaphoreType.DMA((8,)),
         ],
         compiler_params=pltpu.CompilerParams(vmem_limit_bytes=48 << 20),
         cost_estimate=pl.CostEstimate(flops=2 * 10**10, bytes_accessed=10**7, transcendentals=10**6),
         name="coarse_layer",
-    )(*states, mine, other, base, coarse_kernel, there, early, across, early_opposite, opposite)
+    )(*states, base, mine, other, coarse_kernel, there, lower, upper, far_lower, far_upper)
     parts = lax.all_to_all(partial.reshape(128, 8, 256), AXES, 0, 0)
     parts = parts.reshape(1024, 256)
-    table = receive_table()
-    over_rows = (((0,), (0,)), ((), ()))
-    coarse_next = lax.dot_general(parts, table[:, 0:128], over_rows, preferred_element_type=F32)
-    state_adjoint = lax.dot_general(parts, table[:, 128:256], over_rows, preferred_element_type=F32)
-    state_adjoint = state_adjoint + 2.0 * cotangent.reshape(256, 128).astype(F32)
+    sums = lax.dot_general(parts, receive_table(), (((0,), (0,)), ((), ())), preferred_element_type=F32)
+    coarse_next = sums[:, 0:128]
+    state_adjoint = sums[:, 128:256] + 2.0 * cotangent.reshape(256, 128).astype(F32)
     return coarse_next.reshape(256, 1, 1, 128), state_adjoint.reshape(256, 1, 1, 128)
 
 

time: 103 us -> 94.5 us (0.917)
  blocking collectives: 21.3 us -> 17.8 us
  starting transfers between devices: 20.1 us -> 17.5 us
  matrix products: 1.99 us -> 0.33 us
    ppermute x4, waiting for transfers between devices: 15.1 us -> 0.68 us  [the longest x1 0.67 us: local(): lax.ppermute(upper_part, ('b', 'l'), [(i, i ^ 9) for i in range(16)])]
    all_to_all x1, waiting for transfers between devices: 0.01 us -> 11.3 us  [local(): mine = lax.all_to_all(packed, CHIPS, 0, 0)]
    all_to_all x1, blocking collectives: 21.3 us -> 17.8 us  [local(): parts = lax.all_to_all(partial.reshape(128, 8, 256), AXES, 0, 0)]
    ppermute x3, waiting for transfers between devices: 5.05 us -> 8.13 us  [round_ring(): lax.ppermute(v, 'q', [(i, (i + k) % 4) for i in range(4)])]
    ppermute x3, starting transfers between devices: 5.42 us -> 3.59 us  [round_ring(): lax.ppermute(v, 'q', [(i, (i + k) % 4) for i in range(4)])]
    dot_general x2 -> x1, matrix products: 1.99 us -> 0.33 us  [local(): lax.dot_general(parts, receive_table(), (((0,), (0,)), ((), ())), preferr...]
  transfers between devices with their start and end apart: 10 -> 10, of which waited for: 4 -> 6; matrix products, arithmetic and copies ran while one was open for 3% -> 3% of each run, Pallas kernels for 16% -> 18%
where the time goes in v5:
time: 94.5 us; the launch traced here: 93.2 us
  Pallas kernels  31.6 us (33%)
  waiting for transfers between devices  21.5 us (23%)
  blocking collectives  17.8 us (19%)
  starting transfers between devices  17.5 us (19%)
  local copies, waits for them, and re-layouts  3.06 us (3%)
    all_to_all x1, blocking collectives, local(): parts = lax.all_to_all(partial.reshape(128, 8, 256), AXES, 0, 0)  17.8 us
    pallas_call x1, Pallas kernels, local(): pl.pallas_call(coarse_kernel_body, out_shape=jax.ShapeDtypeStruct((8, 16,...  11.9 us
    all_to_all x1, starting transfers between devices, local(): mine = lax.all_to_all(packed, CHIPS, 0, 0)  11.6 us
    all_to_all x1, waiting for transfers between devices, local(): mine = lax.all_to_all(packed, CHIPS, 0, 0)  11.3 us
    pallas_call x1, Pallas kernels, local(): pl.pallas_call(fine_kernel, out_shape=(jax.ShapeDtypeStruct((8, OWN, 16,...  10.4 us
    ppermute x3, waiting for transfers between devices, round_ring(): lax.ppermute(v, 'q', [(i, (i + k) % 4) for i in range(4)])  8.13 us
    pallas_call x1, Pallas kernels, local(): pl.pallas_call(weight_kernel, grid=(LAYERS,), out_shape=jax.ShapeDtypeStr...  6.22 us
    ppermute x3, starting transfers between devices, round_ring(): lax.ppermute(v, 'q', [(i, (i + k) % 4) for i in range(4)])  3.59 us
  transfers between devices with their start and end apart: 10, of which 6 were waited for; matrix products, arithmetic and copies ran while one was open for 3% of the time, Pallas kernels for 18%

profile of v5, /device:TPU:0, one launch (start us, length us, event | category | flops | bytes accessed | tf_op | source)
XLA Modules:
  0.0 93.2 jit_solution(73433246265756265)
XLA Ops:
  0.6 3.0 %pack.1 = bf16[64,80,128]{2,1,0:T(8,128)(2,1)} custom-call(f32[32,2,2,256]{3,2,1,0:T(2,128)} %now_in.1, f32[32,2,2,256]{3,2,1,0:T(2,128)} %prev_in.1, bf16[256,128]{1,0:T(8,128)(2,1)} %bitcast.26), custom_call_target="tpu_custom_call" | custom-call | tf_op jit(solution)/shard_map/pack/pallas_call | solution.py:371
  3.6 0.0 copy-start.1
  3.7 11.6 %all-to-all-start = ((bf16[64,80,128]{2,1,0:T(8,128)(2,1)}), bf16[64,80,128]{2,1,0:T(8,128)(2,1)S(1)}, u32[]{:S(2)}, u32[]{:S(2)}) async-start(bf16[64,80,128]{2,1,0:T(8,128)(2,1)} %pack.1), calls=%async_computation | async-start | bytes 2621440 | tf_op jit(solution)/shard_map/all_to_all | solution.py:386
  15.3 0.1 collective-permute-start
  15.4 0.8 slice.12
  16.2 2.2 %copy.9 = bf16[4,27,32,32]{3,2,1,0:T(8,128)(2,1)} copy(bf16[4,27,32,32]{2,3,1,0:T(8,128)(2,1)} %bitcast.23) | data formatting | bytes 442368 | tf_op jit(solution)/shard_map/transpose | solution.py:403
  18.5 6.2 %spread_weights.1.spread = bf16[4,2,8,256,256]{4,3,2,1,0:T(8,128)(2,1)} custom-call(bf16[4,864,32]{2,1,0:T(8,128)(2,1)} %bitcast.25, bf16[4,864,32]{2,1,0:T(8,128)(2,1)} %bitcast.24, bf16[32,128]{1,0:T(8,128)(2,1)} %constant.6.clone.tile), custom_call_target="tpu_custom_call" | custom-call | flops 10000000000 | bytes 10000000 | tf_op jit(solution)/shard_map/spread_weights/pallas_call | solution.py:388
  24.7 11.3 %all-to-all-done = bf16[64,80,128]{2,1,0:T(8,128)(2,1)S(1)} async-done(((bf16[64,80,128]{2,1,0:T(8,128)(2,1)}), bf16[64,80,128]{2,1,0:T(8,128)(2,1)S(1)}, u32[]{:S(2)}, u32[]{:S(2)}) %all-to-all-start) | async-done | bytes 1310752 | tf_op jit(solution)/shard_map/all_to_all | solution.py:386
  36.0 1.3 %collective-permute-start.3 = (bf16[14,64,256]{2,1,0:T(8,128)(2,1)S(1)}, bf16[14,64,256]{2,1,0:T(8,128)(2,1)S(1)}, u32[]{:S(2)}, u32[]{:S(2)}) collective-permute-start(bf16[14,64,256]{2,1,0:T(8,128)(2,1)S(1)} %slice.13), channel_id=1, source_target_pairs={{0,66},{2,64},{16,82},{18,80},{32,98},{34,96},{48,114},{50,112},{6... | collective-permute-start | bytes 1376264 | tf_op jit(solution)/shard_map/ppermute | solution.py:412
  37.3 0.5 collective-permute-start.2
  37.7 1.3 %collective-permute-done.1 = bf16[64,80,128]{2,1,0:T(8,128)(2,1)S(1)} collective-permute-done((bf16[64,80,128]{2,1,0:T(8,128)(2,1)S(1)}, bf16[64,80,128]{2,1,0:T(8,128)(2,1)S(1)}, u32[]{:S(2)}, u32[]{:S(2)}) %collective-permute-start.1) | collective-permute-done | bytes 1310752 | tf_op jit(solution)/shard_map/ppermute | solution.py:413
  39.1 10.4 %fine_layers.1 = (bf16[8,2,16,256]{3,2,1,0:T(8,128)(2,1)S(1)}, f32[8,2,16,256]{3,2,1,0:T(8,128)S(1)}) custom-call(bf16[8,8,80,128]{3,2,1,0:T(8,128)(2,1)S(1)} %bitcast.18, bf16[8,8,80,128]{3,2,1,0:T(8,128)(2,1)S(1)} %bitcast.20, bf16[4,2,8,256,256]{4,3,2,1,0:T(8,128)(2,1)} %spread_weights.1.spread), custom_call_target="tpu_custom_call" | custom-call | flops 1000000000 | bytes 1000000 | tf_op jit(solution)/shard_map/fine_layers/pallas_call | solution.py:419
  49.5 0.7 collective-permute-done.3.refs_10_
  50.2 0.5 collective-permute-start.7
  50.7 2.3 %collective-permute-start.6 = (bf16[8,2,16,256]{3,2,1,0:T(8,128)(2,1)S(1)}, bf16[8,2,16,256]{3,2,1,0:T(8,128)(2,1)S(1)}, u32[]{:S(2)}, u32[]{:S(2)}) collective-permute-start(bf16[8,2,16,256]{3,2,1,0:T(8,128)(2,1)S(1)} %get-tuple-element.21.refs_0_), channel_id=1, source_target_pairs={{0,12},{4,0},{8,4},{12,8},{1,13},{5,1},{9,5},{13,9},{2,14},{6,2},{... | collective-permute-start | bytes 393224 | tf_op jit(solution)/shard_map/ppermute | solution.py:416
  53.0 0.8 collective-permute-start.5
  53.7 0.5 collective-permute-start.4
  54.3 4.5 %collective-permute-done.6.refs_3_ = bf16[8,2,16,256]{3,2,1,0:T(8,128)(2,1)S(1)} collective-permute-done((bf16[8,2,16,256]{3,2,1,0:T(8,128)(2,1)S(1)}, bf16[8,2,16,256]{3,2,1,0:T(8,128)(2,1)S(1)}, u32[]{:S(2)}, u32[]{:S(2)}) %collective-permute-start.6) | collective-permute-done | bytes 131104 | tf_op jit(solution)/shard_map/ppermute | solution.py:416
  58.7 2.1 %collective-permute-done.5.refs_2_ = bf16[8,2,16,256]{3,2,1,0:T(8,128)(2,1)S(1)} collective-permute-done((bf16[8,2,16,256]{3,2,1,0:T(8,128)(2,1)S(1)}, bf16[8,2,16,256]{3,2,1,0:T(8,128)(2,1)S(1)}, u32[]{:S(2)}, u32[]{:S(2)}) %collective-permute-start.5) | collective-permute-done | bytes 131104 | tf_op jit(solution)/shard_map/ppermute | solution.py:416
  60.9 1.5 %collective-permute-done.4.refs_1_ = bf16[8,2,16,256]{3,2,1,0:T(8,128)(2,1)S(1)} collective-permute-done((bf16[8,2,16,256]{3,2,1,0:T(8,128)(2,1)S(1)}, bf16[8,2,16,256]{3,2,1,0:T(8,128)(2,1)S(1)}, u32[]{:S(2)}, u32[]{:S(2)}) %collective-permute-start.4) | collective-permute-done | bytes 131104 | tf_op jit(solution)/shard_map/ppermute | solution.py:416
  62.4 11.9 %coarse_layer.1 = bf16[8,16,8,256]{3,2,1,0:T(8,128)(2,1)S(1)} custom-call(bf16[8,2,16,256]{3,2,1,0:T(8,128)(2,1)S(1)} %get-tuple-element.21.refs_0_, bf16[8,2,16,256]{3,2,1,0:T(8,128)(2,1)S(1)} %collective-permute-done.4.refs_1_, bf16[8,2,16,256]{3,2,1,0:T(8,128)(2,1)S(1)} %collective-permute-done.5.refs_2_, ...), custom_call_target="tpu_custom_call" | custom-call | flops 20000000000 | bytes 10000000 | tf_op jit(solution)/shard_map/coarse_layer/pallas_call | solution.py:438
  74.4 17.8 %all_to_all.10 = bf16[128,8,256]{2,1,0:T(8,128)(2,1)S(1)} all-to-all(bf16[128,8,256]{2,1,0:T(8,128)(2,1)S(1)} %bitcast.22), channel_id=1, replica_groups=mesh['b'=8,'q'=4,'l'=2,'c'=2] {'b','q','l','c'}, dimensions={0} | all-to-all | bytes 1048576 | tf_op jit(solution)/shard_map/all_to_all | solution.py:455
  92.1 0.3 fusion
  92.5 0.7 slice_add_fusion
  (14 shorter events, 0.1 us)
Async XLA Ops:
  3.6 11.7 %copy-start.1 = (bf16[27,64,256]{2,1,0:T(8,128)(2,1)S(1)}, bf16[27,64,256]{2,1,0:T(8,128)(2,1)}, u32[]{:S(2)}) copy-start(bf16[27,64,256]{2,1,0:T(8,128)(2,1)} %refs_7_.1) | copy-start | bytes 2654212
  3.7 32.4 %all-to-all-start = ((bf16[64,80,128]{2,1,0:T(8,128)(2,1)}), bf16[64,80,128]{2,1,0:T(8,128)(2,1)S(1)}, u32[]{:S(2)}, u32[]{:S(2)}) async-start(bf16[64,80,128]{2,1,0:T(8,128)(2,1)} %pack.1), calls=%async_computation | async-start | bytes 2621440 | tf_op jit(solution)/shard_map/all_to_all | solution.py:386
  15.3 9.4 %collective-permute-start = (bf16[27,64,256]{2,1,0:T(8,128)(2,1)S(1)}, bf16[27,64,256]{2,1,0:T(8,128)(2,1)S(1)}, u32[]{:S(2)}, u32[]{:S(2)}) collective-permute-start(bf16[27,64,256]{2,1,0:T(8,128)(2,1)S(1)} %copy-done.1), channel_id=1, source_target_pairs={{0,1},{1,0},{2,3},{3,2},{4,5},{5,4},{6,7},{7,6},{8,9},{9,8},{10,11... | collective-permute-start | bytes 2654216 | tf_op jit(solution)/shard_map/ppermute | solution.py:385
  36.0 3.0 %collective-permute-start.1 = (bf16[64,80,128]{2,1,0:T(8,128)(2,1)S(1)}, bf16[64,80,128]{2,1,0:T(8,128)(2,1)S(1)}, u32[]{:S(2)}, u32[]{:S(2)}) collective-permute-start(bf16[64,80,128]{2,1,0:T(8,128)(2,1)S(1)} %all-to-all-done), channel_id=1, source_target_pairs={{0,1},{1,0},{2,3},{3,2},{4,5},{5,4},{6,7},{7,6},{8,9},{9,8},{10,11... | collective-permute-start | bytes 3932168 | tf_op jit(solution)/shard_map/ppermute | solution.py:413
  36.0 14.1 %collective-permute-start.3 = (bf16[14,64,256]{2,1,0:T(8,128)(2,1)S(1)}, bf16[14,64,256]{2,1,0:T(8,128)(2,1)S(1)}, u32[]{:S(2)}, u32[]{:S(2)}) collective-permute-start(bf16[14,64,256]{2,1,0:T(8,128)(2,1)S(1)} %slice.13), channel_id=1, source_target_pairs={{0,66},{2,64},{16,82},{18,80},{32,98},{34,96},{48,114},{50,112},{6... | collective-permute-start | bytes 1376264 | tf_op jit(solution)/shard_map/ppermute | solution.py:412
  37.3 12.2 %collective-permute-start.2 = (bf16[13,64,256]{2,1,0:T(8,128)(2,1)}, bf16[13,64,256]{2,1,0:T(8,128)(2,1)S(1)}, u32[]{:S(2)}, u32[]{:S(2)}) collective-permute-start(bf16[13,64,256]{2,1,0:T(8,128)(2,1)} %slice.12), channel_id=1, source_target_pairs={{0,2},{2,0},{1,3},{3,1},{4,6},{6,4},{5,7},{7,5},{8,10},{10,8},{9,1... | collective-permute-start | bytes 1277960 | tf_op jit(solution)/shard_map/ppermute | solution.py:411
  39.1 10.4 %copy-start = (bf16[64,80,128]{2,1,0:T(8,128)(2,1)}, bf16[64,80,128]{2,1,0:T(8,128)(2,1)S(1)}, u32[]{:S(2)}) copy-start(bf16[64,80,128]{2,1,0:T(8,128)(2,1)S(1)} %collective-permute-done.1) | copy-start | bytes 3932164
  50.2 12.2 %collective-permute-start.8 = (bf16[14,64,256]{2,1,0:T(8,128)(2,1)S(1)}, bf16[14,64,256]{2,1,0:T(8,128)(2,1)S(1)}, u32[]{:S(2)}, u32[]{:S(2)}) collective-permute-start(bf16[14,64,256]{2,1,0:T(8,128)(2,1)S(1)} %collective-permute-done.3.refs_10_), channel_id=1, source_target_pairs={{0,1},{1,0},{2,3},{3,2},{4,5},{5,4},{6,7},{7,6},{8,9},{9,8},{10,11... | collective-permute-start | bytes 1376264 | tf_op jit(solution)/shard_map/ppermute | solution.py:437
  50.2 12.2 %collective-permute-start.7 = (bf16[13,64,256]{2,1,0:T(8,128)(2,1)S(1)}, bf16[13,64,256]{2,1,0:T(8,128)(2,1)S(1)}, u32[]{:S(2)}, u32[]{:S(2)}) collective-permute-start(bf16[13,64,256]{2,1,0:T(8,128)(2,1)S(1)} %collective-permute-done.2.refs_9_), channel_id=1, source_target_pairs={{0,1},{1,0},{2,3},{3,2},{4,5},{5,4},{6,7},{7,6},{8,9},{9,8},{10,11... | collective-permute-start | bytes 1277960 | tf_op jit(solution)/shard_map/ppermute | solution.py:436
  50.7 8.0 %collective-permute-start.6 = (bf16[8,2,16,256]{3,2,1,0:T(8,128)(2,1)S(1)}, bf16[8,2,16,256]{3,2,1,0:T(8,128)(2,1)S(1)}, u32[]{:S(2)}, u32[]{:S(2)}) collective-permute-start(bf16[8,2,16,256]{3,2,1,0:T(8,128)(2,1)S(1)} %get-tuple-element.21.refs_0_), channel_id=1, source_target_pairs={{0,12},{4,0},{8,4},{12,8},{1,13},{5,1},{9,5},{13,9},{2,14},{6,2},{... | collective-permute-start | bytes 393224 | tf_op jit(solution)/shard_map/ppermute | solution.py:416
  53.0 7.9 %collective-permute-start.5 = (bf16[8,2,16,256]{3,2,1,0:T(8,128)(2,1)S(1)}, bf16[8,2,16,256]{3,2,1,0:T(8,128)(2,1)S(1)}, u32[]{:S(2)}, u32[]{:S(2)}) collective-permute-start(bf16[8,2,16,256]{3,2,1,0:T(8,128)(2,1)S(1)} %get-tuple-element.21.refs_0_), channel_id=1, source_target_pairs={{0,8},{4,12},{8,0},{12,4},{1,9},{5,13},{9,1},{13,5},{2,10},{6,14},... | collective-permute-start | bytes 393224 | tf_op jit(solution)/shard_map/ppermute | solution.py:416
  53.7 8.7 %collective-permute-start.4 = (bf16[8,2,16,256]{3,2,1,0:T(8,128)(2,1)S(1)}, bf16[8,2,16,256]{3,2,1,0:T(8,128)(2,1)S(1)}, u32[]{:S(2)}, u32[]{:S(2)}) collective-permute-start(bf16[8,2,16,256]{3,2,1,0:T(8,128)(2,1)S(1)} %get-tuple-element.21.refs_0_), channel_id=1, source_target_pairs={{0,4},{4,8},{8,12},{12,0},{1,5},{5,9},{9,13},{13,1},{2,6},{6,10},{... | collective-permute-start | bytes 393224 | tf_op jit(solution)/shard_map/ppermute | solution.py:416
  62.4 29.7 %copy-start.2 = (bf16[1024,256]{1,0:T(8,128)(2,1)S(1)}, bf16[1024,256]{1,0:T(8,128)(2,1)}, u32[]{:S(2)}) copy-start(bf16[1024,256]{1,0:T(8,128)(2,1)} %constant.7.clone) | copy-start | bytes 1572868
  74.3 18.1 %copy-start.3 = (bf16[256,1,1,128]{3,0,2,1:T(8,128)(2,1)S(1)}, bf16[256,1,1,128]{3,0,2,1:T(8,128)(2,1)}, u32[]{:S(2)}) copy-start(bf16[256,1,1,128]{3,0,2,1:T(8,128)(2,1)} %param.11) | copy-start | bytes 196612

commit v6 on v5

--- a/solution.py
+++ b/solution.py
@@ -271,90 +271,100 @@
     base[...] = (split_dot(2.0 * latest - earlier, haar) * scale).reshape(8, OWN, 16, 256)
 
 
-def coarse_kernel_body(*refs):
-    own, base, chunks, pieces = refs[0:4], refs[4], refs[5:7], refs[7:13]
-    out, state, hidden, weights, rows, cots, sems = refs[13:20]
-    b, quarter, l, core = (lax.axis_index(name) for name in AXES)
-    start = 4 * (4 * b + 2 * l + core) - 1
+TAPS = [(x, y, z) for x in (-1, 0, 1) for y in (-1, 0, 1) for z in (-1, 0, 1)]
+
+
+def place_state(state, x, xs, z, wide):
+    before, after = side_rows(wide)
+    state[0, pl.ds(x + 1, xs), z] = before.astype(BF)
+    state[1, pl.ds(x + 1, xs), z] = wide.astype(BF)
+    state[2, pl.ds(x + 1, xs), z] = after.astype(BF)
+
+
+def clear_sides(ref):
+    for y in range(3):
+        for x in (0, 9):
+            ref[y, x] = jnp.zeros(ref.shape[2:], BF)
+
+
+def coarse_forward(state, weights, x0, xs):
+    rows = xs * 96
+    total = jnp.zeros((rows, 256), F32)
+    for number, (ex, ey, ez) in enumerate(TAPS):
+        left = state[1 + ey, pl.ds(x0 + 1 + ex, xs), pl.ds(1 + ez, 6)].reshape(rows, 256)
+        total = total + dot_nt(left, weights[number])
+    return total
+
+
+def coarse_adjoint(hidden, weights, x0, xs):
+    rows = xs * 64
+    total = jnp.zeros((rows, 256), F32)
+    for number, (ex, ey, ez) in enumerate(TAPS):
+        left = hidden[1 - ey, pl.ds(x0 + 1 - ex, xs), pl.ds(1 - ez, 4)].reshape(rows, 256)
+        total = total + dot(left, weights[number])
+    return (-COARSE_STEP * total).reshape(xs, 4, 16, 256)
+
+
+def response_kernel(*refs):
+    chunks, pieces, (out, weights, state, rows, cots, sems) = refs[0:2], refs[2:8], refs[8:14]
+    core = lax.axis_index("c")
     table = sort_table(core)
     copies = []
     spots = ((0, 27, 0), (0, 27, 1), (0, LOWER, 2), (LOWER, 27, 2), (0, LOWER, 3), (LOWER, 27, 3))
+    for i, chunk in enumerate(chunks):
+        copy = pltpu.make_async_copy(chunk.at[:, :, pl.ds(48, 32), :], rows.at[i], sems.at[6 + i])
+        copy.start()
+        copies.append(copy)
     for i, (w, (low, high, part)) in enumerate(zip(pieces, spots)):
         target = weights.at[pl.ds(low, high - low), pl.ds(64 * part, 64), :]
         copy = pltpu.make_async_copy(w, target, sems.at[i])
         copy.start()
         copies.append(copy)
-    for i, chunk in enumerate(chunks):
-        copy = pltpu.make_async_copy(chunk.at[:, :, pl.ds(48, 32), :], rows.at[i], sems.at[6 + i])
-        copy.start()
-        copies.append(copy)
-    for s in range(2):
-        for y in range(3):
-            for x in (0, 9):
-                state[s, y, x] = jnp.zeros((8, 16, 256), BF)
-                hidden[s, y, x] = jnp.zeros((6, 16, 256), BF)
-    def place(s, x, xs, z, wide):
-        before, after = side_rows(wide)
-        state[s, 0, pl.ds(x + 1, xs), z] = before.astype(BF)
-        state[s, 1, pl.ds(x + 1, xs), z] = wide.astype(BF)
-        state[s, 2, pl.ds(x + 1, xs), z] = after.astype(BF)
-
-    for k in range(4):
-        z0 = OWN * ((quarter + 4 - k) % 4)
-        for z in range(OWN):
-            place(0, 0, 8, z0 + z, own[k][:, z].astype(F32))
-
-    for copy in copies[6:]:
+    clear_sides(state)
+    for copy in copies[:2]:
         copy.wait()
     for x in range(8):
         parts = sorted_parts(table, rows.at[0], rows.at[1], x, 8, 32)
         for z in range(COTS):
             cots[x, z] = jnp.concatenate([parts[z], parts[COTS + z]], axis=1)
         for z in range(8):
-            place(1, x, 1, z, cots[x, SHIFT * core + z][None])
-    for copy in copies[:6]:
+            place_state(state, x, 1, z, cots[x, SHIFT * core + z][None])
+    for copy in copies[2:]:
         copy.wait()
-    taps = [(x, y, z) for x in (-1, 0, 1) for y in (-1, 0, 1) for z in (-1, 0, 1)]
-
-    def forward(s, x0, xs):
-        rows = xs * 96
-        total = jnp.zeros((rows, 256), F32)
-        for number, (ex, ey, ez) in enumerate(taps):
-            left = state[s, 1 + ey, pl.ds(x0 + 1 + ex, xs), pl.ds(1 + ez, 6)].reshape(rows, 256)
-            total = total + dot_nt(left, weights[number])
-        return total
-
-    def adjoint(s, x0, xs):
-        rows = xs * 64
-        total = jnp.zeros((rows, 256), F32)
-        for number, (ex, ey, ez) in enumerate(taps):
-            left = hidden[s, 1 - ey, pl.ds(x0 + 1 - ex, xs), pl.ds(1 - ez, 4)].reshape(rows, 256)
-            total = total + dot(left, weights[number])
-        return (-COARSE_STEP * total).reshape(xs, 4, 16, 256)
-
-    def store(s, v, x0, xs):
+    xs = 4
+    for x0 in range(0, 8, xs):
+        out[pl.ds(96 * x0, 96 * xs)] = coarse_forward(state, weights, x0, xs)
+
+
+def coarse_kernel_body(*refs):
+    own, (base, response, weights, out, state, squashed, scaled) = refs[0:4], refs[4:11]
+    b, quarter, l, core = (lax.axis_index(name) for name in AXES)
+    start = 4 * (4 * b + 2 * l + core) - 1
+    for ref in (state, squashed, scaled):
+        clear_sides(ref)
+    for k in range(4):
+        z0 = OWN * ((quarter + 4 - k) % 4)
+        for z in range(OWN):
+            place_state(state, 0, 8, z0 + z, own[k][:, z].astype(F32))
+
+    def store(ref, v, x0, xs):
         v = v.reshape(xs, 6, 16, 256)
         for z in range(6):
             at = start + z
-            part = v[:, z] * jnp.where((at >= 0) & (at < 128), 1.0, 0.0).astype(F32)
-            before, after = side_rows(part)
-            here = (pl.ds(x0 + 1, xs), z)
-            hidden[(s, 0) + here] = before.astype(BF)
-            hidden[(s, 1) + here] = part.astype(BF)
-            hidden[(s, 2) + here] = after.astype(BF)
+            inside = jnp.where((at >= 0) & (at < 128), 1.0, 0.0).astype(F32)
+            place_state(ref, x0, xs, z, v[:, z] * inside)
 
     xs = 4
     for x0 in range(0, 8, xs):
-        squash = jnp.tanh(forward(0, x0, xs))
-        store(0, squash, x0, xs)
-        store(1, (1.0 - squash * squash) * forward(1, x0, xs), x0, xs)
+        squash = jnp.tanh(coarse_forward(state, weights, x0, xs))
+        store(squashed, squash, x0, xs)
+        store(scaled, (1.0 - squash * squash) * response[pl.ds(96 * x0, 96 * xs)], x0, xs)
     near = jnp.where(quarter == 1, 1.0, 0.0).astype(F32)
+    far = jnp.where(quarter == 2, 1.0, 0.0).astype(F32)
     back = swap_table(8, 16)
-    far = jnp.where(quarter == 2, 1.0, 0.0).astype(F32)
-    xs = 4
     for x in range(8):
         if x % xs == 0:
-            force, pull = adjoint(0, x, xs), adjoint(1, x, xs)
+            force, pull = coarse_adjoint(squashed, weights, x, xs), coarse_adjoint(scaled, weights, x, xs)
         at = x % xs
         ground = base[x]
         rows = jnp.concatenate([force[at, 0:2] + near * ground, force[at, 2:4] + far * ground, pull[at]], axis=0)
@@ -435,23 +445,31 @@
     states = round_ring(mid)
     far_lower = lax.ppermute(lower, "c", [(0, 1), (1, 0)])
     far_upper = lax.ppermute(upper, "c", [(0, 1), (1, 0)])
-    partial = pl.pallas_call(
-        coarse_kernel_body,
-        out_shape=jax.ShapeDtypeStruct((8, 16, 8, 256), BF),
-        in_specs=vmem(5) + [pl.BlockSpec(memory_space=pl.ANY)] * 8,
-        out_specs=pl.BlockSpec(memory_space=pltpu.VMEM),
+    response, gathered = pl.pallas_call(
+        response_kernel,
+        out_shape=(jax.ShapeDtypeStruct((768, 256), F32), jax.ShapeDtypeStruct((27, 256, 256), BF)),
+        in_specs=[pl.BlockSpec(memory_space=pl.ANY)] * 8,
+        out_specs=tuple(vmem(2)),
         scratch_shapes=[
-            pltpu.VMEM((2, 3, 10, 8, 16, 256), BF),
-            pltpu.VMEM((2, 3, 10, 6, 16, 256), BF),
-            pltpu.VMEM((27, 256, 256), BF),
+            pltpu.VMEM((3, 10, 8, 16, 256), BF),
             pltpu.VMEM((2, 8, 8, 32, 128), BF),
             pltpu.VMEM((8, COTS, 16, 256), F32),
             pltpu.SemaphoreType.DMA((8,)),
         ],
-        compiler_params=pltpu.CompilerParams(vmem_limit_bytes=48 << 20),
-        cost_estimate=pl.CostEstimate(flops=2 * 10**10, bytes_accessed=10**7, transcendentals=10**6),
+        compiler_params=pltpu.CompilerParams(vmem_limit_bytes=40 << 20),
+        cost_estimate=pl.CostEstimate(flops=5 * 10**9, bytes_accessed=10**7, transcendentals=0),
+        name="response",
+    )(mine, other, coarse_kernel, there, lower, upper, far_lower, far_upper)
+    partial = pl.pallas_call(
+        coarse_kernel_body,
+        out_shape=jax.ShapeDtypeStruct((8, 16, 8, 256), BF),
+        in_specs=vmem(7),
+        out_specs=pl.BlockSpec(memory_space=pltpu.VMEM),
+        scratch_shapes=[pltpu.VMEM((3, 10, 8, 16, 256), BF)] + [pltpu.VMEM((3, 10, 6, 16, 256), BF)] * 2,
+        compiler_params=pltpu.CompilerParams(vmem_limit_bytes=40 << 20),
+        cost_estimate=pl.CostEstimate(flops=10**10, bytes_accessed=10**7, transcendentals=10**6),
         name="coarse_layer",
-    )(*states, base, mine, other, coarse_kernel, there, lower, upper, far_lower, far_upper)
+    )(*states, base, response, gathered)
     parts = lax.all_to_all(partial.reshape(128, 8, 256), AXES, 0, 0)
     parts = parts.reshape(1024, 256)
     sums = lax.dot_general(parts, receive_table(), (((0,), (0,)), ((), ())), preferred_element_type=F32)

time: 94.5 us -> 89.8 us (0.950)
  waiting for transfers between devices: 21.5 us -> 17.5 us
    pallas_call x1, Pallas kernels: 11.9 us -> 7.4 us  [local(): pl.pallas_call(coarse_kernel_body, out_shape=jax.ShapeDtypeStruct((8, 16,...]
    ppermute x3, waiting for transfers between devices: 8.13 us -> 3.96 us  [round_ring(): lax.ppermute(v, 'q', [(i, (i + k) % 4) for i in range(4)])]
    pallas_call x0 -> x1, Pallas kernels: none -> 4.15 us  [local(): pl.pallas_call(response_kernel, out_shape=(jax.ShapeDtypeStruct((768, 256...]
  transfers between devices with their start and end apart: 10 -> 10, of which waited for: 6 -> 7; matrix products, arithmetic and copies ran while one was open for 3% -> 3% of each run, Pallas kernels for 18% -> 23%
where the time goes in v6:
time: 89.8 us; the launch traced here: 88.6 us
  Pallas kernels  31 us (35%)
  blocking collectives  17.7 us (20%)
  starting transfers between devices  17.5 us (19%)
  waiting for transfers between devices  17.5 us (19%)
  local copies, waits for them, and re-layouts  3.05 us (3%)
    all_to_all x1, blocking collectives, local(): parts = lax.all_to_all(partial.reshape(128, 8, 256), AXES, 0, 0)  17.7 us
    all_to_all x1, starting transfers between devices, local(): mine = lax.all_to_all(packed, CHIPS, 0, 0)  11.6 us
    all_to_all x1, waiting for transfers between devices, local(): mine = lax.all_to_all(packed, CHIPS, 0, 0)  11.4 us
    pallas_call x1, Pallas kernels, local(): pl.pallas_call(fine_kernel, out_shape=(jax.ShapeDtypeStruct((8, OWN, 16,...  10.2 us
    pallas_call x1, Pallas kernels, local(): pl.pallas_call(coarse_kernel_body, out_shape=jax.ShapeDtypeStruct((8, 16,...  7.4 us
    pallas_call x1, Pallas kernels, local(): pl.pallas_call(weight_kernel, grid=(LAYERS,), out_shape=jax.ShapeDtypeStr...  6.21 us
    pallas_call x1, Pallas kernels, local(): pl.pallas_call(response_kernel, out_shape=(jax.ShapeDtypeStruct((768, 256...  4.15 us
    ppermute x3, waiting for transfers between devices, round_ring(): lax.ppermute(v, 'q', [(i, (i + k) % 4) for i in range(4)])  3.96 us
  transfers between devices with their start and end apart: 10, of which 7 were waited for; matrix products, arithmetic and copies ran while one was open for 3% of the time, Pallas kernels for 23%

profile of v6, /device:TPU:0, one launch (start us, length us, event | category | flops | bytes accessed | tf_op | source)
XLA Modules:
  0.0 88.6 jit_solution(14975542059986658006)
XLA Ops:
  0.6 3.0 %pack.1 = bf16[64,80,128]{2,1,0:T(8,128)(2,1)} custom-call(f32[32,2,2,256]{3,2,1,0:T(2,128)} %now_in.1, f32[32,2,2,256]{3,2,1,0:T(2,128)} %prev_in.1, bf16[256,128]{1,0:T(8,128)(2,1)} %bitcast.26), custom_call_target="tpu_custom_call" | custom-call | tf_op jit(solution)/shard_map/pack/pallas_call | solution.py:381
  3.7 11.6 %all-to-all-start = ((bf16[64,80,128]{2,1,0:T(8,128)(2,1)}), bf16[64,80,128]{2,1,0:T(8,128)(2,1)S(1)}, u32[]{:S(2)}, u32[]{:S(2)}) async-start(bf16[64,80,128]{2,1,0:T(8,128)(2,1)} %pack.1), calls=%async_computation | async-start | bytes 2621440 | tf_op jit(solution)/shard_map/all_to_all | solution.py:396
  15.4 0.8 slice.12
  16.2 2.2 %copy.9 = bf16[4,27,32,32]{3,2,1,0:T(8,128)(2,1)} copy(bf16[4,27,32,32]{2,3,1,0:T(8,128)(2,1)} %bitcast.23) | data formatting | bytes 442368 | tf_op jit(solution)/shard_map/transpose | solution.py:413
  18.5 6.2 %spread_weights.1.spread = bf16[4,2,8,256,256]{4,3,2,1,0:T(8,128)(2,1)} custom-call(bf16[4,864,32]{2,1,0:T(8,128)(2,1)} %bitcast.25, bf16[4,864,32]{2,1,0:T(8,128)(2,1)} %bitcast.24, bf16[32,128]{1,0:T(8,128)(2,1)} %constant.6.clone.tile), custom_call_target="tpu_custom_call" | custom-call | flops 10000000000 | bytes 10000000 | tf_op jit(solution)/shard_map/spread_weights/pallas_call | solution.py:398
  24.7 11.4 %all-to-all-done = bf16[64,80,128]{2,1,0:T(8,128)(2,1)S(1)} async-done(((bf16[64,80,128]{2,1,0:T(8,128)(2,1)}), bf16[64,80,128]{2,1,0:T(8,128)(2,1)S(1)}, u32[]{:S(2)}, u32[]{:S(2)}) %all-to-all-start) | async-done | bytes 1310752 | tf_op jit(solution)/shard_map/all_to_all | solution.py:396
  36.0 1.3 %collective-permute-start.3 = (bf16[14,64,256]{2,1,0:T(8,128)(2,1)S(1)}, bf16[14,64,256]{2,1,0:T(8,128)(2,1)S(1)}, u32[]{:S(2)}, u32[]{:S(2)}) collective-permute-start(bf16[14,64,256]{2,1,0:T(8,128)(2,1)S(1)} %slice.13), channel_id=1, source_target_pairs={{0,66},{2,64},{16,82},{18,80},{32,98},{34,96},{48,114},{50,112},{6... | collective-permute-start | bytes 1376264 | tf_op jit(solution)/shard_map/ppermute | solution.py:422
  37.3 0.5 collective-permute-start.2
  37.7 1.3 %collective-permute-done.1 = bf16[64,80,128]{2,1,0:T(8,128)(2,1)S(1)} collective-permute-done((bf16[64,80,128]{2,1,0:T(8,128)(2,1)S(1)}, bf16[64,80,128]{2,1,0:T(8,128)(2,1)S(1)}, u32[]{:S(2)}, u32[]{:S(2)}) %collective-permute-start.1) | collective-permute-done | bytes 1310752 | tf_op jit(solution)/shard_map/ppermute | solution.py:423
  39.1 10.2 %fine_layers.1 = (bf16[8,2,16,256]{3,2,1,0:T(8,128)(2,1)S(1)}, f32[8,2,16,256]{3,2,1,0:T(8,128)S(1)}) custom-call(bf16[8,8,80,128]{3,2,1,0:T(8,128)(2,1)S(1)} %bitcast.18, bf16[8,8,80,128]{3,2,1,0:T(8,128)(2,1)S(1)} %bitcast.20, bf16[4,2,8,256,256]{4,3,2,1,0:T(8,128)(2,1)} %spread_weights.1.spread), custom_call_target="tpu_custom_call" | custom-call | flops 1000000000 | bytes 1000000 | tf_op jit(solution)/shard_map/fine_layers/pallas_call | solution.py:429
  49.3 0.1 collective-permute-done.2.refs_4_
  49.4 0.7 collective-permute-done.3.refs_5_
  50.2 0.5 collective-permute-start.7
  50.7 2.3 %collective-permute-start.6 = (bf16[8,2,16,256]{3,2,1,0:T(8,128)(2,1)S(1)}, bf16[8,2,16,256]{3,2,1,0:T(8,128)(2,1)S(1)}, u32[]{:S(2)}, u32[]{:S(2)}) collective-permute-start(bf16[8,2,16,256]{3,2,1,0:T(8,128)(2,1)S(1)} %get-tuple-element.23.refs_0_), channel_id=1, source_target_pairs={{0,12},{4,0},{8,4},{12,8},{1,13},{5,1},{9,5},{13,9},{2,14},{6,2},{... | collective-permute-start | bytes 393224 | tf_op jit(solution)/shard_map/ppermute | solution.py:426
  53.0 0.8 collective-permute-start.5
  53.7 0.5 collective-permute-start.4
  54.3 4.2 %response.1 = (f32[768,256]{1,0:T(8,128)S(1)}, bf16[27,256,256]{2,1,0:T(8,128)(2,1)S(1)}) custom-call(bf16[8,8,80,128]{3,2,1,0:T(8,128)(2,1)S(1)} %bitcast.19, bf16[8,8,80,128]{3,2,1,0:T(8,128)(2,1)S(1)} %bitcast.21, bf16[27,64,256]{2,1,0:T(8,128)(2,1)S(1)} %copy-done, bf16[27,64,256]{2,1,0:T(8,128)(2,1)S(1)} %collective-permute-done.refs_3_, ...), custom_call_target="tpu_custom_call" | custom-call | flops 5000000000 | bytes 10000000 | tf_op jit(solution)/shard_map/response/pallas_call | solution.py:448
  58.4 0.3 collective-permute-done.6.refs_3_
  58.7 2.1 %collective-permute-done.5.refs_2_ = bf16[8,2,16,256]{3,2,1,0:T(8,128)(2,1)S(1)} collective-permute-done((bf16[8,2,16,256]{3,2,1,0:T(8,128)(2,1)S(1)}, bf16[8,2,16,256]{3,2,1,0:T(8,128)(2,1)S(1)}, u32[]{:S(2)}, u32[]{:S(2)}) %collective-permute-start.5) | collective-permute-done | bytes 131104 | tf_op jit(solution)/shard_map/ppermute | solution.py:426
  60.9 1.5 %collective-permute-done.4.refs_1_ = bf16[8,2,16,256]{3,2,1,0:T(8,128)(2,1)S(1)} collective-permute-done((bf16[8,2,16,256]{3,2,1,0:T(8,128)(2,1)S(1)}, bf16[8,2,16,256]{3,2,1,0:T(8,128)(2,1)S(1)}, u32[]{:S(2)}, u32[]{:S(2)}) %collective-permute-start.4) | collective-permute-done | bytes 131104 | tf_op jit(solution)/shard_map/ppermute | solution.py:426
  62.4 7.4 %coarse_layer.1 = bf16[8,16,8,256]{3,2,1,0:T(8,128)(2,1)S(1)} custom-call(bf16[8,2,16,256]{3,2,1,0:T(8,128)(2,1)S(1)} %get-tuple-element.23.refs_0_, bf16[8,2,16,256]{3,2,1,0:T(8,128)(2,1)S(1)} %collective-permute-done.4.refs_1_, bf16[8,2,16,256]{3,2,1,0:T(8,128)(2,1)S(1)} %collective-permute-done.5.refs_2_, ...), custom_call_target="tpu_custom_call" | custom-call | flops 10000000000 | bytes 10000000 | tf_op jit(solution)/shard_map/coarse_layer/pallas_call | solution.py:463
  69.8 17.7 %all_to_all.10 = bf16[128,8,256]{2,1,0:T(8,128)(2,1)S(1)} all-to-all(bf16[128,8,256]{2,1,0:T(8,128)(2,1)S(1)} %bitcast.22), channel_id=1, replica_groups=mesh['b'=8,'q'=4,'l'=2,'c'=2] {'b','q','l','c'}, dimensions={0} | all-to-all | bytes 1048576 | tf_op jit(solution)/shard_map/all_to_all | solution.py:473
  87.5 0.3 fusion
  87.8 0.7 slice_add_fusion
  (13 shorter events, 0.1 us)
Async XLA Ops:
  3.6 11.7 %copy-start = (bf16[27,64,256]{2,1,0:T(8,128)(2,1)S(1)}, bf16[27,64,256]{2,1,0:T(8,128)(2,1)}, u32[]{:S(2)}) copy-start(bf16[27,64,256]{2,1,0:T(8,128)(2,1)} %refs_2_.1) | copy-start | bytes 2654212
  3.7 32.4 %all-to-all-start = ((bf16[64,80,128]{2,1,0:T(8,128)(2,1)}), bf16[64,80,128]{2,1,0:T(8,128)(2,1)S(1)}, u32[]{:S(2)}, u32[]{:S(2)}) async-start(bf16[64,80,128]{2,1,0:T(8,128)(2,1)} %pack.1), calls=%async_computation | async-start | bytes 2621440 | tf_op jit(solution)/shard_map/all_to_all | solution.py:396
  15.3 9.3 %collective-permute-start = (bf16[27,64,256]{2,1,0:T(8,128)(2,1)S(1)}, bf16[27,64,256]{2,1,0:T(8,128)(2,1)S(1)}, u32[]{:S(2)}, u32[]{:S(2)}) collective-permute-start(bf16[27,64,256]{2,1,0:T(8,128)(2,1)S(1)} %copy-done), channel_id=1, source_target_pairs={{0,1},{1,0},{2,3},{3,2},{4,5},{5,4},{6,7},{7,6},{8,9},{9,8},{10,11... | collective-permute-start | bytes 2654216 | tf_op jit(solution)/shard_map/ppermute | solution.py:395
  36.0 3.0 %collective-permute-start.1 = (bf16[64,80,128]{2,1,0:T(8,128)(2,1)S(1)}, bf16[64,80,128]{2,1,0:T(8,128)(2,1)S(1)}, u32[]{:S(2)}, u32[]{:S(2)}) collective-permute-start(bf16[64,80,128]{2,1,0:T(8,128)(2,1)S(1)} %all-to-all-done), channel_id=1, source_target_pairs={{0,1},{1,0},{2,3},{3,2},{4,5},{5,4},{6,7},{7,6},{8,9},{9,8},{10,11... | collective-permute-start | bytes 3932168 | tf_op jit(solution)/shard_map/ppermute | solution.py:423
  36.0 14.1 %collective-permute-start.3 = (bf16[14,64,256]{2,1,0:T(8,128)(2,1)S(1)}, bf16[14,64,256]{2,1,0:T(8,128)(2,1)S(1)}, u32[]{:S(2)}, u32[]{:S(2)}) collective-permute-start(bf16[14,64,256]{2,1,0:T(8,128)(2,1)S(1)} %slice.13), channel_id=1, source_target_pairs={{0,66},{2,64},{16,82},{18,80},{32,98},{34,96},{48,114},{50,112},{6... | collective-permute-start | bytes 1376264 | tf_op jit(solution)/shard_map/ppermute | solution.py:422
  37.3 12.2 %collective-permute-start.2 = (bf16[13,64,256]{2,1,0:T(8,128)(2,1)}, bf16[13,64,256]{2,1,0:T(8,128)(2,1)S(1)}, u32[]{:S(2)}, u32[]{:S(2)}) collective-permute-start(bf16[13,64,256]{2,1,0:T(8,128)(2,1)} %slice.12), channel_id=1, source_target_pairs={{0,2},{2,0},{1,3},{3,1},{4,6},{6,4},{5,7},{7,5},{8,10},{10,8},{9,1... | collective-permute-start | bytes 1277960 | tf_op jit(solution)/shard_map/ppermute | solution.py:421
  50.2 4.1 %collective-permute-start.8 = (bf16[14,64,256]{2,1,0:T(8,128)(2,1)S(1)}, bf16[14,64,256]{2,1,0:T(8,128)(2,1)S(1)}, u32[]{:S(2)}, u32[]{:S(2)}) collective-permute-start(bf16[14,64,256]{2,1,0:T(8,128)(2,1)S(1)} %collective-permute-done.3.refs_5_), channel_id=1, source_target_pairs={{0,1},{1,0},{2,3},{3,2},{4,5},{5,4},{6,7},{7,6},{8,9},{9,8},{10,11... | collective-permute-start | bytes 1376264 | tf_op jit(solution)/shard_map/ppermute | solution.py:447
  50.2 4.1 %collective-permute-start.7 = (bf16[13,64,256]{2,1,0:T(8,128)(2,1)S(1)}, bf16[13,64,256]{2,1,0:T(8,128)(2,1)S(1)}, u32[]{:S(2)}, u32[]{:S(2)}) collective-permute-start(bf16[13,64,256]{2,1,0:T(8,128)(2,1)S(1)} %collective-permute-done.2.refs_4_), channel_id=1, source_target_pairs={{0,1},{1,0},{2,3},{3,2},{4,5},{5,4},{6,7},{7,6},{8,9},{9,8},{10,11... | collective-permute-start | bytes 1277960 | tf_op jit(solution)/shard_map/ppermute | solution.py:446
  50.7 8.0 %collective-permute-start.6 = (bf16[8,2,16,256]{3,2,1,0:T(8,128)(2,1)S(1)}, bf16[8,2,16,256]{3,2,1,0:T(8,128)(2,1)S(1)}, u32[]{:S(2)}, u32[]{:S(2)}) collective-permute-start(bf16[8,2,16,256]{3,2,1,0:T(8,128)(2,1)S(1)} %get-tuple-element.23.refs_0_), channel_id=1, source_target_pairs={{0,12},{4,0},{8,4},{12,8},{1,13},{5,1},{9,5},{13,9},{2,14},{6,2},{... | collective-permute-start | bytes 393224 | tf_op jit(solution)/shard_map/ppermute | solution.py:426
  53.0 7.9 %collective-permute-start.5 = (bf16[8,2,16,256]{3,2,1,0:T(8,128)(2,1)S(1)}, bf16[8,2,16,256]{3,2,1,0:T(8,128)(2,1)S(1)}, u32[]{:S(2)}, u32[]{:S(2)}) collective-permute-start(bf16[8,2,16,256]{3,2,1,0:T(8,128)(2,1)S(1)} %get-tuple-element.23.refs_0_), channel_id=1, source_target_pairs={{0,8},{4,12},{8,0},{12,4},{1,9},{5,13},{9,1},{13,5},{2,10},{6,14},... | collective-permute-start | bytes 393224 | tf_op jit(solution)/shard_map/ppermute | solution.py:426
  53.7 8.7 %collective-permute-start.4 = (bf16[8,2,16,256]{3,2,1,0:T(8,128)(2,1)S(1)}, bf16[8,2,16,256]{3,2,1,0:T(8,128)(2,1)S(1)}, u32[]{:S(2)}, u32[]{:S(2)}) collective-permute-start(bf16[8,2,16,256]{3,2,1,0:T(8,128)(2,1)S(1)} %get-tuple-element.23.refs_0_), channel_id=1, source_target_pairs={{0,4},{4,8},{8,12},{12,0},{1,5},{5,9},{9,13},{13,1},{2,6},{6,10},{... | collective-permute-start | bytes 393224 | tf_op jit(solution)/shard_map/ppermute | solution.py:426
  62.4 25.1 %copy-start.1 = (bf16[1024,256]{1,0:T(8,128)(2,1)S(1)}, bf16[1024,256]{1,0:T(8,128)(2,1)}, u32[]{:S(2)}) copy-start(bf16[1024,256]{1,0:T(8,128)(2,1)} %constant.7.clone) | copy-start | bytes 1572868
  69.8 18.0 %copy-start.2 = (bf16[256,1,1,128]{3,0,2,1:T(8,128)(2,1)S(1)}, bf16[256,1,1,128]{3,0,2,1:T(8,128)(2,1)}, u32[]{:S(2)}) copy-start(bf16[256,1,1,128]{3,0,2,1:T(8,128)(2,1)} %param.11) | copy-start | bytes 196612

commit v7 on v6

--- a/solution.py
+++ b/solution.py
@@ -21,7 +21,6 @@
 NOWS, PREVS, COTS = NOW + SHIFT, NOW - 2 + SHIFT, 8 + SHIFT
 ROWS = (32, 2 * PREVS, 2 * COTS)
 CHUNK = sum(ROWS)
-LOWER = 13
 
 
 def window_start(b, q, l):
@@ -65,7 +64,7 @@
     return jnp.concatenate([ref[:, a, b, :] for a in range(2) for b in range(2)], axis=0)
 
 
-def pack_kernel(now_in, prev_in, cot_in, out, now, prev, cot, first, second, third, sems):
+def pack_kernel(now_in, prev_in, cot_in, out, now, prev, cot, first, second, third, packed, sems):
     copies = []
     for i, (source, target) in enumerate(((now_in, now), (prev_in, prev), (cot_in, cot))):
         copy = pltpu.make_async_copy(source, target, sems.at[i])
@@ -95,7 +94,12 @@
         groups = []
         for table, size, rows in zip((first, second, third), ROWS, (now_rows, prev_rows, cot_rows)):
             groups.append(dot_nt(table[pl.ds(size * t, size * part), :], rows).reshape(part, size, 128))
-        out[pl.ds(t, part)] = jnp.concatenate(groups, axis=1).astype(BF)
+        packed[pl.ds(t, part)] = jnp.concatenate(groups, axis=1).astype(BF)
+        copy = pltpu.make_async_copy(packed.at[pl.ds(t, part)], out.at[pl.ds(t, part)], sems.at[3 + t // part])
+        copy.start()
+        copies.append(copy)
+    for copy in copies[3:]:
+        copy.wait()
 
 
 def sort_table(core):
@@ -306,18 +310,16 @@
 
 
 def response_kernel(*refs):
-    chunks, pieces, (out, weights, state, rows, cots, sems) = refs[0:2], refs[2:8], refs[8:14]
+    chunks, pieces, (out, weights, state, rows, cots, sems) = refs[0:2], refs[2:6], refs[6:12]
     core = lax.axis_index("c")
     table = sort_table(core)
     copies = []
-    spots = ((0, 27, 0), (0, 27, 1), (0, LOWER, 2), (LOWER, 27, 2), (0, LOWER, 3), (LOWER, 27, 3))
     for i, chunk in enumerate(chunks):
-        copy = pltpu.make_async_copy(chunk.at[:, :, pl.ds(48, 32), :], rows.at[i], sems.at[6 + i])
+        copy = pltpu.make_async_copy(chunk.at[:, :, pl.ds(48, 32), :], rows.at[i], sems.at[4 + i])
         copy.start()
         copies.append(copy)
-    for i, (w, (low, high, part)) in enumerate(zip(pieces, spots)):
-        target = weights.at[pl.ds(low, high - low), pl.ds(64 * part, 64), :]
-        copy = pltpu.make_async_copy(w, target, sems.at[i])
+    for i, w in enumerate(pieces):
+        copy = pltpu.make_async_copy(w, weights.at[:, pl.ds(64 * i, 64), :], sems.at[i])
         copy.start()
         copies.append(copy)
     clear_sides(state)
@@ -382,16 +384,15 @@
         pack_kernel,
         out_shape=jax.ShapeDtypeStruct((64, CHUNK, 128), BF),
         in_specs=[pl.BlockSpec(memory_space=pltpu.HBM)] * 3,
-        out_specs=pl.BlockSpec(memory_space=pltpu.VMEM),
+        out_specs=pl.BlockSpec(memory_space=pltpu.HBM),
         scratch_shapes=[pltpu.VMEM((32, 2, 2, 256), F32)] * 2
         + [pltpu.VMEM((256, 128), BF)]
         + [pltpu.VMEM((64 * size, 256), BF) for size in ROWS]
-        + [pltpu.SemaphoreType.DMA((3,))],
+        + [pltpu.VMEM((64, CHUNK, 128), BF), pltpu.SemaphoreType.DMA((7,))],
         compiler_params=pltpu.CompilerParams(vmem_limit_bytes=60 << 20),
         name="pack",
     )(fine_now, fine_prev, cotangent.reshape(256, 128))
     packed, kernel_part = lax.optimization_barrier((packed, coarse_kernel))
-    lower_part, upper_part = kernel_part[:LOWER], kernel_part[LOWER:]
     there = lax.ppermute(kernel_part, "c", [(0, 1), (1, 0)])
     mine = lax.all_to_all(packed, CHIPS, 0, 0)
     tile = np.tile(np.eye(32, dtype=np.float32), (1, 4)).astype(BF)
@@ -415,11 +416,8 @@
         tile,
     )
 
-    mine, weights, there, lower_part, upper_part = lax.optimization_barrier(
-        (mine, weights, there, lower_part, upper_part)
-    )
-    lower = lax.ppermute(lower_part, "l", [(0, 1), (1, 0)])
-    upper = lax.ppermute(upper_part, ("b", "l"), [(i, i ^ 9) for i in range(16)])
+    mine, weights, there, kernel_part = lax.optimization_barrier((mine, weights, there, kernel_part))
+    across = lax.ppermute(kernel_part, ("b", "l", "c"), [(i, i ^ (18 if i % 2 else 2)) for i in range(32)])
     other = lax.ppermute(mine, "c", [(0, 1), (1, 0)]).reshape(8, 8, CHUNK, 128)
     mine = mine.reshape(8, 8, CHUNK, 128)
     def round_ring(v):
@@ -441,25 +439,24 @@
         cost_estimate=pl.CostEstimate(flops=10**9, bytes_accessed=10**6, transcendentals=10**6),
         name="fine_layers",
     )(mine, other, weights)
-    mid, lower, upper = lax.optimization_barrier((mid, lower, upper))
+    mid, across = lax.optimization_barrier((mid, across))
     states = round_ring(mid)
-    far_lower = lax.ppermute(lower, "c", [(0, 1), (1, 0)])
-    far_upper = lax.ppermute(upper, "c", [(0, 1), (1, 0)])
+    opposite = lax.ppermute(across, "c", [(0, 1), (1, 0)])
     response, gathered = pl.pallas_call(
         response_kernel,
         out_shape=(jax.ShapeDtypeStruct((768, 256), F32), jax.ShapeDtypeStruct((27, 256, 256), BF)),
-        in_specs=[pl.BlockSpec(memory_space=pl.ANY)] * 8,
+        in_specs=[pl.BlockSpec(memory_space=pl.ANY)] * 6,
         out_specs=tuple(vmem(2)),
         scratch_shapes=[
             pltpu.VMEM((3, 10, 8, 16, 256), BF),
             pltpu.VMEM((2, 8, 8, 32, 128), BF),
             pltpu.VMEM((8, COTS, 16, 256), F32),
-            pltpu.SemaphoreType.DMA((8,)),
+            pltpu.SemaphoreType.DMA((6,)),
         ],
         compiler_params=pltpu.CompilerParams(vmem_limit_bytes=40 << 20),
         cost_estimate=pl.CostEstimate(flops=5 * 10**9, bytes_accessed=10**7, transcendentals=0),
         name="response",
-    )(mine, other, coarse_kernel, there, lower, upper, far_lower, far_upper)
+    )(mine, other, coarse_kernel, there, across, opposite)
     partial = pl.pallas_call(
         coarse_kernel_body,
         out_shape=jax.ShapeDtypeStruct((8, 16, 8, 256), BF),

time: 89.8 us -> 88.6 us (0.987)
  blocking collectives: 17.7 us -> 19.3 us
  waiting for transfers between devices: 17.5 us -> 16 us
    ppermute x3, waiting for transfers between devices: 3.96 us -> 1.24 us  [round_ring(): lax.ppermute(v, 'q', [(i, (i + k) % 4) for i in range(4)])]
    all_to_all x1, blocking collectives: 17.7 us -> 19.3 us  [local(): parts = lax.all_to_all(partial.reshape(128, 8, 256), AXES, 0, 0)]
    ppermute x4 -> x2, starting transfers between devices: 2.23 us -> 0.75 us  [the longest x1 0.42 us: local(): lax.ppermute(kernel_part, ('b', 'l', 'c'), [(i, i ^ (18 if i % 2 else 2))...]
    ppermute x1, waiting for transfers between devices: 1.32 us -> 2.61 us  [local(): other = lax.ppermute(mine, 'c', [(0, 1), (1, 0)]).reshape(8, 8, CHUNK, 128)]
    ppermute x3, starting transfers between devices: 3.59 us -> 4.8 us  [round_ring(): lax.ppermute(v, 'q', [(i, (i + k) % 4) for i in range(4)])]
  transfers between devices with their start and end apart: 10 -> 8, of which waited for: 7 -> 4; matrix products, arithmetic and copies ran while one was open for 3% -> 3% of each run, Pallas kernels for 23% -> 24%
where the time goes in v7:
time: 88.6 us; the launch traced here: 87.4 us
  Pallas kernels  30.7 us (35%)
  blocking collectives  19.3 us (22%)
  starting transfers between devices  17.3 us (20%)
  waiting for transfers between devices  16 us (18%)
  local copies, waits for them, and re-layouts  2.22 us (3%)
    all_to_all x1, blocking collectives, local(): parts = lax.all_to_all(partial.reshape(128, 8, 256), AXES, 0, 0)  19.3 us
    all_to_all x1, waiting for transfers between devices, local(): mine = lax.all_to_all(packed, CHIPS, 0, 0)  12.2 us
    all_to_all x1, starting transfers between devices, local(): mine = lax.all_to_all(packed, CHIPS, 0, 0)  11.6 us
    pallas_call x1, Pallas kernels, local(): pl.pallas_call(fine_kernel, out_shape=(jax.ShapeDtypeStruct((8, OWN, 16,...  10.2 us
    pallas_call x1, Pallas kernels, local(): pl.pallas_call(coarse_kernel_body, out_shape=jax.ShapeDtypeStruct((8, 16,...  7.4 us
    pallas_call x1, Pallas kernels, local(): pl.pallas_call(weight_kernel, grid=(LAYERS,), out_shape=jax.ShapeDtypeStr...  6.21 us
    ppermute x3, starting transfers between devices, round_ring(): lax.ppermute(v, 'q', [(i, (i + k) % 4) for i in range(4)])  4.8 us
    pallas_call x1, Pallas kernels, local(): pl.pallas_call(response_kernel, out_shape=(jax.ShapeDtypeStruct((768, 256...  4.2 us
  transfers between devices with their start and end apart: 8, of which 4 were waited for; matrix products, arithmetic and copies ran while one was open for 3% of the time, Pallas kernels for 24%

profile of v7, /device:TPU:0, one launch (start us, length us, event | category | flops | bytes accessed | tf_op | source)
XLA Modules:
  0.0 87.4 jit_solution(17915598164988194028)
XLA Ops:
  0.6 2.7 %pack.1 = bf16[64,80,128]{2,1,0:T(8,128)(2,1)} custom-call(f32[32,2,2,256]{3,2,1,0:T(2,128)} %now_in.1, f32[32,2,2,256]{3,2,1,0:T(2,128)} %prev_in.1, bf16[256,128]{1,0:T(8,128)(2,1)} %bitcast.26), custom_call_target="tpu_custom_call" | custom-call | tf_op jit(solution)/shard_map/pack/pallas_call | solution.py:383
  3.3 0.0 copy-start
  3.3 11.6 %all-to-all-start = ((bf16[64,80,128]{2,1,0:T(8,128)(2,1)}), bf16[64,80,128]{2,1,0:T(8,128)(2,1)S(1)}, u32[]{:S(2)}, u32[]{:S(2)}) async-start(bf16[64,80,128]{2,1,0:T(8,128)(2,1)} %pack.1), calls=%async_computation | async-start | bytes 2621440 | tf_op jit(solution)/shard_map/all_to_all | solution.py:397
  15.0 0.1 collective-permute-start
  15.1 2.2 %copy.9 = bf16[4,27,32,32]{3,2,1,0:T(8,128)(2,1)} copy(bf16[4,27,32,32]{2,3,1,0:T(8,128)(2,1)} %bitcast.23) | data formatting | bytes 442368 | tf_op jit(solution)/shard_map/transpose | solution.py:414
  17.3 6.2 %spread_weights.1.spread = bf16[4,2,8,256,256]{4,3,2,1,0:T(8,128)(2,1)} custom-call(bf16[4,864,32]{2,1,0:T(8,128)(2,1)} %bitcast.25, bf16[4,864,32]{2,1,0:T(8,128)(2,1)} %bitcast.24, bf16[32,128]{1,0:T(8,128)(2,1)} %constant.6.clone.tile), custom_call_target="tpu_custom_call" | custom-call | flops 10000000000 | bytes 10000000 | tf_op jit(solution)/shard_map/spread_weights/pallas_call | solution.py:399
  23.5 0.0 collective-permute-done.refs_3_
  23.5 12.2 %all-to-all-done = bf16[64,80,128]{2,1,0:T(8,128)(2,1)S(1)} async-done(((bf16[64,80,128]{2,1,0:T(8,128)(2,1)}), bf16[64,80,128]{2,1,0:T(8,128)(2,1)S(1)}, u32[]{:S(2)}, u32[]{:S(2)}) %all-to-all-start) | async-done | bytes 1310752 | tf_op jit(solution)/shard_map/all_to_all | solution.py:397
  35.7 0.4 collective-permute-start.2
  36.1 2.6 %collective-permute-done.1 = bf16[64,80,128]{2,1,0:T(8,128)(2,1)S(1)} collective-permute-done((bf16[64,80,128]{2,1,0:T(8,128)(2,1)S(1)}, bf16[64,80,128]{2,1,0:T(8,128)(2,1)S(1)}, u32[]{:S(2)}, u32[]{:S(2)}) %collective-permute-start.1) | collective-permute-done | bytes 1310752 | tf_op jit(solution)/shard_map/ppermute | solution.py:421
  38.7 10.2 %fine_layers.1 = (bf16[8,2,16,256]{3,2,1,0:T(8,128)(2,1)S(1)}, f32[8,2,16,256]{3,2,1,0:T(8,128)S(1)}) custom-call(bf16[8,8,80,128]{3,2,1,0:T(8,128)(2,1)S(1)} %bitcast.18, bf16[8,8,80,128]{3,2,1,0:T(8,128)(2,1)S(1)} %bitcast.20, bf16[4,2,8,256,256]{4,3,2,1,0:T(8,128)(2,1)} %spread_weights.1.spread), custom_call_target="tpu_custom_call" | custom-call | flops 1000000000 | bytes 1000000 | tf_op jit(solution)/shard_map/fine_layers/pallas_call | solution.py:427
  48.9 0.0 collective-permute-done.2.refs_4_
  49.0 0.3 collective-permute-start.6
  49.3 1.0 %collective-permute-start.3 = (bf16[8,2,16,256]{3,2,1,0:T(8,128)(2,1)S(1)}, bf16[8,2,16,256]{3,2,1,0:T(8,128)(2,1)S(1)}, u32[]{:S(2)}, u32[]{:S(2)}) collective-permute-start(bf16[8,2,16,256]{3,2,1,0:T(8,128)(2,1)S(1)} %get-tuple-element.20.refs_0_), channel_id=1, source_target_pairs={{0,4},{4,8},{8,12},{12,0},{1,5},{5,9},{9,13},{13,1},{2,6},{6,10},{... | collective-permute-start | bytes 393224 | tf_op jit(solution)/shard_map/ppermute | solution.py:424
  50.3 2.8 %collective-permute-start.4 = (bf16[8,2,16,256]{3,2,1,0:T(8,128)(2,1)S(1)}, bf16[8,2,16,256]{3,2,1,0:T(8,128)(2,1)S(1)}, u32[]{:S(2)}, u32[]{:S(2)}) collective-permute-start(bf16[8,2,16,256]{3,2,1,0:T(8,128)(2,1)S(1)} %get-tuple-element.20.refs_0_), channel_id=1, source_target_pairs={{0,8},{4,12},{8,0},{12,4},{1,9},{5,13},{9,1},{13,5},{2,10},{6,14},... | collective-permute-start | bytes 393224 | tf_op jit(solution)/shard_map/ppermute | solution.py:424
  53.0 1.1 %collective-permute-start.5 = (bf16[8,2,16,256]{3,2,1,0:T(8,128)(2,1)S(1)}, bf16[8,2,16,256]{3,2,1,0:T(8,128)(2,1)S(1)}, u32[]{:S(2)}, u32[]{:S(2)}) collective-permute-start(bf16[8,2,16,256]{3,2,1,0:T(8,128)(2,1)S(1)} %get-tuple-element.20.refs_0_), channel_id=1, source_target_pairs={{0,12},{4,0},{8,4},{12,8},{1,13},{5,1},{9,5},{13,9},{2,14},{6,2},{... | collective-permute-start | bytes 393224 | tf_op jit(solution)/shard_map/ppermute | solution.py:424
  54.1 4.2 %response.1 = (f32[768,256]{1,0:T(8,128)S(1)}, bf16[27,256,256]{2,1,0:T(8,128)(2,1)S(1)}) custom-call(bf16[8,8,80,128]{3,2,1,0:T(8,128)(2,1)S(1)} %bitcast.19, bf16[8,8,80,128]{3,2,1,0:T(8,128)(2,1)S(1)} %bitcast.21, bf16[27,64,256]{2,1,0:T(8,128)(2,1)S(1)} %copy-done, bf16[27,64,256]{2,1,0:T(8,128)(2,1)S(1)} %collective-permute-done.refs_3_, ...), custom_call_target="tpu_custom_call" | custom-call | flops 5000000000 | bytes 10000000 | tf_op jit(solution)/shard_map/response/pallas_call | solution.py:445
  58.3 1.2 %collective-permute-done.4.refs_2_ = bf16[8,2,16,256]{3,2,1,0:T(8,128)(2,1)S(1)} collective-permute-done((bf16[8,2,16,256]{3,2,1,0:T(8,128)(2,1)S(1)}, bf16[8,2,16,256]{3,2,1,0:T(8,128)(2,1)S(1)}, u32[]{:S(2)}, u32[]{:S(2)}) %collective-permute-start.4) | collective-permute-done | bytes 131104 | tf_op jit(solution)/shard_map/ppermute | solution.py:424
  59.5 0.1 collective-permute-done.5.refs_3_
  59.5 7.4 %coarse_layer.1 = bf16[8,16,8,256]{3,2,1,0:T(8,128)(2,1)S(1)} custom-call(bf16[8,2,16,256]{3,2,1,0:T(8,128)(2,1)S(1)} %get-tuple-element.20.refs_0_, bf16[8,2,16,256]{3,2,1,0:T(8,128)(2,1)S(1)} %collective-permute-done.3.refs_1_, bf16[8,2,16,256]{3,2,1,0:T(8,128)(2,1)S(1)} %collective-permute-done.4.refs_2_, ...), custom_call_target="tpu_custom_call" | custom-call | flops 10000000000 | bytes 10000000 | tf_op jit(solution)/shard_map/coarse_layer/pallas_call | solution.py:460
  67.0 0.0 copy-start.2
  67.0 19.3 %all_to_all.10 = bf16[128,8,256]{2,1,0:T(8,128)(2,1)S(1)} all-to-all(bf16[128,8,256]{2,1,0:T(8,128)(2,1)S(1)} %bitcast.22), channel_id=1, replica_groups=mesh['b'=8,'q'=4,'l'=2,'c'=2] {'b','q','l','c'}, dimensions={0} | all-to-all | bytes 1048576 | tf_op jit(solution)/shard_map/all_to_all | solution.py:470
  86.3 0.3 fusion
  86.6 0.7 slice_add_fusion
  (7 shorter events, 0.0 us)
Async XLA Ops:
  3.3 11.7 %copy-start = (bf16[27,64,256]{2,1,0:T(8,128)(2,1)S(1)}, bf16[27,64,256]{2,1,0:T(8,128)(2,1)}, u32[]{:S(2)}) copy-start(bf16[27,64,256]{2,1,0:T(8,128)(2,1)} %refs_2_.1) | copy-start | bytes 2654212
  3.3 32.4 %all-to-all-start = ((bf16[64,80,128]{2,1,0:T(8,128)(2,1)}), bf16[64,80,128]{2,1,0:T(8,128)(2,1)S(1)}, u32[]{:S(2)}, u32[]{:S(2)}) async-start(bf16[64,80,128]{2,1,0:T(8,128)(2,1)} %pack.1), calls=%async_computation | async-start | bytes 2621440 | tf_op jit(solution)/shard_map/all_to_all | solution.py:397
  15.0 8.5 %collective-permute-start = (bf16[27,64,256]{2,1,0:T(8,128)(2,1)S(1)}, bf16[27,64,256]{2,1,0:T(8,128)(2,1)S(1)}, u32[]{:S(2)}, u32[]{:S(2)}) collective-permute-start(bf16[27,64,256]{2,1,0:T(8,128)(2,1)S(1)} %copy-done), channel_id=1, source_target_pairs={{0,1},{1,0},{2,3},{3,2},{4,5},{5,4},{6,7},{7,6},{8,9},{9,8},{10,11... | collective-permute-start | bytes 2654216 | tf_op jit(solution)/shard_map/ppermute | solution.py:396
  35.7 3.0 %collective-permute-start.1 = (bf16[64,80,128]{2,1,0:T(8,128)(2,1)S(1)}, bf16[64,80,128]{2,1,0:T(8,128)(2,1)S(1)}, u32[]{:S(2)}, u32[]{:S(2)}) collective-permute-start(bf16[64,80,128]{2,1,0:T(8,128)(2,1)S(1)} %all-to-all-done), channel_id=1, source_target_pairs={{0,1},{1,0},{2,3},{3,2},{4,5},{5,4},{6,7},{7,6},{8,9},{9,8},{10,11... | collective-permute-start | bytes 3932168 | tf_op jit(solution)/shard_map/ppermute | solution.py:421
  35.7 13.3 %collective-permute-start.2 = (bf16[27,64,256]{2,1,0:T(8,128)(2,1)S(1)}, bf16[27,64,256]{2,1,0:T(8,128)(2,1)S(1)}, u32[]{:S(2)}, u32[]{:S(2)}) collective-permute-start(bf16[27,64,256]{2,1,0:T(8,128)(2,1)S(1)} %copy-done), channel_id=1, source_target_pairs={{0,2},{1,67},{2,0},{3,65},{16,18},{17,83},{18,16},{19,81},{32,34},... | collective-permute-start | bytes 2654216 | tf_op jit(solution)/shard_map/ppermute | solution.py:420
  49.0 5.1 %collective-permute-start.6 = (bf16[27,64,256]{2,1,0:T(8,128)(2,1)S(1)}, bf16[27,64,256]{2,1,0:T(8,128)(2,1)S(1)}, u32[]{:S(2)}, u32[]{:S(2)}) collective-permute-start(bf16[27,64,256]{2,1,0:T(8,128)(2,1)S(1)} %collective-permute-done.2.refs_4_), channel_id=1, source_target_pairs={{0,1},{1,0},{2,3},{3,2},{4,5},{5,4},{6,7},{7,6},{8,9},{9,8},{10,11... | collective-permute-start | bytes 2654216 | tf_op jit(solution)/shard_map/ppermute | solution.py:444
  49.3 9.0 %collective-permute-start.3 = (bf16[8,2,16,256]{3,2,1,0:T(8,128)(2,1)S(1)}, bf16[8,2,16,256]{3,2,1,0:T(8,128)(2,1)S(1)}, u32[]{:S(2)}, u32[]{:S(2)}) collective-permute-start(bf16[8,2,16,256]{3,2,1,0:T(8,128)(2,1)S(1)} %get-tuple-element.20.refs_0_), channel_id=1, source_target_pairs={{0,4},{4,8},{8,12},{12,0},{1,5},{5,9},{9,13},{13,1},{2,6},{6,10},{... | collective-permute-start | bytes 393224 | tf_op jit(solution)/shard_map/ppermute | solution.py:424
  50.3 9.2 %collective-permute-start.4 = (bf16[8,2,16,256]{3,2,1,0:T(8,128)(2,1)S(1)}, bf16[8,2,16,256]{3,2,1,0:T(8,128)(2,1)S(1)}, u32[]{:S(2)}, u32[]{:S(2)}) collective-permute-start(bf16[8,2,16,256]{3,2,1,0:T(8,128)(2,1)S(1)} %get-tuple-element.20.refs_0_), channel_id=1, source_target_pairs={{0,8},{4,12},{8,0},{12,4},{1,9},{5,13},{9,1},{13,5},{2,10},{6,14},... | collective-permute-start | bytes 393224 | tf_op jit(solution)/shard_map/ppermute | solution.py:424
  53.0 6.5 %collective-permute-start.5 = (bf16[8,2,16,256]{3,2,1,0:T(8,128)(2,1)S(1)}, bf16[8,2,16,256]{3,2,1,0:T(8,128)(2,1)S(1)}, u32[]{:S(2)}, u32[]{:S(2)}) collective-permute-start(bf16[8,2,16,256]{3,2,1,0:T(8,128)(2,1)S(1)} %get-tuple-element.20.refs_0_), channel_id=1, source_target_pairs={{0,12},{4,0},{8,4},{12,8},{1,13},{5,1},{9,5},{13,9},{2,14},{6,2},{... | collective-permute-start | bytes 393224 | tf_op jit(solution)/shard_map/ppermute | solution.py:424
  59.5 26.7 %copy-start.1 = (bf16[1024,256]{1,0:T(8,128)(2,1)S(1)}, bf16[1024,256]{1,0:T(8,128)(2,1)}, u32[]{:S(2)}) copy-start(bf16[1024,256]{1,0:T(8,128)(2,1)} %constant.7.clone) | copy-start | bytes 1572868
  67.0 19.7 %copy-start.2 = (bf16[256,1,1,128]{3,0,2,1:T(8,128)(2,1)S(1)}, bf16[256,1,1,128]{3,0,2,1:T(8,128)(2,1)}, u32[]{:S(2)}) copy-start(bf16[256,1,1,128]{3,0,2,1:T(8,128)(2,1)} %param.11) | copy-start | bytes 196612

commit v8 on v7

--- a/solution.py
+++ b/solution.py
@@ -14,6 +14,8 @@
 LAYERS = 4
 AXES = ("b", "q", "l", "c")
 CHIPS = AXES[:3]
+FIRST = ("l", "b", "q")
+SECOND = ("c", "l", "q", "b")
 FINE_STEP = 0.5
 COARSE_STEP = 1.5
 NOW, OWN = 10, 2
@@ -35,10 +37,10 @@
     return jnp.where(mask, 1.0, 0.0).astype(F32)
 
 
-def swap_table(outer, inner):
-    n = outer * inner
-    row, column = iota((n, n), 0), iota((n, n), 1)
-    return ones_where(column == row % outer * inner + row // outer).astype(BF)
+def back_table():
+    row, column = iota((128, 128), 0), iota((128, 128), 1)
+    y = row // 8 % 4 * 4 + row // 32 % 2 * 2 + row // 64
+    return ones_where(column == row % 8 * 16 + y).astype(BF)
 
 
 def haar_signs(lane, channel):
@@ -76,7 +78,7 @@
     for_second = lane - 2 * (1 + k % PREVS) - k // PREVS
     for_third = jnp.where(lane // 128 == k // COTS, lane % 128 - k % COTS, -1000)
     for target in range(0, 64, 2):
-        spots = [(t // 8, t // 2 % 4, t % 2) for t in (target, target + 1)]
+        spots = [(t // 4 % 8, t % 4, t // 32) for t in (target, target + 1)]
         for t, spot in enumerate(spots):
             at = 32 * (target + t)
             first[at : at + 32] = ones_where(for_first == 2 * window_start(*spot)).astype(BF)
@@ -106,11 +108,12 @@
     row, column = iota((128, 128), 0), iota((128, 128), 1)
     y = row % 16
     source = (y + core) % 2
-    return ones_where(column == (source * 8 + y // 2) * 8 + row // 16).astype(BF)
+    return ones_where(column == (source * 8 + y // 2 % 2 * 4 + y // 4) * 8 + row // 16).astype(BF)
 
 
 def sorted_parts(table, mine, other, x, start, stop):
-    rows = jnp.concatenate([mine[x].astype(F32), other[x].astype(F32)], axis=0)
+    rows = [ref[:, x].astype(F32).reshape(8, ref.shape[3], 128) for ref in (mine, other)]
+    rows = jnp.concatenate(rows, axis=0)
     parts = []
     for k in range(start, stop, 8):
         moved = dot(table, rows[:, k : k + 8, :].reshape(128, 128).astype(BF))
@@ -315,7 +318,7 @@
     table = sort_table(core)
     copies = []
     for i, chunk in enumerate(chunks):
-        copy = pltpu.make_async_copy(chunk.at[:, :, pl.ds(48, 32), :], rows.at[i], sems.at[4 + i])
+        copy = pltpu.make_async_copy(chunk.at[:, :, :, pl.ds(48, 32), :], rows.at[i], sems.at[4 + i])
         copy.start()
         copies.append(copy)
     for i, w in enumerate(pieces):
@@ -363,19 +366,19 @@
         store(scaled, (1.0 - squash * squash) * response[pl.ds(96 * x0, 96 * xs)], x0, xs)
     near = jnp.where(quarter == 1, 1.0, 0.0).astype(F32)
     far = jnp.where(quarter == 2, 1.0, 0.0).astype(F32)
-    back = swap_table(8, 16)
+    back = back_table()
     for x in range(8):
         if x % xs == 0:
             force, pull = coarse_adjoint(squashed, weights, x, xs), coarse_adjoint(scaled, weights, x, xs)
         at = x % xs
         ground = base[x]
         rows = jnp.concatenate([force[at, 0:2] + near * ground, force[at, 2:4] + far * ground, pull[at]], axis=0)
-        out[x] = dot(back, rows.reshape(128, 256).astype(BF)).astype(BF).reshape(16, 8, 256)
+        out[:, x] = dot(back, rows.reshape(128, 256).astype(BF)).astype(BF).reshape(16, 8, 256)
 
 
 def receive_table():
     row = np.arange(1024)
-    at = row // 128 * 16 + row // 8 % 4 * 4 + row % 4 + row // 4 % 2 * 128
+    at = row // 8 % 8 * 16 + row // 256 % 2 * 8 + row // 512 * 4 + row % 4 + row // 4 % 2 * 128
     return (np.arange(256)[None] == at[:, None]).astype(BF)
 
 
@@ -394,7 +397,7 @@
     )(fine_now, fine_prev, cotangent.reshape(256, 128))
     packed, kernel_part = lax.optimization_barrier((packed, coarse_kernel))
     there = lax.ppermute(kernel_part, "c", [(0, 1), (1, 0)])
-    mine = lax.all_to_all(packed, CHIPS, 0, 0)
+    mine = lax.all_to_all(packed, FIRST, 0, 0)
     tile = np.tile(np.eye(32, dtype=np.float32), (1, 4)).astype(BF)
     weights = pl.pallas_call(
         weight_kernel,
@@ -418,8 +421,8 @@
 
     mine, weights, there, kernel_part = lax.optimization_barrier((mine, weights, there, kernel_part))
     across = lax.ppermute(kernel_part, ("b", "l", "c"), [(i, i ^ (18 if i % 2 else 2)) for i in range(32)])
-    other = lax.ppermute(mine, "c", [(0, 1), (1, 0)]).reshape(8, 8, CHUNK, 128)
-    mine = mine.reshape(8, 8, CHUNK, 128)
+    other = lax.ppermute(mine, "c", [(0, 1), (1, 0)]).reshape(2, 8, 4, CHUNK, 128)
+    mine = mine.reshape(2, 8, 4, CHUNK, 128)
     def round_ring(v):
         return [v] + [lax.ppermute(v, "q", [(i, (i + k) % 4) for i in range(4)]) for k in range(1, 4)]
 
@@ -449,7 +452,7 @@
         out_specs=tuple(vmem(2)),
         scratch_shapes=[
             pltpu.VMEM((3, 10, 8, 16, 256), BF),
-            pltpu.VMEM((2, 8, 8, 32, 128), BF),
+            pltpu.VMEM((2, 2, 8, 4, 32, 128), BF),
             pltpu.VMEM((8, COTS, 16, 256), F32),
             pltpu.SemaphoreType.DMA((6,)),
         ],
@@ -459,7 +462,7 @@
     )(mine, other, coarse_kernel, there, across, opposite)
     partial = pl.pallas_call(
         coarse_kernel_body,
-        out_shape=jax.ShapeDtypeStruct((8, 16, 8, 256), BF),
+        out_shape=jax.ShapeDtypeStruct((16, 8, 8, 256), BF),
         in_specs=vmem(7),
         out_specs=pl.BlockSpec(memory_space=pltpu.VMEM),
         scratch_shapes=[pltpu.VMEM((3, 10, 8, 16, 256), BF)] + [pltpu.VMEM((3, 10, 6, 16, 256), BF)] * 2,
@@ -467,7 +470,7 @@
         cost_estimate=pl.CostEstimate(flops=10**10, bytes_accessed=10**7, transcendentals=10**6),
         name="coarse_layer",
     )(*states, base, response, gathered)
-    parts = lax.all_to_all(partial.reshape(128, 8, 256), AXES, 0, 0)
+    parts = lax.all_to_all(partial.reshape(128, 8, 256), SECOND, 0, 0)
     parts = parts.reshape(1024, 256)
     sums = lax.dot_general(parts, receive_table(), (((0,), (0,)), ((), ())), preferred_element_type=F32)
     coarse_next = sums[:, 0:128]

time: 88.6 us -> 88.9 us (level)
  waiting for transfers between devices: 16 us -> 18.8 us
  starting transfers between devices: 17.3 us -> 15.4 us
  blocking collectives: 19.3 us -> 18.4 us
    ppermute x3, waiting for transfers between devices: 1.24 us -> 2.71 us  [round_ring(): lax.ppermute(v, 'q', [(i, (i + k) % 4) for i in range(4)])]
    ppermute x3, starting transfers between devices: 4.8 us -> 3.4 us  [round_ring(): lax.ppermute(v, 'q', [(i, (i + k) % 4) for i in range(4)])]
    all_to_all x1, blocking collectives: 19.3 us -> 18.4 us  [local(): parts = lax.all_to_all(partial.reshape(128, 8, 256), SECOND, 0, 0)]
    all_to_all x1, waiting for transfers between devices: 12.2 us -> 13.1 us  [local(): mine = lax.all_to_all(packed, FIRST, 0, 0)]
where the time goes in v8:
time: 88.9 us; the launch traced here: 87.4 us
  Pallas kernels  30.8 us (35%)
  waiting for transfers between devices  18.8 us (21%)
  blocking collectives  18.4 us (21%)
  starting transfers between devices  15.4 us (17%)
  local copies, waits for them, and re-layouts  2.22 us (2%)
    all_to_all x1, blocking collectives, local(): parts = lax.all_to_all(partial.reshape(128, 8, 256), SECOND, 0, 0)  18.4 us
    all_to_all x1, waiting for transfers between devices, local(): mine = lax.all_to_all(packed, FIRST, 0, 0)  13.1 us
    all_to_all x1, starting transfers between devices, local(): mine = lax.all_to_all(packed, FIRST, 0, 0)  11.6 us
    pallas_call x1, Pallas kernels, local(): pl.pallas_call(fine_kernel, out_shape=(jax.ShapeDtypeStruct((8, OWN, 16,...  10.3 us
    pallas_call x1, Pallas kernels, local(): pl.pallas_call(coarse_kernel_body, out_shape=jax.ShapeDtypeStruct((16, 8,...  7.39 us
    pallas_call x1, Pallas kernels, local(): pl.pallas_call(weight_kernel, grid=(LAYERS,), out_shape=jax.ShapeDtypeStr...  6.21 us
    pallas_call x1, Pallas kernels, local(): pl.pallas_call(response_kernel, out_shape=(jax.ShapeDtypeStruct((768, 256...  4.24 us
    ppermute x3, starting transfers between devices, round_ring(): lax.ppermute(v, 'q', [(i, (i + k) % 4) for i in range(4)])  3.4 us
  transfers between devices with their start and end apart: 8, of which 4 were waited for; matrix products, arithmetic and copies ran while one was open for 3% of the time, Pallas kernels for 24%

profile of v8, /device:TPU:0, one launch (start us, length us, event | category | flops | bytes accessed | tf_op | source)
XLA Modules:
  0.0 87.4 jit_solution(17570694119117161569)
XLA Ops:
  0.6 2.7 %pack.1 = bf16[64,80,128]{2,1,0:T(8,128)(2,1)} custom-call(f32[32,2,2,256]{3,2,1,0:T(2,128)} %now_in.1, f32[32,2,2,256]{3,2,1,0:T(2,128)} %prev_in.1, bf16[256,128]{1,0:T(8,128)(2,1)} %bitcast.26), custom_call_target="tpu_custom_call" | custom-call | tf_op jit(solution)/shard_map/pack/pallas_call | solution.py:386
  3.3 0.0 copy-start
  3.3 11.6 %all-to-all-start = ((bf16[64,80,128]{2,1,0:T(8,128)(2,1)}), bf16[64,80,128]{2,1,0:T(8,128)(2,1)S(1)}, u32[]{:S(2)}, u32[]{:S(2)}) async-start(bf16[64,80,128]{2,1,0:T(8,128)(2,1)} %pack.1), calls=%async_computation | async-start | bytes 2621440 | tf_op jit(solution)/shard_map/all_to_all | solution.py:400
  15.0 0.1 collective-permute-start
  15.1 2.2 %copy.9 = bf16[4,27,32,32]{3,2,1,0:T(8,128)(2,1)} copy(bf16[4,27,32,32]{2,3,1,0:T(8,128)(2,1)} %bitcast.23) | data formatting | bytes 442368 | tf_op jit(solution)/shard_map/transpose | solution.py:417
  17.3 6.2 %spread_weights.1.spread = bf16[4,2,8,256,256]{4,3,2,1,0:T(8,128)(2,1)} custom-call(bf16[4,864,32]{2,1,0:T(8,128)(2,1)} %bitcast.25, bf16[4,864,32]{2,1,0:T(8,128)(2,1)} %bitcast.24, bf16[32,128]{1,0:T(8,128)(2,1)} %constant.6.clone.tile), custom_call_target="tpu_custom_call" | custom-call | flops 10000000000 | bytes 10000000 | tf_op jit(solution)/shard_map/spread_weights/pallas_call | solution.py:402
  23.5 0.0 collective-permute-done.refs_3_
  23.5 13.1 %all-to-all-done = bf16[64,80,128]{2,1,0:T(8,128)(2,1)S(1)} async-done(((bf16[64,80,128]{2,1,0:T(8,128)(2,1)}), bf16[64,80,128]{2,1,0:T(8,128)(2,1)S(1)}, u32[]{:S(2)}, u32[]{:S(2)}) %all-to-all-start) | async-done | bytes 1310752 | tf_op jit(solution)/shard_map/all_to_all | solution.py:400
  36.6 0.0 collective-permute-start.1
  36.6 0.0 collective-permute-start.2
  36.6 3.0 %collective-permute-done.1 = bf16[64,80,128]{2,1,0:T(8,128)(2,1)S(1)} collective-permute-done((bf16[64,80,128]{2,1,0:T(8,128)(2,1)S(1)}, bf16[64,80,128]{2,1,0:T(8,128)(2,1)S(1)}, u32[]{:S(2)}, u32[]{:S(2)}) %collective-permute-start.1) | collective-permute-done | bytes 1310752 | tf_op jit(solution)/shard_map/ppermute | solution.py:424
  39.6 10.3 %fine_layers.1 = (bf16[8,2,16,256]{3,2,1,0:T(8,128)(2,1)S(1)}, f32[8,2,16,256]{3,2,1,0:T(8,128)S(1)}) custom-call(bf16[2,8,4,80,128]{4,3,2,1,0:T(8,128)(2,1)S(1)} %bitcast.18, bf16[2,8,4,80,128]{4,3,2,1,0:T(8,128)(2,1)S(1)} %bitcast.20, bf16[4,2,8,256,256]{4,3,2,1,0:T(8,128)(2,1)} %spread_weights.1.spread), custom_call_target="tpu_custom_call" | custom-call | flops 1000000000 | bytes 1000000 | tf_op jit(solution)/shard_map/fine_layers/pallas_call | solution.py:430
  50.0 0.3 collective-permute-start.6
  50.2 0.6 collective-permute-start.3
  50.8 1.9 %collective-permute-start.4 = (bf16[8,2,16,256]{3,2,1,0:T(8,128)(2,1)S(1)}, bf16[8,2,16,256]{3,2,1,0:T(8,128)(2,1)S(1)}, u32[]{:S(2)}, u32[]{:S(2)}) collective-permute-start(bf16[8,2,16,256]{3,2,1,0:T(8,128)(2,1)S(1)} %get-tuple-element.20.refs_0_), channel_id=1, source_target_pairs={{0,8},{4,12},{8,0},{12,4},{1,9},{5,13},{9,1},{13,5},{2,10},{6,14},... | collective-permute-start | bytes 393224 | tf_op jit(solution)/shard_map/ppermute | solution.py:427
  52.7 0.9 %collective-permute-start.5 = (bf16[8,2,16,256]{3,2,1,0:T(8,128)(2,1)S(1)}, bf16[8,2,16,256]{3,2,1,0:T(8,128)(2,1)S(1)}, u32[]{:S(2)}, u32[]{:S(2)}) collective-permute-start(bf16[8,2,16,256]{3,2,1,0:T(8,128)(2,1)S(1)} %get-tuple-element.20.refs_0_), channel_id=1, source_target_pairs={{0,12},{4,0},{8,4},{12,8},{1,13},{5,1},{9,5},{13,9},{2,14},{6,2},{... | collective-permute-start | bytes 393224 | tf_op jit(solution)/shard_map/ppermute | solution.py:427
  53.6 4.2 %response.1 = (f32[768,256]{1,0:T(8,128)S(1)}, bf16[27,256,256]{2,1,0:T(8,128)(2,1)S(1)}) custom-call(bf16[2,8,4,80,128]{4,3,2,1,0:T(8,128)(2,1)S(1)} %bitcast.19, bf16[2,8,4,80,128]{4,3,2,1,0:T(8,128)(2,1)S(1)} %bitcast.21, bf16[27,64,256]{2,1,0:T(8,128)(2,1)S(1)} %copy-done, bf16[27,64,256]{2,1,0:T(8,128)(2,1)S(1)} %collective-permute-done.refs_3_, ...), custom_call_target="tpu_custom_call" | custom-call | flops 5000000000 | bytes 10000000 | tf_op jit(solution)/shard_map/response/pallas_call | solution.py:448
  57.9 2.1 %collective-permute-done.3.refs_1_ = bf16[8,2,16,256]{3,2,1,0:T(8,128)(2,1)S(1)} collective-permute-done((bf16[8,2,16,256]{3,2,1,0:T(8,128)(2,1)S(1)}, bf16[8,2,16,256]{3,2,1,0:T(8,128)(2,1)S(1)}, u32[]{:S(2)}, u32[]{:S(2)}) %collective-permute-start.3) | collective-permute-done | bytes 131104 | tf_op jit(solution)/shard_map/ppermute | solution.py:427
  60.0 0.6 collective-permute-done.5.refs_3_
  60.6 7.4 %coarse_layer.1 = bf16[16,8,8,256]{3,2,1,0:T(8,128)(2,1)S(1)} custom-call(bf16[8,2,16,256]{3,2,1,0:T(8,128)(2,1)S(1)} %get-tuple-element.20.refs_0_, bf16[8,2,16,256]{3,2,1,0:T(8,128)(2,1)S(1)} %collective-permute-done.3.refs_1_, bf16[8,2,16,256]{3,2,1,0:T(8,128)(2,1)S(1)} %collective-permute-done.4.refs_2_, ...), custom_call_target="tpu_custom_call" | custom-call | flops 10000000000 | bytes 10000000 | tf_op jit(solution)/shard_map/coarse_layer/pallas_call | solution.py:463
  68.0 0.0 copy-start.2
  68.0 18.4 %all_to_all.10 = bf16[128,8,256]{2,1,0:T(8,128)(2,1)S(1)} all-to-all(bf16[128,8,256]{2,1,0:T(8,128)(2,1)S(1)} %bitcast.22), channel_id=1, replica_groups=mesh['b'=8,'q'=4,'l'=2,'c'=2] {'c','l','q','b'}, dimensions={0} | all-to-all | bytes 1048576 | tf_op jit(solution)/shard_map/all_to_all | solution.py:473
  86.4 0.3 fusion
  86.7 0.7 slice_add_fusion
  (7 shorter events, 0.0 us)
Async XLA Ops:
  3.3 11.7 %copy-start = (bf16[27,64,256]{2,1,0:T(8,128)(2,1)S(1)}, bf16[27,64,256]{2,1,0:T(8,128)(2,1)}, u32[]{:S(2)}) copy-start(bf16[27,64,256]{2,1,0:T(8,128)(2,1)} %refs_2_.1) | copy-start | bytes 2654212
  3.3 33.3 %all-to-all-start = ((bf16[64,80,128]{2,1,0:T(8,128)(2,1)}), bf16[64,80,128]{2,1,0:T(8,128)(2,1)S(1)}, u32[]{:S(2)}, u32[]{:S(2)}) async-start(bf16[64,80,128]{2,1,0:T(8,128)(2,1)} %pack.1), calls=%async_computation | async-start | bytes 2621440 | tf_op jit(solution)/shard_map/all_to_all | solution.py:400
  15.0 8.5 %collective-permute-start = (bf16[27,64,256]{2,1,0:T(8,128)(2,1)S(1)}, bf16[27,64,256]{2,1,0:T(8,128)(2,1)S(1)}, u32[]{:S(2)}, u32[]{:S(2)}) collective-permute-start(bf16[27,64,256]{2,1,0:T(8,128)(2,1)S(1)} %copy-done), channel_id=1, source_target_pairs={{0,1},{1,0},{2,3},{3,2},{4,5},{5,4},{6,7},{7,6},{8,9},{9,8},{10,11... | collective-permute-start | bytes 2654216 | tf_op jit(solution)/shard_map/ppermute | solution.py:399
  36.6 3.0 %collective-permute-start.1 = (bf16[64,80,128]{2,1,0:T(8,128)(2,1)S(1)}, bf16[64,80,128]{2,1,0:T(8,128)(2,1)S(1)}, u32[]{:S(2)}, u32[]{:S(2)}) collective-permute-start(bf16[64,80,128]{2,1,0:T(8,128)(2,1)S(1)} %all-to-all-done), channel_id=1, source_target_pairs={{0,1},{1,0},{2,3},{3,2},{4,5},{5,4},{6,7},{7,6},{8,9},{9,8},{10,11... | collective-permute-start | bytes 3932168 | tf_op jit(solution)/shard_map/ppermute | solution.py:424
  36.6 13.3 %collective-permute-start.2 = (bf16[27,64,256]{2,1,0:T(8,128)(2,1)S(1)}, bf16[27,64,256]{2,1,0:T(8,128)(2,1)S(1)}, u32[]{:S(2)}, u32[]{:S(2)}) collective-permute-start(bf16[27,64,256]{2,1,0:T(8,128)(2,1)S(1)} %copy-done), channel_id=1, source_target_pairs={{0,2},{1,67},{2,0},{3,65},{16,18},{17,83},{18,16},{19,81},{32,34},... | collective-permute-start | bytes 2654216 | tf_op jit(solution)/shard_map/ppermute | solution.py:423
  50.0 3.7 %collective-permute-start.6 = (bf16[27,64,256]{2,1,0:T(8,128)(2,1)S(1)}, bf16[27,64,256]{2,1,0:T(8,128)(2,1)S(1)}, u32[]{:S(2)}, u32[]{:S(2)}) collective-permute-start(bf16[27,64,256]{2,1,0:T(8,128)(2,1)S(1)} %collective-permute-done.2.refs_4_), channel_id=1, source_target_pairs={{0,1},{1,0},{2,3},{3,2},{4,5},{5,4},{6,7},{7,6},{8,9},{9,8},{10,11... | collective-permute-start | bytes 2654216 | tf_op jit(solution)/shard_map/ppermute | solution.py:447
  50.2 9.7 %collective-permute-start.3 = (bf16[8,2,16,256]{3,2,1,0:T(8,128)(2,1)S(1)}, bf16[8,2,16,256]{3,2,1,0:T(8,128)(2,1)S(1)}, u32[]{:S(2)}, u32[]{:S(2)}) collective-permute-start(bf16[8,2,16,256]{3,2,1,0:T(8,128)(2,1)S(1)} %get-tuple-element.20.refs_0_), channel_id=1, source_target_pairs={{0,4},{4,8},{8,12},{12,0},{1,5},{5,9},{9,13},{13,1},{2,6},{6,10},{... | collective-permute-start | bytes 393224 | tf_op jit(solution)/shard_map/ppermute | solution.py:427
  50.8 9.2 %collective-permute-start.4 = (bf16[8,2,16,256]{3,2,1,0:T(8,128)(2,1)S(1)}, bf16[8,2,16,256]{3,2,1,0:T(8,128)(2,1)S(1)}, u32[]{:S(2)}, u32[]{:S(2)}) collective-permute-start(bf16[8,2,16,256]{3,2,1,0:T(8,128)(2,1)S(1)} %get-tuple-element.20.refs_0_), channel_id=1, source_target_pairs={{0,8},{4,12},{8,0},{12,4},{1,9},{5,13},{9,1},{13,5},{2,10},{6,14},... | collective-permute-start | bytes 393224 | tf_op jit(solution)/shard_map/ppermute | solution.py:427
  52.7 7.9 %collective-permute-start.5 = (bf16[8,2,16,256]{3,2,1,0:T(8,128)(2,1)S(1)}, bf16[8,2,16,256]{3,2,1,0:T(8,128)(2,1)S(1)}, u32[]{:S(2)}, u32[]{:S(2)}) collective-permute-start(bf16[8,2,16,256]{3,2,1,0:T(8,128)(2,1)S(1)} %get-tuple-element.20.refs_0_), channel_id=1, source_target_pairs={{0,12},{4,0},{8,4},{12,8},{1,13},{5,1},{9,5},{13,9},{2,14},{6,2},{... | collective-permute-start | bytes 393224 | tf_op jit(solution)/shard_map/ppermute | solution.py:427
  60.6 25.8 %copy-start.1 = (bf16[1024,256]{1,0:T(8,128)(2,1)S(1)}, bf16[1024,256]{1,0:T(8,128)(2,1)}, u32[]{:S(2)}) copy-start(bf16[1024,256]{1,0:T(8,128)(2,1)} %constant.7.clone) | copy-start | bytes 1572868
  68.0 18.7 %copy-start.2 = (bf16[256,1,1,128]{3,0,2,1:T(8,128)(2,1)S(1)}, bf16[256,1,1,128]{3,0,2,1:T(8,128)(2,1)}, u32[]{:S(2)}) copy-start(bf16[256,1,1,128]{3,0,2,1:T(8,128)(2,1)} %param.11) | copy-start | bytes 196612

commit v9 on v7

--- a/solution.py
+++ b/solution.py
@@ -226,7 +226,7 @@
             s1[x + 1, z + 1] = moved_rows(v).astype(BF)
         return carry
 
-    lax.fori_loop(0, 8, unpack, 0)
+    lax.fori_loop(0, 8, unpack, 0, unroll=2)
 
     now, before = cur, old
     for layer in range(LAYERS):
@@ -421,7 +421,8 @@
     other = lax.ppermute(mine, "c", [(0, 1), (1, 0)]).reshape(8, 8, CHUNK, 128)
     mine = mine.reshape(8, 8, CHUNK, 128)
     def round_ring(v):
-        return [v] + [lax.ppermute(v, "q", [(i, (i + k) % 4) for i in range(4)]) for k in range(1, 4)]
+        moved = {k: lax.ppermute(v, "q", [(i, (i + k) % 4) for i in range(4)]) for k in (2, 1, 3)}
+        return [v, moved[1], moved[2], moved[3]]
 
     buffer = pltpu.VMEM((10, NOW + 2, 16, 256), BF)
     mid, base = pl.pallas_call(

time: 88.6 us -> 88.4 us (level)
  transfers between devices with their start and end apart: 8 -> 8, of which waited for: 4 -> 5; matrix products, arithmetic and copies ran while one was open for 3% -> 3% of each run, Pallas kernels for 24% -> 23%
where the time goes in v9:
time: 88.4 us; the launch traced here: 87.1 us
  Pallas kernels  30.4 us (34%)
  blocking collectives  19.3 us (22%)
  starting transfers between devices  17.5 us (20%)
  waiting for transfers between devices  15.9 us (18%)
  local copies, waits for them, and re-layouts  2.22 us (3%)
    all_to_all x1, blocking collectives, local(): parts = lax.all_to_all(partial.reshape(128, 8, 256), AXES, 0, 0)  19.3 us
    all_to_all x1, waiting for transfers between devices, local(): mine = lax.all_to_all(packed, CHIPS, 0, 0)  12.2 us
    all_to_all x1, starting transfers between devices, local(): mine = lax.all_to_all(packed, CHIPS, 0, 0)  11.6 us
    pallas_call x1, Pallas kernels, local(): pl.pallas_call(fine_kernel, out_shape=(jax.ShapeDtypeStruct((8, OWN, 16,...  9.91 us
    pallas_call x1, Pallas kernels, local(): pl.pallas_call(coarse_kernel_body, out_shape=jax.ShapeDtypeStruct((8, 16,...  7.4 us
    pallas_call x1, Pallas kernels, local(): pl.pallas_call(weight_kernel, grid=(LAYERS,), out_shape=jax.ShapeDtypeStr...  6.21 us
    ppermute x3, starting transfers between devices, round_ring(): lax.ppermute(v, 'q', [(i, (i + k) % 4) for i in range(4)])  4.8 us
    pallas_call x1, Pallas kernels, local(): pl.pallas_call(response_kernel, out_shape=(jax.ShapeDtypeStruct((768, 256...  4.2 us
  transfers between devices with their start and end apart: 8, of which 5 were waited for; matrix products, arithmetic and copies ran while one was open for 3% of the time, Pallas kernels for 23%

profile of v9, /device:TPU:0, one launch (start us, length us, event | category | flops | bytes accessed | tf_op | source)
XLA Modules:
  0.0 87.1 jit_solution(7325760098249243450)
XLA Ops:
  0.6 2.7 %pack.1 = bf16[64,80,128]{2,1,0:T(8,128)(2,1)} custom-call(f32[32,2,2,256]{3,2,1,0:T(2,128)} %now_in.1, f32[32,2,2,256]{3,2,1,0:T(2,128)} %prev_in.1, bf16[256,128]{1,0:T(8,128)(2,1)} %bitcast.26), custom_call_target="tpu_custom_call" | custom-call | tf_op jit(solution)/shard_map/pack/pallas_call | solution.py:383
  3.3 0.0 copy-start
  3.3 11.6 %all-to-all-start = ((bf16[64,80,128]{2,1,0:T(8,128)(2,1)}), bf16[64,80,128]{2,1,0:T(8,128)(2,1)S(1)}, u32[]{:S(2)}, u32[]{:S(2)}) async-start(bf16[64,80,128]{2,1,0:T(8,128)(2,1)} %pack.1), calls=%async_computation | async-start | bytes 2621440 | tf_op jit(solution)/shard_map/all_to_all | solution.py:397
  15.0 0.1 collective-permute-start
  15.1 2.2 %copy.9 = bf16[4,27,32,32]{3,2,1,0:T(8,128)(2,1)} copy(bf16[4,27,32,32]{2,3,1,0:T(8,128)(2,1)} %bitcast.23) | data formatting | bytes 442368 | tf_op jit(solution)/shard_map/transpose | solution.py:414
  17.3 6.2 %spread_weights.1.spread = bf16[4,2,8,256,256]{4,3,2,1,0:T(8,128)(2,1)} custom-call(bf16[4,864,32]{2,1,0:T(8,128)(2,1)} %bitcast.25, bf16[4,864,32]{2,1,0:T(8,128)(2,1)} %bitcast.24, bf16[32,128]{1,0:T(8,128)(2,1)} %constant.6.clone.tile), custom_call_target="tpu_custom_call" | custom-call | flops 10000000000 | bytes 10000000 | tf_op jit(solution)/shard_map/spread_weights/pallas_call | solution.py:399
  23.5 0.0 collective-permute-done.refs_3_
  23.5 12.2 %all-to-all-done = bf16[64,80,128]{2,1,0:T(8,128)(2,1)S(1)} async-done(((bf16[64,80,128]{2,1,0:T(8,128)(2,1)}), bf16[64,80,128]{2,1,0:T(8,128)(2,1)S(1)}, u32[]{:S(2)}, u32[]{:S(2)}) %all-to-all-start) | async-done | bytes 1310752 | tf_op jit(solution)/shard_map/all_to_all | solution.py:397
  35.7 0.4 collective-permute-start.2
  36.1 2.6 %collective-permute-done.1 = bf16[64,80,128]{2,1,0:T(8,128)(2,1)S(1)} collective-permute-done((bf16[64,80,128]{2,1,0:T(8,128)(2,1)S(1)}, bf16[64,80,128]{2,1,0:T(8,128)(2,1)S(1)}, u32[]{:S(2)}, u32[]{:S(2)}) %collective-permute-start.1) | collective-permute-done | bytes 1310752 | tf_op jit(solution)/shard_map/ppermute | solution.py:421
  38.7 9.9 %fine_layers.1 = (bf16[8,2,16,256]{3,2,1,0:T(8,128)(2,1)S(1)}, f32[8,2,16,256]{3,2,1,0:T(8,128)S(1)}) custom-call(bf16[8,8,80,128]{3,2,1,0:T(8,128)(2,1)S(1)} %bitcast.18, bf16[8,8,80,128]{3,2,1,0:T(8,128)(2,1)S(1)} %bitcast.20, bf16[4,2,8,256,256]{4,3,2,1,0:T(8,128)(2,1)} %spread_weights.1.spread), custom_call_target="tpu_custom_call" | custom-call | flops 1000000000 | bytes 1000000 | tf_op jit(solution)/shard_map/fine_layers/pallas_call | solution.py:428
  48.6 0.1 collective-permute-done.2.refs_4_
  48.7 0.6 collective-permute-start.6
  49.3 1.0 %collective-permute-start.3 = (bf16[8,2,16,256]{3,2,1,0:T(8,128)(2,1)S(1)}, bf16[8,2,16,256]{3,2,1,0:T(8,128)(2,1)S(1)}, u32[]{:S(2)}, u32[]{:S(2)}) collective-permute-start(bf16[8,2,16,256]{3,2,1,0:T(8,128)(2,1)S(1)} %get-tuple-element.20.refs_0_), channel_id=1, source_target_pairs={{0,4},{4,8},{8,12},{12,0},{1,5},{5,9},{9,13},{13,1},{2,6},{6,10},{... | collective-permute-start | bytes 393224 | tf_op jit(solution)/shard_map/ppermute | solution.py:424
  50.3 2.7 %collective-permute-start.4 = (bf16[8,2,16,256]{3,2,1,0:T(8,128)(2,1)S(1)}, bf16[8,2,16,256]{3,2,1,0:T(8,128)(2,1)S(1)}, u32[]{:S(2)}, u32[]{:S(2)}) collective-permute-start(bf16[8,2,16,256]{3,2,1,0:T(8,128)(2,1)S(1)} %get-tuple-element.20.refs_0_), channel_id=1, source_target_pairs={{0,8},{4,12},{8,0},{12,4},{1,9},{5,13},{9,1},{13,5},{2,10},{6,14},... | collective-permute-start | bytes 393224 | tf_op jit(solution)/shard_map/ppermute | solution.py:424
  53.0 1.1 %collective-permute-start.5 = (bf16[8,2,16,256]{3,2,1,0:T(8,128)(2,1)S(1)}, bf16[8,2,16,256]{3,2,1,0:T(8,128)(2,1)S(1)}, u32[]{:S(2)}, u32[]{:S(2)}) collective-permute-start(bf16[8,2,16,256]{3,2,1,0:T(8,128)(2,1)S(1)} %get-tuple-element.20.refs_0_), channel_id=1, source_target_pairs={{0,12},{4,0},{8,4},{12,8},{1,13},{5,1},{9,5},{13,9},{2,14},{6,2},{... | collective-permute-start | bytes 393224 | tf_op jit(solution)/shard_map/ppermute | solution.py:424
  54.1 4.2 %response.1 = (f32[768,256]{1,0:T(8,128)S(1)}, bf16[27,256,256]{2,1,0:T(8,128)(2,1)S(1)}) custom-call(bf16[8,8,80,128]{3,2,1,0:T(8,128)(2,1)S(1)} %bitcast.19, bf16[8,8,80,128]{3,2,1,0:T(8,128)(2,1)S(1)} %bitcast.21, bf16[27,64,256]{2,1,0:T(8,128)(2,1)S(1)} %copy-done, bf16[27,64,256]{2,1,0:T(8,128)(2,1)S(1)} %collective-permute-done.refs_3_, ...), custom_call_target="tpu_custom_call" | custom-call | flops 5000000000 | bytes 10000000 | tf_op jit(solution)/shard_map/response/pallas_call | solution.py:446
  58.3 0.9 %collective-permute-done.4.refs_2_ = bf16[8,2,16,256]{3,2,1,0:T(8,128)(2,1)S(1)} collective-permute-done((bf16[8,2,16,256]{3,2,1,0:T(8,128)(2,1)S(1)}, bf16[8,2,16,256]{3,2,1,0:T(8,128)(2,1)S(1)}, u32[]{:S(2)}, u32[]{:S(2)}) %collective-permute-start.4) | collective-permute-done | bytes 131104 | tf_op jit(solution)/shard_map/ppermute | solution.py:424
  59.2 0.1 collective-permute-done.5.refs_3_
  59.3 7.4 %coarse_layer.1 = bf16[8,16,8,256]{3,2,1,0:T(8,128)(2,1)S(1)} custom-call(bf16[8,2,16,256]{3,2,1,0:T(8,128)(2,1)S(1)} %get-tuple-element.20.refs_0_, bf16[8,2,16,256]{3,2,1,0:T(8,128)(2,1)S(1)} %collective-permute-done.3.refs_1_, bf16[8,2,16,256]{3,2,1,0:T(8,128)(2,1)S(1)} %collective-permute-done.4.refs_2_, ...), custom_call_target="tpu_custom_call" | custom-call | flops 10000000000 | bytes 10000000 | tf_op jit(solution)/shard_map/coarse_layer/pallas_call | solution.py:461
  66.7 0.0 copy-start.2
  66.7 19.3 %all_to_all.10 = bf16[128,8,256]{2,1,0:T(8,128)(2,1)S(1)} all-to-all(bf16[128,8,256]{2,1,0:T(8,128)(2,1)S(1)} %bitcast.22), channel_id=1, replica_groups=mesh['b'=8,'q'=4,'l'=2,'c'=2] {'b','q','l','c'}, dimensions={0} | all-to-all | bytes 1048576 | tf_op jit(solution)/shard_map/all_to_all | solution.py:471
  86.1 0.3 fusion
  86.4 0.7 slice_add_fusion
  (7 shorter events, 0.0 us)
Async XLA Ops:
  3.3 11.7 %copy-start = (bf16[27,64,256]{2,1,0:T(8,128)(2,1)S(1)}, bf16[27,64,256]{2,1,0:T(8,128)(2,1)}, u32[]{:S(2)}) copy-start(bf16[27,64,256]{2,1,0:T(8,128)(2,1)} %refs_2_.1) | copy-start | bytes 2654212
  3.3 32.4 %all-to-all-start = ((bf16[64,80,128]{2,1,0:T(8,128)(2,1)}), bf16[64,80,128]{2,1,0:T(8,128)(2,1)S(1)}, u32[]{:S(2)}, u32[]{:S(2)}) async-start(bf16[64,80,128]{2,1,0:T(8,128)(2,1)} %pack.1), calls=%async_computation | async-start | bytes 2621440 | tf_op jit(solution)/shard_map/all_to_all | solution.py:397
  15.0 8.5 %collective-permute-start = (bf16[27,64,256]{2,1,0:T(8,128)(2,1)S(1)}, bf16[27,64,256]{2,1,0:T(8,128)(2,1)S(1)}, u32[]{:S(2)}, u32[]{:S(2)}) collective-permute-start(bf16[27,64,256]{2,1,0:T(8,128)(2,1)S(1)} %copy-done), channel_id=1, source_target_pairs={{0,1},{1,0},{2,3},{3,2},{4,5},{5,4},{6,7},{7,6},{8,9},{9,8},{10,11... | collective-permute-start | bytes 2654216 | tf_op jit(solution)/shard_map/ppermute | solution.py:396
  35.7 3.0 %collective-permute-start.1 = (bf16[64,80,128]{2,1,0:T(8,128)(2,1)S(1)}, bf16[64,80,128]{2,1,0:T(8,128)(2,1)S(1)}, u32[]{:S(2)}, u32[]{:S(2)}) collective-permute-start(bf16[64,80,128]{2,1,0:T(8,128)(2,1)S(1)} %all-to-all-done), channel_id=1, source_target_pairs={{0,1},{1,0},{2,3},{3,2},{4,5},{5,4},{6,7},{7,6},{8,9},{9,8},{10,11... | collective-permute-start | bytes 3932168 | tf_op jit(solution)/shard_map/ppermute | solution.py:421
  35.7 13.0 %collective-permute-start.2 = (bf16[27,64,256]{2,1,0:T(8,128)(2,1)S(1)}, bf16[27,64,256]{2,1,0:T(8,128)(2,1)S(1)}, u32[]{:S(2)}, u32[]{:S(2)}) collective-permute-start(bf16[27,64,256]{2,1,0:T(8,128)(2,1)S(1)} %copy-done), channel_id=1, source_target_pairs={{0,2},{1,67},{2,0},{3,65},{16,18},{17,83},{18,16},{19,81},{32,34},... | collective-permute-start | bytes 2654216 | tf_op jit(solution)/shard_map/ppermute | solution.py:420
  48.7 5.4 %collective-permute-start.6 = (bf16[27,64,256]{2,1,0:T(8,128)(2,1)S(1)}, bf16[27,64,256]{2,1,0:T(8,128)(2,1)S(1)}, u32[]{:S(2)}, u32[]{:S(2)}) collective-permute-start(bf16[27,64,256]{2,1,0:T(8,128)(2,1)S(1)} %collective-permute-done.2.refs_4_), channel_id=1, source_target_pairs={{0,1},{1,0},{2,3},{3,2},{4,5},{5,4},{6,7},{7,6},{8,9},{9,8},{10,11... | collective-permute-start | bytes 2654216 | tf_op jit(solution)/shard_map/ppermute | solution.py:445
  49.3 9.0 %collective-permute-start.3 = (bf16[8,2,16,256]{3,2,1,0:T(8,128)(2,1)S(1)}, bf16[8,2,16,256]{3,2,1,0:T(8,128)(2,1)S(1)}, u32[]{:S(2)}, u32[]{:S(2)}) collective-permute-start(bf16[8,2,16,256]{3,2,1,0:T(8,128)(2,1)S(1)} %get-tuple-element.20.refs_0_), channel_id=1, source_target_pairs={{0,4},{4,8},{8,12},{12,0},{1,5},{5,9},{9,13},{13,1},{2,6},{6,10},{... | collective-permute-start | bytes 393224 | tf_op jit(solution)/shard_map/ppermute | solution.py:424
  50.3 8.9 %collective-permute-start.4 = (bf16[8,2,16,256]{3,2,1,0:T(8,128)(2,1)S(1)}, bf16[8,2,16,256]{3,2,1,0:T(8,128)(2,1)S(1)}, u32[]{:S(2)}, u32[]{:S(2)}) collective-permute-start(bf16[8,2,16,256]{3,2,1,0:T(8,128)(2,1)S(1)} %get-tuple-element.20.refs_0_), channel_id=1, source_target_pairs={{0,8},{4,12},{8,0},{12,4},{1,9},{5,13},{9,1},{13,5},{2,10},{6,14},... | collective-permute-start | bytes 393224 | tf_op jit(solution)/shard_map/ppermute | solution.py:424
  53.0 6.3 %collective-permute-start.5 = (bf16[8,2,16,256]{3,2,1,0:T(8,128)(2,1)S(1)}, bf16[8,2,16,256]{3,2,1,0:T(8,128)(2,1)S(1)}, u32[]{:S(2)}, u32[]{:S(2)}) collective-permute-start(bf16[8,2,16,256]{3,2,1,0:T(8,128)(2,1)S(1)} %get-tuple-element.20.refs_0_), channel_id=1, source_target_pairs={{0,12},{4,0},{8,4},{12,8},{1,13},{5,1},{9,5},{13,9},{2,14},{6,2},{... | collective-permute-start | bytes 393224 | tf_op jit(solution)/shard_map/ppermute | solution.py:424
  59.3 26.8 %copy-start.1 = (bf16[1024,256]{1,0:T(8,128)(2,1)S(1)}, bf16[1024,256]{1,0:T(8,128)(2,1)}, u32[]{:S(2)}) copy-start(bf16[1024,256]{1,0:T(8,128)(2,1)} %constant.7.clone) | copy-start | bytes 1572868
  66.7 19.7 %copy-start.2 = (bf16[256,1,1,128]{3,0,2,1:T(8,128)(2,1)S(1)}, bf16[256,1,1,128]{3,0,2,1:T(8,128)(2,1)}, u32[]{:S(2)}) copy-start(bf16[256,1,1,128]{3,0,2,1:T(8,128)(2,1)} %param.11) | copy-start | bytes 196612
